TPU v7x, 512 devices: a whole 4x8x8 slice. The times are simulated.
512 devices in a mesh: pop: 16 (over x, y_hi), tp: 32 (over z, y_lo, core).
Axes of the slice: x: 4, y: 8 (y_hi: 4, y_lo: 2; y = y_hi * 2 + y_lo), z: 8, core: 2. Of those that a mesh axis runs over, the one named last changes fastest.
Arguments:
- states: bfloat16 [256, 5120], P(None, 'pop'), may hold values from -6 to 6
- token_ids: int32 [640, 4], replicated, may hold values from 0 to 255
- gate_matrix: bfloat16 [5120, 16384], P('pop', 'tp'), may hold values from -0.078125 to 0.078125
- up_matrix: bfloat16 [5120, 16384], P('pop', 'tp'), may hold values from -0.078125 to 0.078125
- down_matrix: bfloat16 [16384, 5120], P('tp', 'pop'), may hold values from -0.046875 to 0.046875
- gate_left: bfloat16 [640, 5120], P(None, 'pop'), may hold values from -6 to 6
- gate_right: bfloat16 [640, 16384], P('pop', 'tp'), may hold values from -6 to 6
- up_left: bfloat16 [640, 5120], P(None, 'pop'), may hold values from -6 to 6
- up_right: bfloat16 [640, 16384], P('pop', 'tp'), may hold values from -6 to 6
- down_left: bfloat16 [640, 16384], P('pop', 'tp'), may hold values from -6 to 6
- down_right: bfloat16 [640, 5120], P(None, 'pop'), may hold values from -6 to 6
- target: bfloat16 [2560, 5120], P('tp', 'pop'), may hold values from -4 to 4
Outputs:
- layer_out: float32 [2560, 5120], P('tp', 'pop')
- gate_update: float32 [5120, 16384], P('pop', 'tp')
- up_update: float32 [5120, 16384], P('pop', 'tp')
- down_update: float32 [16384, 5120], P('tp', 'pop')
All inputs are finite; a program needn't handle non-finite values.
Results may differ from a plain program's by a relative error of at most 0.0029.
Values may be sent and summed in bfloat16 or wider, within the bound.
No kernel may reach another device: no remote copies, remote signals or barrier semaphores. Data moves between devices by JAX's collectives and lax.ppermute only.
A program may use at most 128 MiB of HBM per device.

v0:
```python
import math

import jax
import jax.numpy as jnp
from jax import lax
from jax.sharding import PartitionSpec as P

D = 5120
FF = 16384


spread = 0.5
epsilon = 1e-06


def outer_sum(left, right):
    return lax.dot_general(
        left,
        right,
        (((0,), (0,)), ((), ())),
        precision=lax.Precision.HIGHEST,
        preferred_element_type=jnp.float32,
    )


def build_hidden(gate_base, up_base, id_rows, gate_dot, up_dot, right_gate, right_up):
    count, tokens = id_rows.shape
    flat_ids = id_rows.reshape(-1)
    unit_count = gate_base.shape[1]
    gate_pre = (
        jnp.take(gate_base, flat_ids, axis=0).reshape(count, tokens, unit_count)
        + spread * gate_dot[:, :, None] * right_gate.astype(jnp.float32)[:, None, :]
    )
    up_pre = (
        jnp.take(up_base, flat_ids, axis=0).reshape(count, tokens, unit_count)
        + spread * up_dot[:, :, None] * right_up.astype(jnp.float32)[:, None, :]
    )
    return (jax.nn.silu(gate_pre) * up_pre).astype(jnp.bfloat16).reshape(count * tokens, unit_count)


def per_device(
    states,
    token_ids,
    gate_matrix,
    up_matrix,
    down_matrix,
    gate_left,
    gate_right,
    up_left,
    up_right,
    down_left,
    down_right,
    target,
):
    group_index = lax.axis_index("pop")
    unit_index = lax.axis_index("tp")
    members, tokens = token_ids.shape
    group_size = gate_right.shape[0]
    slice_width = states.shape[1]
    rows_here = target.shape[0]
    inverse_width = 1.0 / math.sqrt(D)
    right_gate, right_up, left_down = (
        lax.all_gather(gate_right, "pop", axis=0, tiled=True),
        lax.all_gather(up_right, "pop", axis=0, tiled=True),
        lax.all_gather(down_left, "pop", axis=0, tiled=True),
    )
    gate_part = jnp.dot(states, gate_matrix, preferred_element_type=jnp.float32)
    up_part = jnp.dot(states, up_matrix, preferred_element_type=jnp.float32)
    picked = jnp.take(states, token_ids.reshape(-1), axis=0).reshape(members, tokens, slice_width)
    gate_dots = jnp.einsum("mjd,md->mj", picked, gate_left, preferred_element_type=jnp.float32)
    up_dots = jnp.einsum("mjd,md->mj", picked, up_left, preferred_element_type=jnp.float32)
    gate_base, up_base = lax.psum((gate_part, up_part), "pop")
    gate_sums, up_sums = (
        lax.psum_scatter(gate_dots, "pop", scatter_dimension=0, tiled=True),
        lax.psum_scatter(up_dots, "pop", scatter_dimension=0, tiled=True),
    )
    own_ids = lax.dynamic_slice_in_dim(token_ids, group_index * group_size, group_size, 0)
    own_hidden = build_hidden(
        gate_base,
        up_base,
        own_ids,
        gate_sums * inverse_width,
        up_sums * inverse_width,
        gate_right,
        up_right,
    )
    hidden = lax.all_gather(own_hidden, "pop", axis=0, tiled=True)
    down_dots = jnp.einsum(
        "mjf,mf->mj",
        hidden.reshape(members, tokens, -1),
        left_down,
        preferred_element_type=jnp.float32,
    ).reshape(-1)
    summed = lax.psum_scatter(
        jnp.dot(hidden, down_matrix, preferred_element_type=jnp.float32),
        "tp",
        scatter_dimension=0,
        tiled=True,
    )
    own_dots = lax.psum_scatter(down_dots, "tp", scatter_dimension=0, tiled=True) * (
        1.0 / math.sqrt(FF)
    )
    members_here = rows_here // tokens
    right_block = lax.dynamic_slice_in_dim(down_right, unit_index * members_here, members_here, 0)
    extra = (
        spread
        * own_dots.reshape(members_here, tokens)[:, :, None]
        * right_block.astype(jnp.float32)[:, None, :]
    )
    raw_out = summed + extra.reshape(rows_here, slice_width)
    error = raw_out - target.astype(jnp.float32)
    partial_loss = jnp.sum((error * error).reshape(members_here, tokens * slice_width), axis=1) / (
        tokens * D
    )
    group_loss = lax.psum(partial_loss, "pop")
    losses = lax.all_gather(group_loss, "tp", axis=0, tiled=True)
    mean_loss = jnp.mean(losses)
    spread_loss = jnp.mean((losses - mean_loss) ** 2)
    weights = -(losses - mean_loss) / jnp.sqrt(spread_loss + epsilon) * (1.0 / math.sqrt(members))
    gate_scaled = weights[:, None] * gate_left.astype(jnp.float32)
    up_scaled = weights[:, None] * up_left.astype(jnp.float32)
    down_scaled = weights[:, None] * down_right.astype(jnp.float32)
    gate_update = outer_sum(gate_scaled, right_gate.astype(jnp.float32))
    up_update = outer_sum(up_scaled, right_up.astype(jnp.float32))
    down_update = outer_sum(left_down.astype(jnp.float32), down_scaled)
    return (raw_out, gate_update, up_update, down_update)


def solution(mesh):
    return jax.shard_map(
        per_device,
        mesh=mesh,
        in_specs=(
            P(None, "pop"),
            P(),
            P("pop", "tp"),
            P("pop", "tp"),
            P("tp", "pop"),
            P(None, "pop"),
            P("pop", "tp"),
            P(None, "pop"),
            P("pop", "tp"),
            P("pop", "tp"),
            P(None, "pop"),
            P("tp", "pop"),
        ),
        out_specs=(P("tp", "pop"), P("pop", "tp"), P("pop", "tp"), P("tp", "pop")),
        check_vma=False,
    )
```

profile of v0, /device:TPU:1, one launch (start us, length us, event | category | flops | bytes accessed | tf_op | source)
XLA Modules:
  0.0 840.9 jit_solution(1398454806246019871)
XLA Ops:
  7.2 0.9 copy.31
  8.1 0.7 compare_and_fusion
  8.9 3.0 copy.36
  11.9 1.1 copy.32
  13.0 0.2 reshape.95
  13.3 7.5 gather_fusion
  20.8 1.6 gather.10
  22.3 0.2 copy.30
  22.6 5.8 fusion
  28.4 2.0 copy.34
  30.5 5.1 fusion.1
  35.6 1.1 fusion.24
  36.7 2.1 fusion.23
  38.9 0.8 constant_dynamic-slice_fusion.1
  39.9 0.1 mul.134
  40.1 0.1 mul.127
  40.3 81.7 %reduce-scatter.12.cloned.1.call-done = f32[40,4]{1,0:T(8,128)} async-done(((f32[640,4]{1,0:T(8,128)}), f32[40,4]{1,0:T(8,128)}) %reduce-scatter.12.cloned.1.call-update) | async-done | bytes 656
  121.9 0.7 broadcast_multiply_fusion
  122.7 0.1 mul.131
  122.8 91.0 %reduce-scatter.10.cloned.1.call-done = f32[40,4]{1,0:T(8,128)} async-done(((f32[640,4]{1,0:T(8,128)}), f32[40,4]{1,0:T(8,128)}) %reduce-scatter.10.cloned.1.call-update) | async-done | bytes 656
  213.7 0.7 broadcast_multiply_fusion.1
  214.5 0.1 mul.124
  214.6 167.8 %all-reduce.7.cloned.1.call-done = (f32[256,512]{1,0:T(8,128)}, f32[256,512]{1,0:T(8,128)}) async-done(((f32[256,512]{1,0:T(8,128)}, f32[256,512]{1,0:T(8,128)}), (f32[256,512]{1,0:T(8,128)}, f32[256,512]{1,0:T(8,128)})) %all-reduce.7.cloned.1.call-update) | async-done | bytes 1048592 | tf_op jit(solution)/shard_map/psum | solution.py:72
  382.4 2.1 gather_fusion.2
  384.5 0.8 gather_fusion.1
  385.3 0.9 fusion.18
  386.2 76.2 %all-gather.2.cloned.1.call-done = bf16[2560,512]{1,0:T(8,128)(2,1)} async-done(((bf16[160,512]{1,0:T(8,128)(2,1)}), bf16[2560,512]{1,0:T(8,128)(2,1)}) %all-gather.2.cloned.1.call-update) | async-done | bytes 2621456 | tf_op jit(solution)/shard_map/all_gather | solution.py:87
  462.4 5.2 fusion.25
  467.6 1.2 constant_dynamic-slice_fusion
  468.9 0.7 mul.142
  469.6 0.6 fusion.22
  471.5 42.5 %all_gather.18 = bf16[640,512]{1,0:T(8,128)(2,1)} all-gather(bf16[40,512]{1,0:T(8,128)(2,1)S(1)} %copy-done.12), channel_id=1, replica_groups=mesh['pop'=16,'tp'=32] {'pop'}, dimensions={0}, use_global_device_ids=true | all-gather | bytes 696320 | tf_op jit(solution)/shard_map/all_gather | solution.py:63
  514.0 41.6 %all_gather.19 = bf16[640,512]{1,0:T(8,128)(2,1)} all-gather(bf16[40,512]{1,0:T(8,128)(2,1)} %param.22), channel_id=1, replica_groups=mesh['pop'=16,'tp'=32] {'pop'}, dimensions={0}, use_global_device_ids=true | all-gather | bytes 696320 | tf_op jit(solution)/shard_map/all_gather | solution.py:64
  555.6 43.7 %all_gather.16 = bf16[640,512]{1,0:T(8,128)(2,1)} all-gather(bf16[40,512]{1,0:T(8,128)(2,1)} %param.23), channel_id=1, replica_groups=mesh['pop'=16,'tp'=32] {'pop'}, dimensions={0}, use_global_device_ids=true | all-gather | bytes 696320 | tf_op jit(solution)/shard_map/all_gather | solution.py:65
  599.2 2.8 reshape.96
  602.0 4.2 fusion.2
  606.2 0.2 reshape.97
  606.4 120.2 %all-reduce.3 = f32[2560]{0:T(1024)S(1)} all-reduce(f32[2560]{0:T(1024)S(1)} %reshape.97), channel_id=5, replica_groups=mesh['pop'=16,'tp'=32] {'tp'}, use_global_device_ids=true, to_apply=%region_5.7.clone | all-reduce | flops 2560 | bytes 20480
  726.8 1.8 multiply_reduce_fusion
  728.7 0.1 reduce_sum.36
  728.8 32.5 %psum.23 = f32[20]{0:T(128)S(1)} all-reduce(f32[20]{0:T(128)S(1)} %broadcast_multiply_fusion.2), channel_id=1, replica_groups=mesh['pop'=16,'tp'=32] {'pop'}, use_global_device_ids=true, to_apply=%region_8.10 | all-reduce | flops 20 | bytes 160 | tf_op jit(solution)/shard_map/psum | solution.py:115
  761.4 0.2 dynamic-update-slice
  761.6 63.9 %all-reduce = f32[640]{0:T(1024)S(1)} all-reduce(f32[640]{0:T(1024)S(1)} %dynamic-update-slice), channel_id=1, replica_groups=mesh['pop'=16,'tp'=32] {'tp'}, use_global_device_ids=true, to_apply=%add | all-reduce | flops 640 | bytes 5120
  825.5 0.6 reduce_sum.37
  826.7 0.6 multiply_reduce_fusion.1
  828.1 2.8 convolution_bitcast_fusion
  830.8 1.8 fusion.11
  832.6 1.8 fusion.8
  (59 shorter events, 1.0 us)
Async XLA Ops:
  7.2 455.3 %copy-start = (bf16[512,320]{0,1:T(8,128)(2,1)S(1)}, bf16[512,320]{0,1:T(8,128)(2,1)}, u32[]{:S(2)}) copy-start(bf16[512,320]{0,1:T(8,128)(2,1)} %param.18) | copy-start | bytes 983044
  7.2 114.8 %reduce-scatter.12.cloned.1.call-start = ((), (), s32[]{:S(2)}) async-start(), calls=%async_computation.6 | async-start | bytes 348160
  22.6 5.9 copy-start.7
  22.6 7.9 copy-start.6
  28.4 185.4 %reduce-scatter.10.cloned.1.call-start = ((), (), s32[]{:S(2)}) async-start(), calls=%async_computation.5 | async-start | bytes 348160
  30.4 5.2 copy-start.9
  30.4 5.2 copy-start.11
  35.5 4.4 copy-start.13
  35.5 4.5 copy-start.12
  35.6 346.8 %all-reduce.7.cloned.1.call-start = ((), (), s32[]{:S(2)}) async-start(), calls=%async_computation.7 | async-start | bytes 2097152 | tf_op jit(solution)/shard_map/psum | solution.py:72
  38.8 423.6 %all-gather.2.cloned.1.call-start = ((), (), s32[]{:S(2)}) async-start(), calls=%async_computation.3 | async-start | bytes 2785280 | tf_op jit(solution)/shard_map/all_gather | solution.py:87
  382.4 2.1 copy-start.2
  386.2 340.6 %reduce-scatter.8.cloned.1.call-start = ((), (), s32[]{:S(2)}) async-start(), calls=%async_computation.4 | async-start | bytes 4055040 | tf_op jit(solution)/shard_map/reduce_scatter | solution.py:94
  467.6 2.1 copy-start.15
  467.6 131.6 %copy-start.1 = (bf16[2560,512]{1,0:T(8,128)(2,1)S(1)}, bf16[2560,512]{1,0:T(8,128)(2,1)}, u32[]{:S(2)}) copy-start(bf16[2560,512]{1,0:T(8,128)(2,1)} %all-gather.2.cloned.1.call-done) | copy-start | bytes 7864324
  602.0 124.8 %copy-start.10 = (f32[80,320]{1,0:T(8,128)S(1)}, f32[80,320]{1,0:T(8,128)}, u32[]{:S(2)}) copy-start(f32[80,320]{1,0:T(8,128)} %mul.142) | copy-start | bytes 307204
  602.0 124.8 %copy-start.14 = (bf16[80,320]{1,0:T(8,128)(2,1)S(1)}, bf16[80,320]{1,0:T(8,128)(2,1)}, u32[]{:S(2)}) copy-start(bf16[80,320]{1,0:T(8,128)(2,1)} %param.25) | copy-start | bytes 153604
  602.0 226.1 %copy-start.5 = (bf16[640,512]{1,0:T(8,128)(2,1)S(1)}, bf16[640,512]{1,0:T(8,128)(2,1)}, u32[]{:S(2)}) copy-start(bf16[640,512]{1,0:T(8,128)(2,1)} %all_gather.16) | copy-start | bytes 1966084
  606.2 224.6 %copy-start.4 = (bf16[640,512]{1,0:T(8,128)(2,1)S(1)}, bf16[640,512]{1,0:T(8,128)(2,1)}, u32[]{:S(2)}) copy-start(bf16[640,512]{1,0:T(8,128)(2,1)} %all_gather.18) | copy-start | bytes 1966084
  726.8 105.9 %copy-start.3 = (bf16[640,512]{1,0:T(8,128)(2,1)S(1)}, bf16[640,512]{1,0:T(8,128)(2,1)}, u32[]{:S(2)}) copy-start(bf16[640,512]{1,0:T(8,128)(2,1)} %all_gather.19) | copy-start | bytes 1966084
  726.8 105.9 %copy-start.8 = (bf16[640,320]{0,1:T(8,128)(2,1)S(1)}, bf16[640,320]{0,1:T(8,128)(2,1)}, u32[]{:S(2)}) copy-start(bf16[640,320]{0,1:T(8,128)(2,1)} %param.21) | copy-start | bytes 1228804
Sparse Core Ops, SparseCore 0:
  28.5 93.4 reduce-scatter.11
  126.0 87.6 reduce-scatter.9
  217.3 165.0 all-reduce.6
  386.3 76.0 all-gather.1
  467.7 130.0 reduce-scatter.7
where the time goes:
time: 842 us; the launch traced here: 841 us
  waiting for transfers between devices  417 us (50%)
  blocking collectives  344 us (41%)
  matrix products  29.7 us (4%)
  local copies, waits for them, and re-layouts  26.9 us (3%)
  between operations  16.7 us (2%)
    unnamed x2, blocking collectives  184 us
    unnamed x7, waiting for transfers between devices  173 us
    psum x1, waiting for transfers between devices, per_device(): gate_base, up_base = lax.psum((gate_part, up_part), 'pop')  168 us
    all_gather x1, waiting for transfers between devices, per_device(): hidden = lax.all_gather(own_hidden, 'pop', axis=0, tiled=True)  76.2 us
    all_gather x1, blocking collectives, per_device(): lax.all_gather(down_left, 'pop', axis=0, tiled=True)  43.7 us
    all_gather x1, blocking collectives, per_device(): lax.all_gather(gate_right, 'pop', axis=0, tiled=True)  42.5 us
    all_gather x1, blocking collectives, per_device(): lax.all_gather(up_right, 'pop', axis=0, tiled=True)  41.6 us
    psum x1, blocking collectives, per_device(): group_loss = lax.psum(partial_loss, 'pop')  32.5 us
  transfers between devices with their start and end apart: 5, of which 4 were waited for; matrix products, arithmetic and copies ran while one was open for 3% of the time, Pallas kernels for 0%

commit v1 on v0

v1 whole, which is shorter than its diff:
```python
import math

import jax
import jax.numpy as jnp
from jax import lax
from jax.experimental import pallas as pl
from jax.experimental.pallas import tpu as pltpu
from jax.sharding import Mesh, PartitionSpec as P

D = 5120
FF = 16384
MEMBERS = 640
TOKENS = 4
ROWS = MEMBERS * TOKENS
BANK = 256

spread = 0.5
epsilon = 1e-06

f32 = jnp.float32
bf16 = jnp.bfloat16

NX, NYH, NZ, NYL, NC = 4, 4, 8, 2, 2
POP = ("x", "yh")
TP = ("z", "yl", "c")
EVERY = POP + TP
GROUP = MEMBERS // (NX * NYH)
UNITS = 512
OWN = UNITS // (NX * NYH)
WIDTH = D // (NX * NYH)
X_ROWS = ROWS // NX
X_MEMBERS = MEMBERS // NX
BLOCK = ROWS // (NZ * NYL * NC)
BLOCK_MEMBERS = BLOCK // TOKENS
PADDED = 384


def position(x, yh, z, yl, c):
    return (((x * NYH + yh) * NZ + z) * NYL + yl) * NC + c


def to_owner():
    pairs = []
    for x in range(NX):
        for yh in range(NYH):
            for z in range(NZ):
                for yl in range(NYL):
                    for c in range(NC):
                        column, row = yl * NC + c, x * NZ + z
                        pairs.append((position(x, yh, z, yl, c), position(column, yh, 0, 0, 0) + row))
    return pairs


def split_three(value):
    high = value.astype(bf16)
    rest = value - high.astype(f32)
    middle = rest.astype(bf16)
    low = (rest - middle.astype(f32)).astype(bf16)
    return high, middle, low


def hidden_kernel(ids_ref, base_ref, dots_ref, rights_ref, out_ref):
    step = 128 * TOKENS
    scale = f32(1.0 / math.sqrt(D))
    base = jnp.concatenate(split_three(base_ref[...]), axis=0)
    repeat = (
        lax.broadcasted_iota(jnp.int32, (128, step), 1) // TOKENS
        == lax.broadcasted_iota(jnp.int32, (128, step), 0)
    ).astype(f32).astype(bf16)
    token = lax.broadcasted_iota(jnp.int32, (1, step), 1) % TOKENS
    for part in range(MEMBERS // 128):
        members = slice(part * 128, (part + 1) * 128)
        rows = slice(part * step, (part + 1) * step)
        chosen = (
            lax.broadcasted_iota(jnp.int32, (BANK, step), 0) == ids_ref[:, rows]
        ).astype(f32).astype(bf16)
        picked = jnp.dot(base, chosen, preferred_element_type=f32)
        picked = picked[: 2 * OWN] + picked[2 * OWN : 4 * OWN] + picked[4 * OWN :]
        dots = jnp.concatenate(split_three(dots_ref[:, members]), axis=0)
        dots = jnp.dot(dots, repeat, preferred_element_type=f32)
        dots = (dots[:8] + dots[8:16] + dots[16:]) * scale
        right = jnp.dot(rights_ref[:, members], repeat, preferred_element_type=f32)
        gate_dot = jnp.zeros((1, step), f32)
        up_dot = jnp.zeros((1, step), f32)
        for j in range(TOKENS):
            gate_dot = jnp.where(token == j, dots[j : j + 1], gate_dot)
            up_dot = jnp.where(token == j, dots[TOKENS + j : TOKENS + j + 1], up_dot)
        gate_pre = picked[:OWN] + spread * gate_dot * right[:OWN]
        up_pre = picked[OWN:] + spread * up_dot * right[OWN:]
        out_ref[:, rows] = (gate_pre / (1.0 + jnp.exp(-gate_pre)) * up_pre).astype(bf16)


def activate(ids, base, dots, rights):
    return pl.pallas_call(
        hidden_kernel,
        out_shape=jax.ShapeDtypeStruct((OWN, ROWS), bf16),
        compiler_params=pltpu.CompilerParams(vmem_limit_bytes=32 * 1024 * 1024),
    )(ids, base, dots, rights)


def outer_sum(left, right):
    high = lax.reduce_precision(left, 8, 7)
    low = left - high
    dims = (((0,), (0,)), ((), ()))
    return lax.dot_general(
        high.astype(bf16), right, dims, preferred_element_type=f32
    ) + lax.dot_general(low.astype(bf16), right, dims, preferred_element_type=f32)


def outer_sum_right(left, right):
    high = lax.reduce_precision(right, 8, 7)
    low = right - high
    dims = (((0,), (0,)), ((), ()))
    return lax.dot_general(
        left, high.astype(bf16), dims, preferred_element_type=f32
    ) + lax.dot_general(left, low.astype(bf16), dims, preferred_element_type=f32)


def per_device(
    states,
    token_ids,
    gate_matrix,
    up_matrix,
    down_matrix,
    gate_left,
    gate_right,
    up_left,
    up_right,
    down_left,
    down_right,
    target,
):
    x_index = lax.axis_index("x")
    tp_index = lax.axis_index(TP)

    down_all = lax.all_gather(down_matrix, "x", axis=0, tiled=True)
    left_down = lax.all_gather(
        down_left.reshape(GROUP * 4, UNITS // 4), POP, axis=0, tiled=True
    ).reshape(MEMBERS, UNITS)
    rights = lax.all_gather(
        jnp.concatenate([gate_right, up_right], axis=0), POP, axis=0, tiled=True
    ).reshape(NX * NYH, 2, GROUP, UNITS)
    right_gate = rights[:, 0].reshape(MEMBERS, UNITS)
    right_up = rights[:, 1].reshape(MEMBERS, UNITS)
    own_right = lax.dynamic_slice_in_dim(down_right, tp_index * BLOCK_MEMBERS, BLOCK_MEMBERS, 0)
    forth = to_owner()
    back = [(b, a) for a, b in forth]
    moved = lax.ppermute(jnp.concatenate([target, own_right], axis=0), EVERY, back)
    piece_target, piece_right = moved[:BLOCK].astype(f32), moved[BLOCK:].astype(f32)

    dims = (((0,), (1,)), ((), ()))
    gate_part = lax.dot_general(gate_matrix, states, dims, preferred_element_type=f32)
    up_part = lax.dot_general(up_matrix, states, dims, preferred_element_type=f32)
    ids = token_ids.T
    bank = lax.broadcasted_iota(jnp.int32, (BANK, MEMBERS), 0)
    dots = []
    for left in (gate_left, up_left):
        inner = lax.dot_general(states, left, (((1,), (1,)), ((), ())), preferred_element_type=f32)
        for j in range(TOKENS):
            dots.append(jnp.sum(jnp.where(bank == ids[j : j + 1], inner, 0.0), axis=0))
    dots = jnp.pad(jnp.stack(dots), ((0, 0), (0, 3 * BANK - MEMBERS)))
    dots = dots.reshape(8, 3, BANK).transpose(1, 0, 2).reshape(24, BANK)

    first = jnp.concatenate(
        [
            gate_part.reshape(NX, 128, BANK),
            up_part.reshape(NX, 128, BANK),
            jnp.broadcast_to(dots, (NX, 24, BANK)),
            jnp.concatenate(
                [
                    gate_right.astype(f32).reshape(GROUP, NX, 128),
                    up_right.astype(f32).reshape(GROUP, NX, 128),
                ],
                axis=2,
            ).transpose(1, 0, 2),
        ],
        axis=1,
    )
    first = lax.all_to_all(first, "x", 0, 0)
    summed = jnp.sum(first[:, :280], axis=0)
    factors = first[:, 280:].reshape(X_MEMBERS, 2, NYH, OWN)
    factors = factors.transpose(2, 1, 3, 0).reshape(NYH, 2 * OWN, X_MEMBERS)
    second = jnp.concatenate(
        [
            summed[:256]
            .reshape(2, NYH, OWN, BANK)
            .transpose(1, 0, 2, 3)
            .reshape(NYH, 2 * OWN, BANK),
            jnp.broadcast_to(summed[256:], (NYH, 24, BANK)),
            jnp.pad(factors, ((0, 0), (0, 0), (0, BANK - X_MEMBERS))),
        ],
        axis=1,
    )
    second = lax.all_to_all(second, "yh", 0, 0)
    summed = jnp.sum(second[:, :88], axis=0)
    base = summed[:64]
    dots = summed[64:].reshape(3, 8, BANK).transpose(1, 0, 2).reshape(8, 3 * BANK)[:, :MEMBERS]
    factors = second[:, 88:, :X_MEMBERS].astype(bf16).reshape(NYH, 2 * OWN, NX, GROUP)
    factors = factors.transpose(1, 2, 0, 3).reshape(2 * OWN, MEMBERS)
    own_hidden = activate(token_ids.reshape(1, ROWS), base, dots, factors)

    outgoing = jnp.broadcast_to(
        own_hidden.reshape(OWN, NX, X_ROWS).transpose(1, 0, 2)[:, None],
        (NX, NYH, OWN, X_ROWS),
    ).reshape(NX * NYH * OWN, X_ROWS)
    hidden = lax.all_to_all(outgoing, POP, 0, 0, tiled=True)

    x_left = lax.dynamic_slice_in_dim(left_down, x_index * X_MEMBERS, X_MEMBERS, 0)
    against = lax.dot_general(hidden, x_left, (((0,), (1,)), ((), ())), preferred_element_type=f32)
    own_member = (
        lax.broadcasted_iota(jnp.int32, (X_ROWS, X_MEMBERS), 0) // TOKENS
        == lax.broadcasted_iota(jnp.int32, (X_ROWS, X_MEMBERS), 1)
    )
    down_dots = jnp.sum(jnp.where(own_member, against, 0.0), axis=1, keepdims=True)
    at_dot = lax.broadcasted_iota(jnp.int32, (X_ROWS, PADDED), 1) == WIDTH
    slices = []
    for x in range(NX):
        part = lax.dot_general(
            hidden,
            down_all[x * UNITS : (x + 1) * UNITS],
            (((0,), (0,)), ((), ())),
            preferred_element_type=f32,
        )
        part = jnp.pad(part, ((0, 0), (0, PADDED - WIDTH)))
        slices.append(jnp.where(at_dot, down_dots, part))
    sent = jnp.stack([jnp.stack([slices[0], slices[2]]), jnp.stack([slices[1], slices[3]])])
    got = lax.all_to_all(sent, "c", 0, 0)
    pair = (got[0] + got[1]).astype(bf16)
    pair = pair.reshape(NYL, NZ, BLOCK, PADDED).transpose(1, 0, 2, 3)
    got = lax.all_to_all(pair.reshape(NZ * NYL, BLOCK, PADDED), ("z", "yl"), 0, 0)
    total = jnp.sum(got.astype(f32), axis=0)
    scaled_dot = spread * (total[:, WIDTH : WIDTH + 1] * (1.0 / math.sqrt(FF)))
    extra = scaled_dot.reshape(BLOCK_MEMBERS, TOKENS, 1) * piece_right[:, None, :]
    raw = total[:, :WIDTH] + extra.reshape(BLOCK, WIDTH)
    raw_out = lax.ppermute(raw, EVERY, forth)

    error = raw - piece_target
    part_loss = jnp.sum((error * error).reshape(BLOCK_MEMBERS, TOKENS * WIDTH), axis=1)
    lanes = jnp.pad(part_loss[None, :], ((0, 7), (0, 128 - BLOCK_MEMBERS)))
    near = lax.all_to_all(
        jnp.broadcast_to(lanes, (NYH * NYL * NC, 8, 128)), ("yh", "yl", "c"), 0, 0
    )
    block_loss = jnp.sum(near, axis=0)
    far = lax.all_to_all(jnp.broadcast_to(block_loss, (NX * NZ, 8, 128)), ("x", "z"), 0, 0)
    losses = far[:, 0, :BLOCK_MEMBERS].reshape(MEMBERS) / (TOKENS * D)

    mean_loss = jnp.mean(losses)
    spread_loss = jnp.mean((losses - mean_loss) ** 2)
    weights = -(losses - mean_loss) / jnp.sqrt(spread_loss + epsilon) * (1.0 / math.sqrt(MEMBERS))
    gate_update = outer_sum(weights[:, None] * gate_left.astype(f32), right_gate)
    up_update = outer_sum(weights[:, None] * up_left.astype(f32), right_up)
    down_update = outer_sum_right(left_down, weights[:, None] * down_right.astype(f32))
    return (raw_out, gate_update, up_update, down_update)


def solution(mesh):
    cut = Mesh(mesh.devices.reshape(NX, NYH, NZ, NYL, NC), EVERY)
    return jax.shard_map(
        per_device,
        mesh=cut,
        in_specs=(
            P(None, POP),
            P(),
            P(POP, TP),
            P(POP, TP),
            P(TP, POP),
            P(None, POP),
            P(POP, TP),
            P(None, POP),
            P(POP, TP),
            P(POP, TP),
            P(None, POP),
            P(TP, POP),
        ),
        out_specs=(P(TP, POP), P(POP, TP), P(POP, TP), P(TP, POP)),
        check_vma=False,
    )
```

time: 842 us -> 226 us (0.27)
  waiting for transfers between devices: 417 us -> 52.2 us
  blocking collectives: 344 us -> 80 us
  starting transfers between devices: 0.21 us -> 47 us
  matrix products: 29.7 us -> 12.2 us
  local copies, waits for them, and re-layouts: 26.9 us -> 9.69 us
    unnamed x2 -> x0, blocking collectives: 184 us -> none
    unnamed x7 -> x2, waiting for transfers between devices: 173 us -> 0.73 us
    psum x1 -> x0, waiting for transfers between devices: 168 us -> none  [per_device(): gate_base, up_base = lax.psum((gate_part, up_part), 'pop')]
    all_gather x3 -> x1, blocking collectives: 128 us -> 49.1 us  [per_device(): lax.all_gather(down_left.reshape(GROUP * 4, UNITS // 4), POP, axis=0, til...]
    all_gather x1 -> x2, waiting for transfers between devices: 76.2 us -> 6.43 us  [the longest x1 6.41 us: per_device(): lax.all_gather(jnp.concatenate([gate_right, up_right], axis=0), POP, axis...]
    all_to_all x0 -> x5, starting transfers between devices: none -> 40.9 us  [the longest x1 13.3 us: per_device(): lax.all_to_all(pair.reshape(NZ * NYL, BLOCK, PADDED), ('z', 'yl'), 0, 0)]
    psum x1 -> x0, blocking collectives: 32.5 us -> none  [per_device(): group_loss = lax.psum(partial_loss, 'pop')]
    all_to_all x0 -> x2, blocking collectives: none -> 30.8 us  [the longest x1 17.9 us: per_device(): first = lax.all_to_all(first, 'x', 0, 0)]
  transfers between devices with their start and end apart: 5 -> 9, of which waited for: 4 -> 5; matrix products, arithmetic and copies ran while one was open for 3% -> 3% of each run, Pallas kernels for 0% -> 0%
where the time goes in v1:
time: 226 us; the launch traced here: 224 us
  blocking collectives  80 us (35%)
  waiting for transfers between devices  52.2 us (23%)
  starting transfers between devices  47 us (21%)
  between operations  17.5 us (8%)
  matrix products  12.2 us (5%)
  local copies, waits for them, and re-layouts  9.69 us (4%)
  other arithmetic  4.78 us (2%)
    all_gather x1, blocking collectives, per_device(): lax.all_gather(down_left.reshape(GROUP * 4, UNITS // 4), POP, axis=0, til...  49.1 us
    ppermute x1, waiting for transfers between devices, per_device(): lax.ppermute(jnp.concatenate([target, own_right], axis=0), EVERY, back)  22 us
    all_to_all x1, blocking collectives, per_device(): first = lax.all_to_all(first, 'x', 0, 0)  17.9 us
    all_to_all x1, waiting for transfers between devices, per_device(): second = lax.all_to_all(second, 'yh', 0, 0)  15.8 us
    all_to_all x1, starting transfers between devices, per_device(): lax.all_to_all(pair.reshape(NZ * NYL, BLOCK, PADDED), ('z', 'yl'), 0, 0)  13.3 us
    all_to_all x1, blocking collectives, per_device(): got = lax.all_to_all(sent, 'c', 0, 0)  12.9 us
    all_to_all x1, starting transfers between devices, per_device(): second = lax.all_to_all(second, 'yh', 0, 0)  10.5 us
    all_to_all x1, starting transfers between devices, per_device(): lax.all_to_all(jnp.broadcast_to(block_loss, (NX * NZ, 8, 128)), ('x', 'z'...  6.58 us
  transfers between devices with their start and end apart: 9, of which 5 were waited for; matrix products, arithmetic and copies ran while one was open for 3% of the time, Pallas kernels for 0%

profile of v1, /device:TPU:1, one launch (start us, length us, event | category | flops | bytes accessed | tf_op | source)
XLA Modules:
  0.0 224.3 jit_solution(918632217298221736)
XLA Ops:
  8.0 0.9 slice_reduce_fusion.2
  8.9 1.5 fusion.36
  10.4 1.9 select_reduce_fusion.4
  12.6 0.3 fusion.34
  12.9 0.4 copy-done.6
  13.3 0.3 fusion.35
  13.8 17.9 %all_to_all.42 = f32[4,320,256]{2,1,0:T(8,128)S(1)} all-to-all(f32[4,320,256]{2,1,0:T(8,128)S(1)} %pad_maximum_fusion.1), channel_id=1, replica_groups=mesh['x'=4,'yh'=4,'z'=8,'yl'=2,'c'=2] {'x'}, dimensions={0} | all-to-all | bytes 2621440 | tf_op jit(solution)/shard_map/all_to_all | solution.py:179
  32.1 0.3 reshape.115
  32.4 0.9 select_maximum_fusion
  33.3 10.5 %all-to-all-start.1 = ((f32[4,152,256]{2,1,0:T(8,128)}), f32[4,152,256]{2,1,0:T(8,128)S(1)}, u32[]{:S(2)}, u32[]{:S(2)}) async-start(f32[4,152,256]{2,1,0:T(8,128)} %select_maximum_fusion), calls=%async_computation.1 | async-start | bytes 1245184 | tf_op jit(solution)/shard_map/all_to_all | solution.py:194
  43.9 0.7 all-gather.3.cloned.1.call-update
  45.0 15.8 %all-to-all-done.1 = f32[4,152,256]{2,1,0:T(8,128)S(1)} async-done(((f32[4,152,256]{2,1,0:T(8,128)}), f32[4,152,256]{2,1,0:T(8,128)S(1)}, u32[]{:S(2)}, u32[]{:S(2)}) %all-to-all-start.1) | async-done | bytes 622624 | tf_op jit(solution)/shard_map/all_to_all | solution.py:194
  61.3 0.9 shard_map.147
  62.3 0.9 broadcast_in_dim.61
  63.2 4.9 %all-to-all-start.2 = ((bf16[16,32,640]{2,1,0:T(8,128)(2,1)}), bf16[16,32,640]{2,1,0:T(8,128)(2,1)S(1)}, u32[]{:S(2)}, u32[]{:S(2)}) async-start(bf16[16,32,640]{2,1,0:T(8,128)(2,1)} %bitcast.18), calls=%async_computation.2 | async-start | bytes 1310720 | tf_op jit(solution)/shard_map/all_to_all | solution.py:206
  68.2 49.1 %all_gather.9 = bf16[2560,128]{1,0:T(8,128)(2,1)S(1)} all-gather(bf16[160,128]{1,0:T(8,128)(2,1)S(1)} %reshape.122), channel_id=1, replica_groups=mesh['x'=4,'yh'=4,'z'=8,'yl'=2,'c'=2] {'x','yh'}, dimensions={0}, use_global_device_ids=true | all-gather | bytes 696320 | tf_op jit(solution)/shard_map/all_gather | solution.py:137
  117.3 0.4 reshape.123
  117.7 0.3 fusion.2
  118.1 1.5 fusion.18
  119.6 0.4 fusion.20
  120.0 0.4 fusion.22
  120.5 0.4 fusion.24
  120.9 0.3 select_bitcast_fusion.3
  121.8 12.9 %all_to_all.43 = f32[2,2,640,384]{2,3,1,0:T(8,128)S(1)} all-to-all(f32[2,2,640,384]{2,3,1,0:T(8,128)S(1)} %pad_maximum_fusion), channel_id=1, replica_groups=mesh['x'=4,'yh'=4,'z'=8,'yl'=2,'c'=2] {'c'}, dimensions={0} | all-to-all | bytes 7864320 | tf_op jit(solution)/shard_map/all_to_all | solution.py:227
  134.9 0.7 copy.96
  135.5 1.1 copy.97
  136.6 13.3 %all-to-all-start.4 = ((bf16[16,80,384]{2,1,0:T(8,128)(2,1)}), bf16[16,80,384]{2,1,0:T(8,128)(2,1)S(1)}, u32[]{:S(2)}, u32[]{:S(2)}) async-start(bf16[16,80,384]{2,1,0:T(8,128)(2,1)} %bitcast.28), calls=%async_computation.4 | async-start | bytes 1966080 | tf_op jit(solution)/shard_map/all_to_all | solution.py:230
  150.0 0.6 pad_maximum_fusion.2
  150.9 4.1 %collective-permute-start = (bf16[100,320]{1,0:T(8,128)(2,1)S(1)}, bf16[100,320]{1,0:T(8,128)(2,1)S(1)}, u32[]{:S(2)}, u32[]{:S(2)}) collective-permute-start(bf16[100,320]{1,0:T(8,128)(2,1)S(1)} %pad_maximum_fusion.3), channel_id=1, source_target_pairs={{0,0},{128,1},{256,2},{384,3},{1,4},{129,5},{257,6},{385,7},{2,8},... | collective-permute-start | bytes 192008 | tf_op jit(solution)/shard_map/ppermute | solution.py:148
  155.0 22.0 %collective-permute-done = bf16[100,320]{1,0:T(8,128)(2,1)S(1)} collective-permute-done((bf16[100,320]{1,0:T(8,128)(2,1)S(1)}, bf16[100,320]{1,0:T(8,128)(2,1)S(1)}, u32[]{:S(2)}, u32[]{:S(2)}) %collective-permute-start) | collective-permute-done | bytes 64032 | tf_op jit(solution)/shard_map/ppermute | solution.py:148
  177.8 0.6 broadcast_in_dim.65
  178.5 5.6 %all-to-all-start.5 = ((f32[16,8,128]{2,1,0:T(8,128)}), f32[16,8,128]{2,1,0:T(8,128)S(1)}, u32[]{:S(2)}, u32[]{:S(2)}) async-start(f32[16,8,128]{2,1,0:T(8,128)} %broadcast_in_dim.65), calls=%async_computation.5 | async-start | bytes 131072 | tf_op jit(solution)/shard_map/all_to_all | solution.py:240
  184.1 2.0 collective-permute-start.1
  186.1 5.8 %all-to-all-done.5 = f32[16,8,128]{2,1,0:T(8,128)S(1)} async-done(((f32[16,8,128]{2,1,0:T(8,128)}), f32[16,8,128]{2,1,0:T(8,128)S(1)}, u32[]{:S(2)}, u32[]{:S(2)}) %all-to-all-start.5) | async-done | bytes 65568 | tf_op jit(solution)/shard_map/all_to_all | solution.py:240
  191.9 0.7 broadcast_in_dim.66
  192.6 6.6 %all-to-all-start.6 = ((f32[32,8,128]{2,1,0:T(8,128)}), f32[32,8,128]{2,1,0:T(8,128)S(1)}, u32[]{:S(2)}, u32[]{:S(2)}) async-start(f32[32,8,128]{2,1,0:T(8,128)} %broadcast_in_dim.66), calls=%async_computation.6 | async-start | bytes 262144 | tf_op jit(solution)/shard_map/all_to_all | solution.py:244
  199.2 6.4 %all-gather.5.cloned.1.call-done = bf16[1280,512]{1,0:T(8,128)(2,1)} async-done(((bf16[80,512]{1,0:T(8,128)(2,1)}), bf16[1280,512]{1,0:T(8,128)(2,1)}) %all-gather.5.cloned.1.call-update) | async-done | bytes 1310736 | tf_op jit(solution)/shard_map/all_gather | solution.py:140
  205.6 1.4 fusion.33
  207.0 1.4 all-to-all-done.6
  208.3 0.6 fusion.32
  209.6 0.6 multiply_reduce_fusion.2
  211.1 0.4 fusion.11
  211.6 1.3 fusion.1
  212.9 0.4 fusion.10
  213.3 1.3 convolution_add_fusion.1
  214.6 0.4 fusion.9
  215.0 1.3 convolution_add_fusion.2
  216.3 0.6 copy.110
  (89 shorter events, 3.5 us)
Async XLA Ops:
  8.0 4.6 %copy-start = (bf16[320,512]{1,0:T(8,128)(2,1)S(1)}, bf16[320,512]{1,0:T(8,128)(2,1)}, u32[]{:S(2)}) copy-start(bf16[320,512]{1,0:T(8,128)(2,1)} %param.14) | copy-start | bytes 983044
  10.4 2.2 copy-start.4
  12.3 1.0 copy-start.6
  12.3 1.3 copy-start.7
  12.3 1.3 copy-start.8
  32.4 12.2 %copy-start.11 = (s32[640,4]{0,1:T(4,128)S(1)}, s32[640,4]{0,1:T(4,128)}, u32[]{:S(2)}) copy-start(s32[640,4]{0,1:T(4,128)} %param.13) | copy-start | bytes 30724
  33.3 27.5 %all-to-all-start.1 = ((f32[4,152,256]{2,1,0:T(8,128)}), f32[4,152,256]{2,1,0:T(8,128)S(1)}, u32[]{:S(2)}, u32[]{:S(2)}) async-start(f32[4,152,256]{2,1,0:T(8,128)} %select_maximum_fusion), calls=%async_computation.1 | async-start | bytes 1245184 | tf_op jit(solution)/shard_map/all_to_all | solution.py:194
  43.9 74.2 %all-gather.3.cloned.1.call-start = ((), (), s32[]{:S(2)}) async-start(), calls=%async_computation.7 | async-start | bytes 1638400 | tf_op jit(solution)/shard_map/all_gather | solution.py:136
  62.3 5.9 %copy-start.10 = (bf16[40,512]{1,0:T(8,128)(2,1)S(1)}, bf16[40,512]{1,0:T(8,128)(2,1)}, u32[]{:S(2)}) copy-start(bf16[40,512]{1,0:T(8,128)(2,1)} %param.21) | copy-start | bytes 122884
  63.2 54.5 %all-to-all-start.2 = ((bf16[16,32,640]{2,1,0:T(8,128)(2,1)}), bf16[16,32,640]{2,1,0:T(8,128)(2,1)S(1)}, u32[]{:S(2)}, u32[]{:S(2)}) async-start(bf16[16,32,640]{2,1,0:T(8,128)(2,1)} %bitcast.18), calls=%async_computation.2 | async-start | bytes 1310720 | tf_op jit(solution)/shard_map/all_to_all | solution.py:206
  118.1 1.5 copy-start.5
  136.6 14.0 %copy-start.2 = (bf16[640,320]{0,1:T(8,128)(2,1)S(1)}, bf16[640,320]{0,1:T(8,128)(2,1)}, u32[]{:S(2)}) copy-start(bf16[640,320]{0,1:T(8,128)(2,1)} %param.22) | copy-start | bytes 1228804
  136.6 14.2 %copy-start.9 = (bf16[80,320]{1,0:T(8,128)(2,1)S(1)}, bf16[80,320]{1,0:T(8,128)(2,1)}, u32[]{:S(2)}) copy-start(bf16[80,320]{1,0:T(8,128)(2,1)} %param.23) | copy-start | bytes 153604
  136.6 40.5 %all-to-all-start.4 = ((bf16[16,80,384]{2,1,0:T(8,128)(2,1)}), bf16[16,80,384]{2,1,0:T(8,128)(2,1)S(1)}, u32[]{:S(2)}, u32[]{:S(2)}) async-start(bf16[16,80,384]{2,1,0:T(8,128)(2,1)} %bitcast.28), calls=%async_computation.4 | async-start | bytes 1966080 | tf_op jit(solution)/shard_map/all_to_all | solution.py:230
  149.9 55.7 %all-gather.5.cloned.1.call-start = ((), (), s32[]{:S(2)}) async-start(), calls=%async_computation.8 | async-start | bytes 1392640 | tf_op jit(solution)/shard_map/all_gather | solution.py:140
  150.9 26.1 %collective-permute-start = (bf16[100,320]{1,0:T(8,128)(2,1)S(1)}, bf16[100,320]{1,0:T(8,128)(2,1)S(1)}, u32[]{:S(2)}, u32[]{:S(2)}) collective-permute-start(bf16[100,320]{1,0:T(8,128)(2,1)S(1)} %pad_maximum_fusion.3), channel_id=1, source_target_pairs={{0,0},{128,1},{256,2},{384,3},{1,4},{129,5},{257,6},{385,7},{2,8},... | collective-permute-start | bytes 192008 | tf_op jit(solution)/shard_map/ppermute | solution.py:148
  178.5 13.4 %all-to-all-start.5 = ((f32[16,8,128]{2,1,0:T(8,128)}), f32[16,8,128]{2,1,0:T(8,128)S(1)}, u32[]{:S(2)}, u32[]{:S(2)}) async-start(f32[16,8,128]{2,1,0:T(8,128)} %broadcast_in_dim.65), calls=%async_computation.5 | async-start | bytes 131072 | tf_op jit(solution)/shard_map/all_to_all | solution.py:240
  184.1 22.9 %collective-permute-start.1 = (f32[80,320]{1,0:T(8,128)S(1)}, f32[80,320]{1,0:T(8,128)S(1)}, u32[]{:S(2)}, u32[]{:S(2)}) collective-permute-start(f32[80,320]{1,0:T(8,128)S(1)} %get-tuple-element.21), channel_id=1, source_target_pairs={{0,0},{1,128},{2,256},{3,384},{4,1},{5,129},{6,257},{7,385},{8,2},... | collective-permute-start | bytes 307208 | tf_op jit(solution)/shard_map/ppermute | solution.py:235
  192.6 15.7 %all-to-all-start.6 = ((f32[32,8,128]{2,1,0:T(8,128)}), f32[32,8,128]{2,1,0:T(8,128)S(1)}, u32[]{:S(2)}, u32[]{:S(2)}) async-start(f32[32,8,128]{2,1,0:T(8,128)} %broadcast_in_dim.66), calls=%async_computation.6 | async-start | bytes 262144 | tf_op jit(solution)/shard_map/all_to_all | solution.py:244
  211.6 1.3 copy-start.1
  213.3 1.3 copy-start.3
Sparse Core Ops, SparseCore 0:
  46.8 41.9 all-gather.2
Sparse Core Ops, SparseCore 1:
  154.0 51.5 all-gather.4

commit v2 on v1

v2 whole, which is shorter than its diff:
```python
import math

import jax
import jax.numpy as jnp
from jax import lax
from jax.experimental import pallas as pl
from jax.experimental.pallas import tpu as pltpu
from jax.sharding import Mesh, PartitionSpec as P

D = 5120
FF = 16384
MEMBERS = 640
TOKENS = 4
ROWS = MEMBERS * TOKENS
BANK = 256

spread = 0.5
epsilon = 1e-06

f32 = jnp.float32
bf16 = jnp.bfloat16

NX, NYH, NZH, NZL, NYL, NC = 4, 4, 4, 2, 2, 2
POP = ("x", "yh")
TP = ("zh", "zl", "yl", "c")
EVERY = POP + TP
GROUP = MEMBERS // (NX * NYH)
UNITS = 512
OWN = UNITS // (NX * NYH)
WIDTH = D // (NX * NYH)
CHUNK = 128
CHUNKS = MEMBERS // CHUNK
PART = ROWS // (NX * NC)
BLOCK = ROWS // (NZH * NZL * NYL * NC)
BLOCK_MEMBERS = BLOCK // TOKENS
PADDED = 384
REST = PADDED - PART
KEPT = UNITS + CHUNK


def to_owner():
    pairs = []
    for x in range(NX):
        for yh in range(NYH):
            for zh in range(NZH):
                for column in range(NZL * NYL):
                    for c in range(NC):
                        here = (x * NYH + yh) * 32 + (zh * 4 + column) * NC + c
                        row = (zh * NX + x) * NC + c
                        pairs.append((here, (column * NYH + yh) * 32 + row))
    return pairs


def split_three(value):
    high = value.astype(bf16)
    rest = value - high.astype(f32)
    middle = rest.astype(bf16)
    low = (rest - middle.astype(f32)).astype(bf16)
    return high, middle, low


SMEM = pl.BlockSpec(memory_space=pltpu.SMEM)
VMEM = pl.BlockSpec(memory_space=pltpu.VMEM)
ANY = pl.BlockSpec(memory_space=pl.ANY)
PARAMS = pltpu.CompilerParams(vmem_limit_bytes=40 * 1024 * 1024)
WIDE = pltpu.CompilerParams(vmem_limit_bytes=60 * 1024 * 1024)
NT = (((1,), (1,)), ((), ()))


def fetch(sources, targets, arrived):
    copies = [
        pltpu.make_async_copy(source, target, arrived.at[k])
        for k, (source, target) in enumerate(zip(sources, targets, strict=True))
    ]
    for copy in copies:
        copy.start()
    return copies


def front_kernel(*refs):
    out_ref, held, arrived = refs[9], refs[10:19], refs[19]
    copies = fetch(refs[:9], held, arrived)
    ids_ref, states_ref, gate_left_ref, up_left_ref, gate_ref, up_ref = held[:6]
    copies[0].wait()
    copies[1].wait()
    states = jnp.transpose(states_ref[...].astype(f32)).astype(bf16)
    bank = lax.broadcasted_iota(jnp.int32, (BANK, MEMBERS), 0)
    line = lax.broadcasted_iota(jnp.int32, (8, MEMBERS), 0)
    dots = jnp.zeros((8, MEMBERS), f32)
    for kind, left in enumerate((gate_left_ref, up_left_ref)):
        copies[2 + kind].wait()
        inner = jnp.dot(states, left[...], preferred_element_type=f32)
        for j in range(TOKENS):
            chosen = jnp.where(bank == ids_ref[j : j + 1, :], inner, 0.0)
            row = jnp.sum(chosen, axis=0, keepdims=True)
            dots = jnp.where(line == kind * TOKENS + j, row, dots)
    groups = [x * NYH + yh for yh in range(NYH) for x in range(NX)]
    dots = jnp.concatenate([dots[:, g * GROUP : (g + 1) * GROUP] for g in groups], axis=1)
    for kind, matrix in enumerate((gate_ref, up_ref)):
        copies[4 + kind].wait()
        part = jnp.dot(states, matrix[...], preferred_element_type=f32)
        for x in range(NX):
            out_ref[x, kind * BANK : (kind + 1) * BANK] = part[:, x * CHUNK : (x + 1) * CHUNK]
    for kind in range(3):
        copies[6 + kind].wait()
        start = 2 * BANK + kind * GROUP
        for x in range(NX):
            out_ref[x, start : start + GROUP] = held[6 + kind][
                :, x * CHUNK : (x + 1) * CHUNK
            ].astype(f32)
    for x in range(NX):
        for k in range(CHUNKS):
            start = 2 * BANK + 3 * GROUP + 8 * k
            out_ref[x, start : start + 8] = dots[:, k * CHUNK : (k + 1) * CHUNK]


def front(*arrays):
    return pl.pallas_call(
        front_kernel,
        out_shape=jax.ShapeDtypeStruct((NX, 2 * BANK + 4 * GROUP, CHUNK), f32),
        in_specs=[ANY] * 9,
        scratch_shapes=[pltpu.VMEM(array.shape, array.dtype) for array in arrays]
        + [pltpu.SemaphoreType.DMA((9,))],
        compiler_params=WIDE,
    )(*arrays)


def middle_kernel(got_ref, out_ref):
    base = got_ref[0, : 2 * BANK]
    dots = got_ref[0, 2 * BANK + 3 * GROUP :]
    for x in range(1, NX):
        base += got_ref[x, : 2 * BANK]
        dots += got_ref[x, 2 * BANK + 3 * GROUP :]
    base = jnp.transpose(base)
    rights = []
    for kind in range(3):
        start = 2 * BANK + kind * GROUP
        rights += [got_ref[x, start : start + GROUP] for x in range(NX)]
    rights.append(jnp.zeros((2 * BANK - 3 * NX * GROUP, CHUNK), f32))
    rights = jnp.transpose(jnp.concatenate(rights, axis=0))
    for yh in range(NYH):
        out_ref[yh, :OWN] = base[yh * OWN : (yh + 1) * OWN]
        out_ref[yh, OWN : 2 * OWN] = rights[yh * OWN : (yh + 1) * OWN]
        out_ref[yh, 2 * OWN + 8 :] = jnp.zeros((8, 2 * BANK), f32)
        for k in range(CHUNKS):
            line = 2 * OWN + 8 * (k // 4)
            lane = (k % 4) * CHUNK
            out_ref[yh, line : line + 8, lane : lane + CHUNK] = dots[8 * k : 8 * k + 8]


def middle(got):
    return pl.pallas_call(
        middle_kernel,
        out_shape=jax.ShapeDtypeStruct((NYH, 2 * OWN + 16, 2 * BANK), f32),
        compiler_params=PARAMS,
    )(got)


def columns_kernel(place_ref, down_ref, right_ref, *out_refs):
    member = lax.broadcasted_iota(jnp.int32, (MEMBERS, CHUNK), 0)
    lane = lax.broadcasted_iota(jnp.int32, (MEMBERS, CHUNK), 1)
    quarter = BLOCK_MEMBERS
    row = sum((lane >= k * quarter).astype(jnp.int32) for k in range(1, NZH))
    wanted = lane + row * (NX * NC - 1) * quarter
    right = right_ref[...]
    for out_ref in out_refs:
        out_ref[:, :UNITS] = down_ref[...]
    for k in range(NX):
        start = (lax.rem(place_ref[0] + k, NX) * NC + place_ref[2]) * quarter
        chosen = member == jnp.where(lane < NZH * quarter, wanted + start, MEMBERS)
        chosen = jnp.dot(
            right, chosen.astype(f32).astype(bf16), preferred_element_type=f32
        ).astype(bf16)
        if k == 2:
            for out_ref in out_refs[1:]:
                out_ref[:, KEPT:] = chosen
        else:
            out_refs[(0, 1, None, 2)[k]][:, UNITS:KEPT] = chosen


def down_columns(place, down, right):
    own = jax.ShapeDtypeStruct((WIDTH, KEPT), bf16)
    leaving = jax.ShapeDtypeStruct((WIDTH, KEPT + CHUNK), bf16)
    return pl.pallas_call(
        columns_kernel,
        out_shape=[own, leaving, leaving],
        in_specs=[SMEM, VMEM, VMEM],
        compiler_params=PARAMS,
    )(place, down, right)


def hidden_kernel(ids_ref, got_ref, out_ref, hidden_ref, down_ref):
    base = got_ref[0, :OWN]
    all_dots = got_ref[0, 2 * OWN :]
    for yh in range(1, NYH):
        base += got_ref[yh, :OWN]
        all_dots += got_ref[yh, 2 * OWN :]
    along = NX * GROUP
    rights = [
        jnp.concatenate(
            [
                got_ref[yh, OWN : 2 * OWN, kind * along : (kind + 1) * along]
                for yh in range(NYH)
            ],
            axis=1,
        )
        for kind in range(3)
    ]
    rights = jnp.concatenate(rights, axis=0).astype(bf16)
    step = CHUNK * TOKENS
    scale = f32(1.0 / math.sqrt(D))
    base = jnp.concatenate([base[:, :BANK], base[:, BANK:]], axis=0)
    base = jnp.concatenate(split_three(base), axis=0)
    repeat = (
        lax.broadcasted_iota(jnp.int32, (CHUNK, step), 1) // TOKENS
        == lax.broadcasted_iota(jnp.int32, (CHUNK, step), 0)
    ).astype(f32).astype(bf16)
    token = lax.broadcasted_iota(jnp.int32, (1, step), 1) % TOKENS
    for part in range(CHUNKS):
        rows = slice(part * step, (part + 1) * step)
        chosen = (
            lax.broadcasted_iota(jnp.int32, (BANK, step), 0) == ids_ref[:, rows]
        ).astype(f32).astype(bf16)
        picked = jnp.dot(base, chosen, preferred_element_type=f32)
        picked = picked[: 2 * OWN] + picked[2 * OWN : 4 * OWN] + picked[4 * OWN :]
        line, lane = 8 * (part // 4), (part % 4) * CHUNK
        dots = all_dots[line : line + 8, lane : lane + CHUNK]
        dots = jnp.concatenate(split_three(dots), axis=0)
        dots = jnp.dot(dots, repeat, preferred_element_type=f32)
        dots = (dots[:8] + dots[8:16] + dots[16:]) * scale
        right = jnp.dot(
            rights[:, part * CHUNK : (part + 1) * CHUNK], repeat, preferred_element_type=f32
        )
        gate_dot = jnp.zeros((1, step), f32)
        up_dot = jnp.zeros((1, step), f32)
        for j in range(TOKENS):
            gate_dot = jnp.where(token == j, dots[j : j + 1], gate_dot)
            up_dot = jnp.where(token == j, dots[TOKENS + j : TOKENS + j + 1], up_dot)
        gate_pre = picked[:OWN] + spread * gate_dot * right[:OWN]
        up_pre = picked[OWN:] + spread * up_dot * right[OWN : 2 * OWN]
        hidden = (gate_pre / (1.0 + jnp.exp(-gate_pre)) * up_pre).astype(bf16)
        hidden_ref[:, rows] = hidden
        down_ref[:, rows] = jnp.sum(
            hidden.astype(f32) * right[2 * OWN :], axis=0, keepdims=True
        )
    line = lax.broadcasted_iota(jnp.int32, (OWN, REST), 0)
    for x in range(NX):
        for c in range(NC):
            starts = [((x * NZH + zh) * NC + c) * BLOCK for zh in range(NZH)]
            dots = jnp.concatenate([down_ref[:, k : k + BLOCK] for k in starts], axis=1)
            down = jnp.zeros((OWN, REST), f32)
            for k in range(PART // REST):
                piece = dots[:, k * REST : (k + 1) * REST]
                high = piece.astype(bf16).astype(f32)
                down = jnp.where(line == k, high, down)
                down = jnp.where(line == k + 8, piece - high, down)
            block = jnp.concatenate(
                [hidden_ref[:, k : k + BLOCK].astype(f32) for k in starts] + [down], axis=1
            ).astype(bf16)
            for yh in range(NYH):
                out_ref[c, x, yh] = block


def activate(ids, got):
    return pl.pallas_call(
        hidden_kernel,
        out_shape=jax.ShapeDtypeStruct((NC, NX, NYH, OWN, PADDED), bf16),
        scratch_shapes=[pltpu.VMEM((OWN, ROWS), bf16), pltpu.VMEM((1, ROWS), f32)],
        compiler_params=PARAMS,
    )(ids, got)


def project_kernel(place_ref, hidden_ref, *refs):
    out_ref, held, arrived = refs[2 * NX], refs[2 * NX + 1 : 4 * NX + 1], refs[4 * NX + 1]
    own = list(refs[:NX])
    own[1], own[3] = own[1].at[:, :KEPT], own[3].at[:, :KEPT]
    other = [ref.at[:, :UNITS] for ref in refs[NX : 2 * NX]]
    copies = fetch(own + other, held, arrived)
    own_refs, other_refs = held[:NX], held[NX:]
    x_here, c_here = place_ref[0], place_ref[2]
    dots = jnp.zeros((16, CHUNK), f32)
    for source in range(NC * NX * NYH):
        dots += hidden_ref[source * OWN : source * OWN + 16, PADDED - CHUNK :].astype(f32)
    dots = dots[:8] + dots[8:]
    eye = lax.broadcasted_iota(jnp.int32, (REST, REST), 0) == lax.broadcasted_iota(
        jnp.int32, (REST, REST), 1
    )
    columns = []
    for k in range(PART // REST):
        row = dots[k : k + 1, CHUNK - REST :]
        columns.append(jnp.sum(jnp.where(eye, row, 0.0), axis=1, keepdims=True))
    dot = jnp.concatenate(columns, axis=0) * f32(spread / math.sqrt(FF))
    own_member = (
        lax.broadcasted_iota(jnp.int32, (PART, CHUNK), 0) // TOKENS
        == lax.broadcasted_iota(jnp.int32, (PART, CHUNK), 1)
    )
    shares = jnp.where(own_member, dot, 0.0)
    high = shares.astype(bf16)
    low = (shares - high.astype(f32)).astype(bf16)
    shares = jnp.concatenate([high, low], axis=1)
    start = pl.multiple_of(c_here * UNITS, UNITS)
    own_rows = hidden_ref[pl.ds(start, UNITS), :].astype(f32)
    start = pl.multiple_of((1 - c_here) * UNITS, UNITS)
    other_rows = hidden_ref[pl.ds(start, UNITS), :].astype(f32)
    own_rows = jnp.transpose(own_rows)[:PART].astype(bf16)
    other_rows = jnp.transpose(other_rows)[:PART].astype(bf16)
    for k in range(NX):
        x = lax.rem(x_here - k + NX, NX)
        copies[k].wait()
        copies[NX + k].wait()
        total = lax.dot_general(
            own_rows, own_refs[k][:, :UNITS], NT, preferred_element_type=f32
        )
        total += lax.dot_general(
            other_rows, other_refs[k][...], NT, preferred_element_type=f32
        )
        right = own_refs[k][:, KEPT:] if k == 2 else own_refs[k][:, UNITS:KEPT]
        right = jnp.concatenate([right, right], axis=1)
        total += lax.dot_general(shares, right, NT, preferred_element_type=f32)
        for zh in range(NZH):
            top = total[zh * BLOCK : zh * BLOCK + BLOCK // 2]
            bottom = total[zh * BLOCK + BLOCK // 2 : (zh + 1) * BLOCK]
            out_ref[zh * NX + x] = jnp.concatenate([top, bottom], axis=1).astype(bf16)


def project(place, hidden, own, other):
    return pl.pallas_call(
        project_kernel,
        out_shape=jax.ShapeDtypeStruct((NZH * NX, BLOCK // 2, 2 * WIDTH), bf16),
        in_specs=[SMEM, VMEM] + [ANY] * (2 * NX),
        scratch_shapes=[
            pltpu.VMEM((WIDTH, KEPT + CHUNK if k == 2 else KEPT), bf16) for k in range(NX)
        ]
        + [pltpu.VMEM((WIDTH, UNITS), bf16)] * NX
        + [pltpu.SemaphoreType.DMA((2 * NX,))],
        compiler_params=WIDE,
    )(place, hidden, *own, *other)


def loss_kernel(place_ref, got_ref, target_ref, raw_ref, out_ref):
    total = got_ref[0].astype(f32)
    for source in range(1, NZH * NX):
        total += got_ref[source].astype(f32)
    raw = jnp.concatenate([total[:, :WIDTH], total[:, WIDTH:]], axis=0)
    raw_ref[...] = raw
    error = raw - target_ref[...].astype(f32)
    squares = jnp.sum(error * error, axis=1, keepdims=True)
    member = (
        lax.broadcasted_iota(jnp.int32, (BLOCK, CHUNK), 0) // TOKENS
        + place_ref[3] * BLOCK_MEMBERS
        - lax.broadcasted_iota(jnp.int32, (BLOCK, CHUNK), 1)
    )
    line = lax.broadcasted_iota(jnp.int32, (8, CHUNK), 0)
    placed = jnp.zeros((8, CHUNK), f32)
    for k in range(CHUNKS):
        here = jnp.sum(jnp.where(member == k * CHUNK, squares, 0.0), axis=0, keepdims=True)
        placed = jnp.where(line == k, here, placed)
    for k in range(NYH * NZL * NYL):
        out_ref[k] = placed


def piece_losses(place, got, target):
    return pl.pallas_call(
        loss_kernel,
        out_shape=[
            jax.ShapeDtypeStruct((BLOCK, WIDTH), f32),
            jax.ShapeDtypeStruct((NYH * NZL * NYL, 8, CHUNK), f32),
        ],
        in_specs=[SMEM] + [VMEM] * 2,
        compiler_params=PARAMS,
    )(place, got, target)


def update_kernel(place_ref, far_ref, *refs):
    left_hbm, blocks = refs[:3], refs[3:7]
    out_hbm, factor_ref, left_refs = refs[7:10], refs[10], refs[11:14]
    out_refs, arrived, left_sem = refs[14:17], refs[17], refs[18]
    copies = fetch(left_hbm, left_refs, arrived)
    leaving = []
    x_here = place_ref[0]
    group = NYH * GROUP
    for kind in range(3):
        for k, block in enumerate(blocks):
            start = pl.multiple_of(lax.rem(x_here - k + NX, NX) * group, group)
            factor_ref[kind, pl.ds(start, group), :] = block[kind]
    losses = far_ref[0]
    for source in range(1, NX * NC * NZH):
        losses += far_ref[source]
    losses = losses * f32(1.0 / (TOKENS * D))
    valid = lax.broadcasted_iota(jnp.int32, (8, CHUNK), 0) < CHUNKS
    mean = jnp.sum(losses, keepdims=True) * f32(1.0 / MEMBERS)
    offset = jnp.where(valid, losses - mean, 0.0)
    variance = jnp.sum(offset * offset, keepdims=True) * f32(1.0 / MEMBERS)
    weights = -offset / jnp.sqrt(variance + epsilon) * f32(1.0 / math.sqrt(MEMBERS))
    weights = jnp.concatenate([weights[k : k + 1] for k in range(CHUNKS)], axis=1)
    for kind in range(3):
        copies[kind].wait()
        scaled = left_refs[kind][...].astype(f32) * weights
        high = scaled.astype(bf16)
        low = (scaled - high.astype(f32)).astype(bf16)
        for part in range(2):
            lines = slice(part * (WIDTH // 2), (part + 1) * (WIDTH // 2))
            out_refs[kind][lines] = jnp.dot(
                high[lines], factor_ref[kind], preferred_element_type=f32
            ) + jnp.dot(low[lines], factor_ref[kind], preferred_element_type=f32)
            copy = pltpu.make_async_copy(
                out_refs[kind].at[lines], out_hbm[kind].at[lines], left_sem.at[2 * kind + part]
            )
            copy.start()
            leaving.append(copy)
    for copy in leaving:
        copy.wait()


def updates(place, far, lefts, blocks):
    out = jax.ShapeDtypeStruct((WIDTH, UNITS), f32)
    return pl.pallas_call(
        update_kernel,
        out_shape=[out] * 3,
        in_specs=[SMEM, VMEM] + [ANY] * 3 + [VMEM] * NX,
        out_specs=[ANY] * 3,
        scratch_shapes=[pltpu.VMEM((3, MEMBERS, UNITS), bf16)]
        + [pltpu.VMEM((WIDTH, MEMBERS), bf16)] * 3
        + [pltpu.VMEM((WIDTH, UNITS), f32)] * 3
        + [pltpu.SemaphoreType.DMA((3,)), pltpu.SemaphoreType.DMA((6,))],
        compiler_params=WIDE,
    )(place, far, *lefts, *blocks)


def after(earlier, *arrays):
    return lax.optimization_barrier((earlier, *arrays))[1:]


def shifted(value, axis, size, k):
    return lax.ppermute(value, axis, [(i, (i + k) % size) for i in range(size)])


def per_device(
    states,
    token_ids,
    gate_matrix,
    up_matrix,
    down_matrix,
    gate_left,
    gate_right,
    up_left,
    up_right,
    down_left,
    down_right,
    target,
):
    x_index, yh_index, c_index = (lax.axis_index(axis) for axis in ("x", "yh", "c"))
    block = (lax.axis_index("zh") * NX + x_index) * NC + c_index
    place = jnp.stack([x_index, yh_index, c_index, block]).astype(jnp.int32)
    forth = to_owner()
    back = [(b, a) for a, b in forth]

    own_factors = jnp.concatenate([gate_right, up_right, down_left], axis=0)
    along = [shifted(own_factors, "yh", NYH, k) for k in (1, 2, 3)]
    columns = down_columns(place, down_matrix.T, down_right.T)

    got = front(
        token_ids.T,
        states.T,
        gate_left.T,
        up_left.T,
        gate_matrix,
        up_matrix,
        gate_right,
        up_right,
        down_left,
    )
    sent = middle(lax.all_to_all(got, "x", 0, 0))
    piece_target = lax.ppermute(target, EVERY, back)
    partner = shifted(columns[0], "c", NC, 1)
    sent, along[0], along[2], columns, piece_target, partner = lax.optimization_barrier(
        (sent, along[0], along[2], columns, piece_target, partner)
    )
    got = lax.all_to_all(sent, "yh", 0, 0)

    before = shifted(columns[1], "x", NX, 1)
    later = shifted(columns[2], "x", NX, 3)
    ids = token_ids.reshape(NX, NYH, GROUP * TOKENS).transpose(1, 0, 2).reshape(1, ROWS)
    outgoing = activate(ids, got)
    outgoing, before, later, along[1] = lax.optimization_barrier(
        (outgoing, before, later, along[1])
    )

    hidden = lax.all_to_all(
        outgoing.reshape(NC * NX * NYH * OWN, PADDED), ("c", "x", "yh"), 0, 0, tiled=True
    )
    half = WIDTH // 2
    opposite = jnp.concatenate(
        [shifted(before[:half], "x", NX, 1), shifted(later[half:], "x", NX, 3)], axis=0
    )
    columns = [columns[0], before, opposite, later]
    others = [partner] + [shifted(column, "c", NC, 1) for column in columns[1:]]

    pieces = project(place, hidden, columns, others)
    (along,) = after(hidden, along)
    got = lax.all_to_all(pieces, ("zh", "zl", "yl"), 0, 0)
    around = jnp.stack([own_factors] + along).reshape(NYH, 3, GROUP, UNITS)
    around = jnp.concatenate(
        [
            lax.dynamic_index_in_dim(around, lax.rem(yh_index - k + NYH, NYH), 0, keepdims=False)
            for k in range(NYH)
        ],
        axis=1,
    )
    arounds = [shifted(around, "x", NX, k) for k in (1, 2, 3)]
    raw, sent = piece_losses(place, got, piece_target)
    raw_out = lax.ppermute(raw, EVERY, forth)

    near = lax.all_to_all(sent, ("yh", "zl", "yl"), 0, 0)
    near = jnp.broadcast_to(jnp.sum(near, axis=0), (NX * NC * NZH, 8, CHUNK))
    near, arounds = lax.optimization_barrier((near, arounds))
    far = lax.all_to_all(near, ("x", "c", "zh"), 0, 0)
    gate_update, up_update, down_update = updates(
        place,
        far,
        (gate_left.T, up_left.T, down_right.T),
        (around, *arounds),
    )
    return (raw_out, gate_update, up_update, down_update.T)


def solution(mesh):
    cut = Mesh(mesh.devices.reshape(NX, NYH, NZH, NZL, NYL, NC), EVERY)
    return jax.shard_map(
        per_device,
        mesh=cut,
        in_specs=(
            P(None, POP),
            P(),
            P(POP, TP),
            P(POP, TP),
            P(TP, POP),
            P(None, POP),
            P(POP, TP),
            P(None, POP),
            P(POP, TP),
            P(POP, TP),
            P(None, POP),
            P(TP, POP),
        ),
        out_specs=(P(TP, POP), P(POP, TP), P(POP, TP), P(TP, POP)),
        check_vma=False,
    )
```

time: 226 us -> 178 us (0.79)
  blocking collectives: 80 us -> 11.6 us
  starting transfers between devices: 47 us -> 102 us
  Pallas kernels: 0.94 us -> 21.5 us
  waiting for transfers between devices: 52.2 us -> 34.1 us
  between operations: 17.5 us -> 1.22 us
  matrix products: 12.2 us -> 0 us
  other arithmetic: 4.78 us -> 0.2 us
  local copies, waits for them, and re-layouts: 9.69 us -> 6.4 us
    ppermute x1 -> x15, starting transfers between devices: 4.09 us -> 56.6 us  [the longest x14 55.2 us: shifted(): return lax.ppermute(value, axis, [(i, (i + k) % size) for i in range(size)])]
    all_gather x1 -> x0, blocking collectives: 49.1 us -> none  [per_device(): lax.all_gather(down_left.reshape(GROUP * 4, UNITS // 4), POP, axis=0, til...]
    pallas_call x1 -> x7, Pallas kernels: 0.94 us -> 21.5 us  [the longest x1 6.31 us: project(): pl.pallas_call(project_kernel, out_shape=jax.ShapeDtypeStruct((NZH * NX,...]
    all_to_all x2 -> x1, blocking collectives: 30.8 us -> 11.6 us  [per_device(): near = lax.all_to_all(sent, ('yh', 'zl', 'yl'), 0, 0)]
    dot_general x15 -> x0, matrix products: 12.2 us -> none  [the longest x2 3.4 us: per_device(): lax.dot_general(states, left, (((1,), (1,)), ((), ())), preferred_element...]
    ppermute x1 -> x15, waiting for transfers between devices: 22 us -> 11.2 us  [the longest x14 11.2 us: shifted(): return lax.ppermute(value, axis, [(i, (i + k) % size) for i in range(size)])]
    all_gather x2 -> x0, waiting for transfers between devices: 6.43 us -> none  [the longest x1 6.41 us: per_device(): lax.all_gather(jnp.concatenate([gate_right, up_right], axis=0), POP, axis...]
    all_to_all x5, starting transfers between devices: 40.9 us -> 44.5 us  [the longest x1 15.5 us: per_device(): got = lax.all_to_all(pieces, ('zh', 'zl', 'yl'), 0, 0)]
  transfers between devices with their start and end apart: 9 -> 21, of which waited for: 5 -> 7; matrix products, arithmetic and copies ran while one was open for 3% -> 1% of each run, Pallas kernels for 0% -> 3%
where the time goes in v2:
time: 178 us; the launch traced here: 177 us
  starting transfers between devices  102 us (57%)
  waiting for transfers between devices  34.1 us (19%)
  Pallas kernels  21.5 us (12%)
  blocking collectives  11.6 us (7%)
  local copies, waits for them, and re-layouts  6.4 us (4%)
    ppermute x14, starting transfers between devices, shifted(): return lax.ppermute(value, axis, [(i, (i + k) % size) for i in range(size)])  55.2 us
    all_to_all x1, starting transfers between devices, per_device(): got = lax.all_to_all(pieces, ('zh', 'zl', 'yl'), 0, 0)  15.5 us
    all_to_all x1, waiting for transfers between devices, per_device(): got = lax.all_to_all(pieces, ('zh', 'zl', 'yl'), 0, 0)  12.5 us
    all_to_all x1, blocking collectives, per_device(): near = lax.all_to_all(sent, ('yh', 'zl', 'yl'), 0, 0)  11.6 us
    ppermute x14, waiting for transfers between devices, shifted(): return lax.ppermute(value, axis, [(i, (i + k) % size) for i in range(size)])  11.2 us
    all_to_all x1, starting transfers between devices, per_device(): lax.all_to_all(outgoing.reshape(NC * NX * NYH * OWN, PADDED), ('c', 'x',...  11 us
    all_to_all x1, waiting for transfers between devices, per_device(): far = lax.all_to_all(near, ('x', 'c', 'zh'), 0, 0)  10.3 us
    all_to_all x1, starting transfers between devices, per_device(): far = lax.all_to_all(near, ('x', 'c', 'zh'), 0, 0)  9.15 us
  transfers between devices with their start and end apart: 21, of which 7 were waited for; matrix products, arithmetic and copies ran while one was open for 1% of the time, Pallas kernels for 3%

profile of v2, /device:TPU:1, one launch (start us, length us, event | category | flops | bytes accessed | tf_op | source)
XLA Modules:
  0.0 176.8 jit_solution(18232364587182134164)
XLA Ops:
  0.6 4.3 %shard_map.147 = f32[4,672,128]{2,1,0:T(8,128)} custom-call(s32[4,640]{1,0:T(4,128)} %bitcast.40, bf16[320,256]{1,0:T(8,128)(2,1)} %bitcast.35, bf16[320,640]{1,0:T(8,128)(2,1)} %bitcast.30, bf16[320,640]{1,0:T(8,128)(2,1)} %bitcast.32, bf16[320,512]{1,0:T(8,128)(2,1)} %refs_4_.1, bf16[320,512]{1,0:T(8,128)(2,1)} %refs_5_.1, bf16[40,512]{1,0:T(8,128)(2,1)} %refs_6_.1, ...), custom_call_target="tpu_custom_call" | custom-call | tf_op jit(solution)/shard_map/pallas_call | solution.py:118
  5.0 5.0 %all-to-all-start = ((f32[4,672,128]{2,1,0:T(8,128)}), f32[4,672,128]{2,1,0:T(8,128)S(1)}, u32[]{:S(2)}, u32[]{:S(2)}) async-start(f32[4,672,128]{2,1,0:T(8,128)} %shard_map.147), calls=%async_computation | async-start | bytes 2752512 | tf_op jit(solution)/shard_map/all_to_all | solution.py:473
  10.0 0.1 pad_add_fusion.place_ref
  10.0 1.2 shard_map.149
  11.2 7.5 %collective-permute-start.3 = (bf16[320,640]{1,0:T(8,128)(2,1)S(1)}, bf16[320,640]{1,0:T(8,128)(2,1)}, u32[]{:S(2)}, u32[]{:S(2)}) collective-permute-start(bf16[320,640]{1,0:T(8,128)(2,1)S(1)} %get-tuple-element.38.refs_0_), channel_id=1, source_target_pairs={{0,1},{1,0},{2,3},{3,2},{4,5},{5,4},{6,7},{7,6},{8,9},{9,8},{10,11... | collective-permute-start | bytes 1228808 | tf_op jit(solution)/shard_map/ppermute | solution.py:435
  18.8 0.8 constant_dynamic-update-slice_fusion.1
  19.6 0.8 constant_dynamic-update-slice_fusion
  20.4 2.0 %collective-permute-start = (bf16[120,512]{1,0:T(8,128)(2,1)S(1)}, bf16[120,512]{1,0:T(8,128)(2,1)S(1)}, u32[]{:S(2)}, u32[]{:S(2)}) collective-permute-start(bf16[120,512]{1,0:T(8,128)(2,1)S(1)} %constant_dynamic-update-slice_fusion), channel_id=1, source_target_pairs={{0,32},{32,64},{64,96},{96,0},{1,33},{33,65},{65,97},{97,1},{2,34}... | collective-permute-start | bytes 368648 | tf_op jit(solution)/shard_map/ppermute | solution.py:435
  22.4 5.5 %collective-permute-start.1 = (bf16[120,512]{1,0:T(8,128)(2,1)S(1)}, bf16[120,512]{1,0:T(8,128)(2,1)S(1)}, u32[]{:S(2)}, u32[]{:S(2)}) collective-permute-start(bf16[120,512]{1,0:T(8,128)(2,1)S(1)} %constant_dynamic-update-slice_fusion), channel_id=1, source_target_pairs={{0,96},{32,0},{64,32},{96,64},{1,97},{33,1},{65,33},{97,65},{2,98}... | collective-permute-start | bytes 368648 | tf_op jit(solution)/shard_map/ppermute | solution.py:435
  27.9 1.5 collective-permute-start.2
  29.4 1.0 shard_map.148
  30.4 1.1 collective-permute-done
  31.5 0.6 collective-permute-done.1
  32.1 0.6 copy-done.21
  32.7 3.8 %all-to-all-start.1 = ((f32[4,80,512]{2,1,0:T(8,128)}), f32[4,80,512]{2,1,0:T(8,128)S(1)}, u32[]{:S(2)}, u32[]{:S(2)}) async-start(f32[4,80,512]{2,1,0:T(8,128)} %shard_map.148), calls=%async_computation.1 | async-start | bytes 1310720 | tf_op jit(solution)/shard_map/all_to_all | solution.py:479
  36.6 5.4 %collective-permute-start.4 = (bf16[320,768]{1,0:T(8,128)(2,1)S(1)}, bf16[320,768]{1,0:T(8,128)(2,1)S(1)}, u32[]{:S(2)}, u32[]{:S(2)}) collective-permute-start(bf16[320,768]{1,0:T(8,128)(2,1)S(1)} %get-tuple-element.35), channel_id=1, source_target_pairs={{0,128},{128,256},{256,384},{384,0},{1,129},{129,257},{257,385},{3... | collective-permute-start | bytes 1474568 | tf_op jit(solution)/shard_map/ppermute | solution.py:435
  42.0 5.1 %collective-permute-start.5 = (bf16[320,768]{1,0:T(8,128)(2,1)S(1)}, bf16[320,768]{1,0:T(8,128)(2,1)S(1)}, u32[]{:S(2)}, u32[]{:S(2)}) collective-permute-start(bf16[320,768]{1,0:T(8,128)(2,1)S(1)} %get-tuple-element.36), channel_id=1, source_target_pairs={{0,384},{128,0},{256,128},{384,256},{1,385},{129,1},{257,129},{385... | collective-permute-start | bytes 1474568 | tf_op jit(solution)/shard_map/ppermute | solution.py:435
  47.1 7.2 %collective-permute-start.6 = (bf16[120,512]{1,0:T(8,128)(2,1)}, bf16[120,512]{1,0:T(8,128)(2,1)S(1)}, u32[]{:S(2)}, u32[]{:S(2)}) collective-permute-start(bf16[120,512]{1,0:T(8,128)(2,1)} %copy-done.16), channel_id=1, source_target_pairs={{0,64},{32,96},{64,0},{96,32},{1,65},{33,97},{65,1},{97,33},{2,66}... | collective-permute-start | bytes 368648 | tf_op jit(solution)/shard_map/ppermute | solution.py:435
  54.3 0.2 copy.16
  54.5 0.2 reshape.27
  54.7 0.1 reshape.28.ids_ref
  54.8 2.5 %shard_map.150 = bf16[2,4,4,32,384]{4,3,2,1,0:T(8,128)(2,1)} custom-call(s32[1,2560]{1,0:T(1,128)S(1)} %reshape.28.ids_ref, f32[4,80,512]{2,1,0:T(8,128)S(1)} %all-to-all-done.1.got_ref), custom_call_target="tpu_custom_call" | custom-call | tf_op jit(solution)/shard_map/pallas_call | solution.py:265
  57.3 3.2 %collective-permute-done.6 = bf16[120,512]{1,0:T(8,128)(2,1)S(1)} collective-permute-done((bf16[120,512]{1,0:T(8,128)(2,1)}, bf16[120,512]{1,0:T(8,128)(2,1)S(1)}, u32[]{:S(2)}, u32[]{:S(2)}) %collective-permute-start.6) | collective-permute-done | bytes 122912 | tf_op jit(solution)/shard_map/ppermute | solution.py:435
  60.6 0.6 copy-done.23
  61.2 11.0 %all-to-all-start.2 = ((bf16[32,32,384]{2,1,0:T(8,128)(2,1)}), bf16[32,32,384]{2,1,0:T(8,128)(2,1)S(1)}, u32[]{:S(2)}, u32[]{:S(2)}) async-start(bf16[32,32,384]{2,1,0:T(8,128)(2,1)} %bitcast.11), calls=%async_computation.2 | async-start | bytes 1572864 | tf_op jit(solution)/shard_map/all_to_all | solution.py:489
  72.2 3.3 %collective-permute-start.7 = (bf16[160,768]{1,0:T(8,128)(2,1)S(1)}, bf16[160,768]{1,0:T(8,128)(2,1)S(1)}, u32[]{:S(2)}, u32[]{:S(2)}) collective-permute-start(bf16[160,768]{1,0:T(8,128)(2,1)S(1)} %slice.6), channel_id=1, source_target_pairs={{0,128},{128,256},{256,384},{384,0},{1,129},{129,257},{257,385},{3... | collective-permute-start | bytes 737288 | tf_op jit(solution)/shard_map/ppermute | solution.py:435
  75.6 3.2 %collective-permute-start.8 = (bf16[160,768]{1,0:T(8,128)(2,1)S(1)}, bf16[160,768]{1,0:T(8,128)(2,1)S(1)}, u32[]{:S(2)}, u32[]{:S(2)}) collective-permute-start(bf16[160,768]{1,0:T(8,128)(2,1)S(1)} %slice.7), channel_id=1, source_target_pairs={{0,384},{128,0},{256,128},{384,256},{1,385},{129,1},{257,129},{385... | collective-permute-start | bytes 737288 | tf_op jit(solution)/shard_map/ppermute | solution.py:435
  78.8 2.7 %collective-permute-start.9 = (bf16[320,768]{1,0:T(8,128)(2,1)S(1)}, bf16[320,768]{1,0:T(8,128)(2,1)S(1)}, u32[]{:S(2)}, u32[]{:S(2)}) collective-permute-start(bf16[320,768]{1,0:T(8,128)(2,1)S(1)} %collective-permute-done.4.refs_1_), channel_id=1, source_target_pairs={{0,1},{1,0},{2,3},{3,2},{4,5},{5,4},{6,7},{7,6},{8,9},{9,8},{10,11... | collective-permute-start | bytes 1474568 | tf_op jit(solution)/shard_map/ppermute | solution.py:435
  81.5 1.9 %collective-permute-start.11 = (bf16[320,768]{1,0:T(8,128)(2,1)S(1)}, bf16[320,768]{1,0:T(8,128)(2,1)S(1)}, u32[]{:S(2)}, u32[]{:S(2)}) collective-permute-start(bf16[320,768]{1,0:T(8,128)(2,1)S(1)} %collective-permute-done.5.refs_3_), channel_id=1, source_target_pairs={{0,1},{1,0},{2,3},{3,2},{4,5},{5,4},{6,7},{7,6},{8,9},{9,8},{10,11... | collective-permute-start | bytes 1474568 | tf_op jit(solution)/shard_map/ppermute | solution.py:435
  83.4 4.7 %collective-permute-done.7 = bf16[160,768]{1,0:T(8,128)(2,1)S(1)} collective-permute-done((bf16[160,768]{1,0:T(8,128)(2,1)S(1)}, bf16[160,768]{1,0:T(8,128)(2,1)S(1)}, u32[]{:S(2)}, u32[]{:S(2)}) %collective-permute-start.7) | collective-permute-done | bytes 245792 | tf_op jit(solution)/shard_map/ppermute | solution.py:435
  88.2 2.6 %collective-permute-start.10 = (bf16[320,768]{1,0:T(8,128)(2,1)S(1)}, bf16[320,768]{1,0:T(8,128)(2,1)}, u32[]{:S(2)}, u32[]{:S(2)}) collective-permute-start(bf16[320,768]{1,0:T(8,128)(2,1)S(1)} %constant_dynamic-update-slice_fusion.3.refs_2_), channel_id=1, source_target_pairs={{0,1},{1,0},{2,3},{3,2},{4,5},{5,4},{6,7},{7,6},{8,9},{9,8},{10,11... | collective-permute-start | bytes 1474568 | tf_op jit(solution)/shard_map/ppermute | solution.py:435
  90.9 1.6 collective-permute-done.10.refs_6_
  92.5 0.9 copy-done.5
  93.4 6.3 %shard_map.151 = bf16[16,40,640]{2,1,0:T(8,128)(2,1)} custom-call(s32[4]{0:T(128)} %copy-done.3, bf16[1024,384]{1,0:T(8,128)(2,1)} %bitcast.29, bf16[320,640]{1,0:T(8,128)(2,1)} %copy-done.1, bf16[320,768]{1,0:T(8,128)(2,1)} %copy-done.7, bf16[320,768]{1,0:T(8,128)(2,1)} %copy-done.9, bf16[320,768]{1,0:T(8,128)(2,1)} %copy-done.8, ...), custom_call_target="tpu_custom_call" | custom-call | tf_op jit(solution)/shard_map/pallas_call | solution.py:327
  99.7 15.5 %all-to-all-start.3 = ((bf16[16,40,640]{2,1,0:T(8,128)(2,1)}), bf16[16,40,640]{2,1,0:T(8,128)(2,1)S(1)}, u32[]{:S(2)}, u32[]{:S(2)}) async-start(bf16[16,40,640]{2,1,0:T(8,128)(2,1)} %shard_map.151), calls=%async_computation.3 | async-start | bytes 1638400 | tf_op jit(solution)/shard_map/all_to_all | solution.py:501
  115.5 2.2 %collective-permute-start.13 = (bf16[3,160,512]{2,1,0:T(8,128)(2,1)S(1)}, bf16[3,160,512]{2,1,0:T(8,128)(2,1)S(1)}, u32[]{:S(2)}, u32[]{:S(2)}) collective-permute-start(bf16[3,160,512]{2,1,0:T(8,128)(2,1)S(1)} %pad_maximum_fusion.1.refs_3_), channel_id=1, source_target_pairs={{0,128},{128,256},{256,384},{384,0},{1,129},{129,257},{257,385},{3... | collective-permute-start | bytes 1474568 | tf_op jit(solution)/shard_map/ppermute | solution.py:435
  117.7 3.7 %collective-permute-start.14 = (bf16[3,160,512]{2,1,0:T(8,128)(2,1)S(1)}, bf16[3,160,512]{2,1,0:T(8,128)(2,1)S(1)}, u32[]{:S(2)}, u32[]{:S(2)}) collective-permute-start(bf16[3,160,512]{2,1,0:T(8,128)(2,1)S(1)} %pad_maximum_fusion.1.refs_3_), channel_id=1, source_target_pairs={{0,256},{128,384},{256,0},{384,128},{1,257},{129,385},{257,1},{385... | collective-permute-start | bytes 1474568 | tf_op jit(solution)/shard_map/ppermute | solution.py:435
  121.4 2.8 %collective-permute-start.15 = (bf16[3,160,512]{2,1,0:T(8,128)(2,1)S(1)}, bf16[3,160,512]{2,1,0:T(8,128)(2,1)S(1)}, u32[]{:S(2)}, u32[]{:S(2)}) collective-permute-start(bf16[3,160,512]{2,1,0:T(8,128)(2,1)S(1)} %pad_maximum_fusion.1.refs_3_), channel_id=1, source_target_pairs={{0,384},{128,0},{256,128},{384,256},{1,385},{129,1},{257,129},{385... | collective-permute-start | bytes 1474568 | tf_op jit(solution)/shard_map/ppermute | solution.py:435
  124.2 12.5 %all-to-all-done.3.got_ref = bf16[16,40,640]{2,1,0:T(8,128)(2,1)S(1)} async-done(((bf16[16,40,640]{2,1,0:T(8,128)(2,1)}), bf16[16,40,640]{2,1,0:T(8,128)(2,1)S(1)}, u32[]{:S(2)}, u32[]{:S(2)}) %all-to-all-start.3) | async-done | bytes 819232 | tf_op jit(solution)/shard_map/all_to_all | solution.py:501
  136.7 0.8 shard_map.152
  137.5 11.6 %all_to_all.36 = f32[16,8,128]{2,1,0:T(8,128)S(1)} all-to-all(f32[16,8,128]{2,1,0:T(8,128)S(1)} %get-tuple-element.44), channel_id=1, replica_groups=mesh['x'=4,'yh'=4,'zh'=4,'zl'=2,'yl'=2,'c'=2] {'yh','zl','yl'}, dimensions={0} | all-to-all | bytes 131072 | tf_op jit(solution)/shard_map/all_to_all | solution.py:514
  149.2 0.7 broadcast_in_dim.3
  149.9 9.2 %all-to-all-start.5 = ((f32[32,8,128]{2,1,0:T(8,128)}), f32[32,8,128]{2,1,0:T(8,128)S(1)}, u32[]{:S(2)}, u32[]{:S(2)}) async-start(f32[32,8,128]{2,1,0:T(8,128)} %broadcast_in_dim.3), calls=%async_computation.5 | async-start | bytes 262144 | tf_op jit(solution)/shard_map/all_to_all | solution.py:517
  159.1 0.7 collective-permute-start.12
  159.7 10.3 %all-to-all-done.5.far_ref = f32[32,8,128]{2,1,0:T(8,128)S(1)} async-done(((f32[32,8,128]{2,1,0:T(8,128)}), f32[32,8,128]{2,1,0:T(8,128)S(1)}, u32[]{:S(2)}, u32[]{:S(2)}) %all-to-all-start.5) | async-done | bytes 131104 | tf_op jit(solution)/shard_map/all_to_all | solution.py:517
  170.1 0.6 copy-done.10
  170.8 5.4 %shard_map.153 = (f32[320,512]{1,0:T(8,128)}, f32[320,512]{1,0:T(8,128)}, f32[320,512]{1,0:T(8,128)}) custom-call(s32[4]{0:T(128)} %copy-done.3, f32[32,8,128]{2,1,0:T(8,128)} %copy-done.10, bf16[320,640]{1,0:T(8,128)(2,1)} %bitcast.31, bf16[320,640]{1,0:T(8,128)(2,1)} %bitcast.33, bf16[320,640]{1,0:T(8,128)(2,1)} %bitcast.26, ...), custom_call_target="tpu_custom_call" | custom-call | tf_op jit(solution)/shard_map/pallas_call | solution.py:417
  176.2 0.7 copy.22
  (72 shorter events, 0.4 us)
Async XLA Ops:
  4.9 5.1 %copy-start = (bf16[640,320]{0,1:T(8,128)(2,1)S(1)}, bf16[640,320]{0,1:T(8,128)(2,1)}, u32[]{:S(2)}) copy-start(bf16[640,320]{0,1:T(8,128)(2,1)} %param.22) | copy-start | bytes 1228804
  4.9 5.1 %copy-start.2 = (bf16[512,320]{0,1:T(8,128)(2,1)S(1)}, bf16[512,320]{0,1:T(8,128)(2,1)}, u32[]{:S(2)}) copy-start(bf16[512,320]{0,1:T(8,128)(2,1)} %param.16) | copy-start | bytes 983044
  5.0 13.8 %copy-start.18 = (bf16[40,512]{1,0:T(8,128)(2,1)S(1)}, bf16[40,512]{1,0:T(8,128)(2,1)}, u32[]{:S(2)}) copy-start(bf16[40,512]{1,0:T(8,128)(2,1)} %refs_6_.1) | copy-start | bytes 122884
  5.0 24.4 %all-to-all-start = ((f32[4,672,128]{2,1,0:T(8,128)}), f32[4,672,128]{2,1,0:T(8,128)S(1)}, u32[]{:S(2)}, u32[]{:S(2)}) async-start(f32[4,672,128]{2,1,0:T(8,128)} %shard_map.147), calls=%async_computation | async-start | bytes 2752512 | tf_op jit(solution)/shard_map/all_to_all | solution.py:473
  10.0 20.4 %copy-start.3 = (s32[4]{0:T(128)}, s32[4]{0:T(128)S(1)}, u32[]{:S(2)}) copy-start(s32[4]{0:T(128)S(1)} %pad_add_fusion.place_ref) | copy-start | bytes 52
  11.2 20.8 %copy-start.1 = (bf16[320,640]{1,0:T(8,128)(2,1)}, bf16[320,640]{1,0:T(8,128)(2,1)S(1)}, u32[]{:S(2)}) copy-start(bf16[320,640]{1,0:T(8,128)(2,1)S(1)} %get-tuple-element.38.refs_0_) | copy-start | bytes 1228804
  11.2 20.8 %collective-permute-start.3 = (bf16[320,640]{1,0:T(8,128)(2,1)S(1)}, bf16[320,640]{1,0:T(8,128)(2,1)}, u32[]{:S(2)}, u32[]{:S(2)}) collective-permute-start(bf16[320,640]{1,0:T(8,128)(2,1)S(1)} %get-tuple-element.38.refs_0_), channel_id=1, source_target_pairs={{0,1},{1,0},{2,3},{3,2},{4,5},{5,4},{6,7},{7,6},{8,9},{9,8},{10,11... | collective-permute-start | bytes 1228808 | tf_op jit(solution)/shard_map/ppermute | solution.py:435
  20.3 16.2 %copy-start.16 = (bf16[120,512]{1,0:T(8,128)(2,1)}, bf16[120,512]{1,0:T(8,128)(2,1)S(1)}, u32[]{:S(2)}) copy-start(bf16[120,512]{1,0:T(8,128)(2,1)S(1)} %constant_dynamic-update-slice_fusion) | copy-start | bytes 368644
  20.4 34.0 %copy-start.25 = (s32[640,4]{0,1:T(4,128)S(1)}, s32[640,4]{0,1:T(4,128)}, u32[]{:S(2)}) copy-start(s32[640,4]{0,1:T(4,128)} %param.13) | copy-start | bytes 30724
  20.4 11.2 %collective-permute-start = (bf16[120,512]{1,0:T(8,128)(2,1)S(1)}, bf16[120,512]{1,0:T(8,128)(2,1)S(1)}, u32[]{:S(2)}, u32[]{:S(2)}) collective-permute-start(bf16[120,512]{1,0:T(8,128)(2,1)S(1)} %constant_dynamic-update-slice_fusion), channel_id=1, source_target_pairs={{0,32},{32,64},{64,96},{96,0},{1,33},{33,65},{65,97},{97,1},{2,34}... | collective-permute-start | bytes 368648 | tf_op jit(solution)/shard_map/ppermute | solution.py:435
  22.4 9.7 %collective-permute-start.1 = (bf16[120,512]{1,0:T(8,128)(2,1)S(1)}, bf16[120,512]{1,0:T(8,128)(2,1)S(1)}, u32[]{:S(2)}, u32[]{:S(2)}) collective-permute-start(bf16[120,512]{1,0:T(8,128)(2,1)S(1)} %constant_dynamic-update-slice_fusion), channel_id=1, source_target_pairs={{0,96},{32,0},{64,32},{96,64},{1,97},{33,1},{65,33},{97,65},{2,98}... | collective-permute-start | bytes 368648 | tf_op jit(solution)/shard_map/ppermute | solution.py:435
  27.9 2.5 %collective-permute-start.2 = (bf16[80,320]{1,0:T(8,128)(2,1)}, bf16[80,320]{1,0:T(8,128)(2,1)S(1)}, u32[]{:S(2)}, u32[]{:S(2)}) collective-permute-start(bf16[80,320]{1,0:T(8,128)(2,1)} %param.23), channel_id=1, source_target_pairs={{0,0},{1,1},{128,2},{129,3},{256,4},{257,5},{384,6},{385,7},{8,8},... | collective-permute-start | bytes 153608 | tf_op jit(solution)/shard_map/ppermute | solution.py:474
  31.5 5.1 %copy-start.19 = (bf16[120,512]{1,0:T(8,128)(2,1)}, bf16[120,512]{1,0:T(8,128)(2,1)S(1)}, u32[]{:S(2)}) copy-start(bf16[120,512]{1,0:T(8,128)(2,1)S(1)} %collective-permute-done) | copy-start | bytes 368644
  32.1 0.6 copy-start.21
  32.7 22.1 %all-to-all-start.1 = ((f32[4,80,512]{2,1,0:T(8,128)}), f32[4,80,512]{2,1,0:T(8,128)S(1)}, u32[]{:S(2)}, u32[]{:S(2)}) async-start(f32[4,80,512]{2,1,0:T(8,128)} %shard_map.148), calls=%async_computation.1 | async-start | bytes 1310720 | tf_op jit(solution)/shard_map/all_to_all | solution.py:479
  36.6 24.0 %collective-permute-start.4 = (bf16[320,768]{1,0:T(8,128)(2,1)S(1)}, bf16[320,768]{1,0:T(8,128)(2,1)S(1)}, u32[]{:S(2)}, u32[]{:S(2)}) collective-permute-start(bf16[320,768]{1,0:T(8,128)(2,1)S(1)} %get-tuple-element.35), channel_id=1, source_target_pairs={{0,128},{128,256},{256,384},{384,0},{1,129},{129,257},{257,385},{3... | collective-permute-start | bytes 1474568 | tf_op jit(solution)/shard_map/ppermute | solution.py:435
  42.0 18.6 %collective-permute-start.5 = (bf16[320,768]{1,0:T(8,128)(2,1)S(1)}, bf16[320,768]{1,0:T(8,128)(2,1)S(1)}, u32[]{:S(2)}, u32[]{:S(2)}) collective-permute-start(bf16[320,768]{1,0:T(8,128)(2,1)S(1)} %get-tuple-element.36), channel_id=1, source_target_pairs={{0,384},{128,0},{256,128},{384,256},{1,385},{129,1},{257,129},{385... | collective-permute-start | bytes 1474568 | tf_op jit(solution)/shard_map/ppermute | solution.py:435
  47.1 13.4 %collective-permute-start.6 = (bf16[120,512]{1,0:T(8,128)(2,1)}, bf16[120,512]{1,0:T(8,128)(2,1)S(1)}, u32[]{:S(2)}, u32[]{:S(2)}) collective-permute-start(bf16[120,512]{1,0:T(8,128)(2,1)} %copy-done.16), channel_id=1, source_target_pairs={{0,64},{32,96},{64,0},{96,32},{1,65},{33,97},{65,1},{97,33},{2,66}... | collective-permute-start | bytes 368648 | tf_op jit(solution)/shard_map/ppermute | solution.py:435
  60.5 0.7 copy-start.23
  60.6 27.6 %copy-start.7 = (bf16[320,768]{1,0:T(8,128)(2,1)}, bf16[320,768]{1,0:T(8,128)(2,1)S(1)}, u32[]{:S(2)}) copy-start(bf16[320,768]{1,0:T(8,128)(2,1)S(1)} %collective-permute-done.4.refs_1_) | copy-start | bytes 1474564
  60.6 27.6 %copy-start.8 = (bf16[320,768]{1,0:T(8,128)(2,1)}, bf16[320,768]{1,0:T(8,128)(2,1)S(1)}, u32[]{:S(2)}) copy-start(bf16[320,768]{1,0:T(8,128)(2,1)S(1)} %collective-permute-done.5.refs_3_) | copy-start | bytes 1474564
  61.2 31.3 %all-to-all-start.2 = ((bf16[32,32,384]{2,1,0:T(8,128)(2,1)}), bf16[32,32,384]{2,1,0:T(8,128)(2,1)S(1)}, u32[]{:S(2)}, u32[]{:S(2)}) async-start(bf16[32,32,384]{2,1,0:T(8,128)(2,1)} %bitcast.11), calls=%async_computation.2 | async-start | bytes 1572864 | tf_op jit(solution)/shard_map/all_to_all | solution.py:489
  72.2 15.9 %collective-permute-start.7 = (bf16[160,768]{1,0:T(8,128)(2,1)S(1)}, bf16[160,768]{1,0:T(8,128)(2,1)S(1)}, u32[]{:S(2)}, u32[]{:S(2)}) collective-permute-start(bf16[160,768]{1,0:T(8,128)(2,1)S(1)} %slice.6), channel_id=1, source_target_pairs={{0,128},{128,256},{256,384},{384,0},{1,129},{129,257},{257,385},{3... | collective-permute-start | bytes 737288 | tf_op jit(solution)/shard_map/ppermute | solution.py:435
  75.6 12.6 %collective-permute-start.8 = (bf16[160,768]{1,0:T(8,128)(2,1)S(1)}, bf16[160,768]{1,0:T(8,128)(2,1)S(1)}, u32[]{:S(2)}, u32[]{:S(2)}) collective-permute-start(bf16[160,768]{1,0:T(8,128)(2,1)S(1)} %slice.7), channel_id=1, source_target_pairs={{0,384},{128,0},{256,128},{384,256},{1,385},{129,1},{257,129},{385... | collective-permute-start | bytes 737288 | tf_op jit(solution)/shard_map/ppermute | solution.py:435
  78.8 12.1 %collective-permute-start.9 = (bf16[320,768]{1,0:T(8,128)(2,1)S(1)}, bf16[320,768]{1,0:T(8,128)(2,1)S(1)}, u32[]{:S(2)}, u32[]{:S(2)}) collective-permute-start(bf16[320,768]{1,0:T(8,128)(2,1)S(1)} %collective-permute-done.4.refs_1_), channel_id=1, source_target_pairs={{0,1},{1,0},{2,3},{3,2},{4,5},{5,4},{6,7},{7,6},{8,9},{9,8},{10,11... | collective-permute-start | bytes 1474568 | tf_op jit(solution)/shard_map/ppermute | solution.py:435
  81.5 9.4 %collective-permute-start.11 = (bf16[320,768]{1,0:T(8,128)(2,1)S(1)}, bf16[320,768]{1,0:T(8,128)(2,1)S(1)}, u32[]{:S(2)}, u32[]{:S(2)}) collective-permute-start(bf16[320,768]{1,0:T(8,128)(2,1)S(1)} %collective-permute-done.5.refs_3_), channel_id=1, source_target_pairs={{0,1},{1,0},{2,3},{3,2},{4,5},{5,4},{6,7},{7,6},{8,9},{9,8},{10,11... | collective-permute-start | bytes 1474568 | tf_op jit(solution)/shard_map/ppermute | solution.py:435
  88.2 4.3 %copy-start.9 = (bf16[320,768]{1,0:T(8,128)(2,1)}, bf16[320,768]{1,0:T(8,128)(2,1)S(1)}, u32[]{:S(2)}) copy-start(bf16[320,768]{1,0:T(8,128)(2,1)S(1)} %constant_dynamic-update-slice_fusion.3.refs_2_) | copy-start | bytes 1474564
  88.2 4.2 %collective-permute-start.10 = (bf16[320,768]{1,0:T(8,128)(2,1)S(1)}, bf16[320,768]{1,0:T(8,128)(2,1)}, u32[]{:S(2)}, u32[]{:S(2)}) collective-permute-start(bf16[320,768]{1,0:T(8,128)(2,1)S(1)} %constant_dynamic-update-slice_fusion.3.refs_2_), channel_id=1, source_target_pairs={{0,1},{1,0},{2,3},{3,2},{4,5},{5,4},{6,7},{7,6},{8,9},{9,8},{10,11... | collective-permute-start | bytes 1474568 | tf_op jit(solution)/shard_map/ppermute | solution.py:435
  90.9 1.6 copy-start.14
  90.9 1.6 copy-start.15
  92.5 0.9 copy-start.5
  99.7 15.6 %copy-start.17 = (bf16[120,512]{1,0:T(8,128)(2,1)S(1)}, bf16[120,512]{1,0:T(8,128)(2,1)}, u32[]{:S(2)}) copy-start(bf16[120,512]{1,0:T(8,128)(2,1)} %copy-done.16) | copy-start | bytes 368644
  99.7 15.6 %copy-start.20 = (bf16[120,512]{1,0:T(8,128)(2,1)S(1)}, bf16[120,512]{1,0:T(8,128)(2,1)}, u32[]{:S(2)}) copy-start(bf16[120,512]{1,0:T(8,128)(2,1)} %copy-done.19) | copy-start | bytes 368644
  99.7 15.6 %copy-start.22 = (bf16[120,512]{1,0:T(8,128)(2,1)S(1)}, bf16[120,512]{1,0:T(8,128)(2,1)}, u32[]{:S(2)}) copy-start(bf16[120,512]{1,0:T(8,128)(2,1)} %copy-done.21) | copy-start | bytes 368644
  99.7 15.6 %copy-start.24 = (bf16[120,512]{1,0:T(8,128)(2,1)S(1)}, bf16[120,512]{1,0:T(8,128)(2,1)}, u32[]{:S(2)}) copy-start(bf16[120,512]{1,0:T(8,128)(2,1)} %copy-done.23) | copy-start | bytes 368644
  99.7 37.0 %all-to-all-start.3 = ((bf16[16,40,640]{2,1,0:T(8,128)(2,1)}), bf16[16,40,640]{2,1,0:T(8,128)(2,1)S(1)}, u32[]{:S(2)}, u32[]{:S(2)}) async-start(bf16[16,40,640]{2,1,0:T(8,128)(2,1)} %shard_map.151), calls=%async_computation.3 | async-start | bytes 1638400 | tf_op jit(solution)/shard_map/all_to_all | solution.py:501
  115.3 21.4 %copy-start.4 = (s32[4]{0:T(128)S(1)}, s32[4]{0:T(128)}, u32[]{:S(2)}) copy-start(s32[4]{0:T(128)} %copy-done.3) | copy-start | bytes 52
  115.5 54.6 %copy-start.6 = (bf16[3,160,512]{2,1,0:T(8,128)(2,1)}, bf16[3,160,512]{2,1,0:T(8,128)(2,1)S(1)}, u32[]{:S(2)}) copy-start(bf16[3,160,512]{2,1,0:T(8,128)(2,1)S(1)} %pad_maximum_fusion.1.refs_3_) | copy-start | bytes 1474564
  115.5 33.6 %collective-permute-start.13 = (bf16[3,160,512]{2,1,0:T(8,128)(2,1)S(1)}, bf16[3,160,512]{2,1,0:T(8,128)(2,1)S(1)}, u32[]{:S(2)}, u32[]{:S(2)}) collective-permute-start(bf16[3,160,512]{2,1,0:T(8,128)(2,1)S(1)} %pad_maximum_fusion.1.refs_3_), channel_id=1, source_target_pairs={{0,128},{128,256},{256,384},{384,0},{1,129},{129,257},{257,385},{3... | collective-permute-start | bytes 1474568 | tf_op jit(solution)/shard_map/ppermute | solution.py:435
  117.7 31.4 %collective-permute-start.14 = (bf16[3,160,512]{2,1,0:T(8,128)(2,1)S(1)}, bf16[3,160,512]{2,1,0:T(8,128)(2,1)S(1)}, u32[]{:S(2)}, u32[]{:S(2)}) collective-permute-start(bf16[3,160,512]{2,1,0:T(8,128)(2,1)S(1)} %pad_maximum_fusion.1.refs_3_), channel_id=1, source_target_pairs={{0,256},{128,384},{256,0},{384,128},{1,257},{129,385},{257,1},{385... | collective-permute-start | bytes 1474568 | tf_op jit(solution)/shard_map/ppermute | solution.py:435
  121.4 27.7 %collective-permute-start.15 = (bf16[3,160,512]{2,1,0:T(8,128)(2,1)S(1)}, bf16[3,160,512]{2,1,0:T(8,128)(2,1)S(1)}, u32[]{:S(2)}, u32[]{:S(2)}) collective-permute-start(bf16[3,160,512]{2,1,0:T(8,128)(2,1)S(1)} %pad_maximum_fusion.1.refs_3_), channel_id=1, source_target_pairs={{0,384},{128,0},{256,128},{384,256},{1,385},{129,1},{257,129},{385... | collective-permute-start | bytes 1474568 | tf_op jit(solution)/shard_map/ppermute | solution.py:435
  149.1 21.0 %copy-start.11 = (bf16[3,160,512]{2,1,0:T(8,128)(2,1)}, bf16[3,160,512]{2,1,0:T(8,128)(2,1)S(1)}, u32[]{:S(2)}) copy-start(bf16[3,160,512]{2,1,0:T(8,128)(2,1)S(1)} %collective-permute-done.13.refs_4_) | copy-start | bytes 1474564
  149.1 21.0 %copy-start.12 = (bf16[3,160,512]{2,1,0:T(8,128)(2,1)}, bf16[3,160,512]{2,1,0:T(8,128)(2,1)S(1)}, u32[]{:S(2)}) copy-start(bf16[3,160,512]{2,1,0:T(8,128)(2,1)S(1)} %collective-permute-done.14.refs_5_) | copy-start | bytes 1474564
  149.1 21.0 %copy-start.13 = (bf16[3,160,512]{2,1,0:T(8,128)(2,1)}, bf16[3,160,512]{2,1,0:T(8,128)(2,1)S(1)}, u32[]{:S(2)}) copy-start(bf16[3,160,512]{2,1,0:T(8,128)(2,1)S(1)} %collective-permute-done.15.refs_6_) | copy-start | bytes 1474564
  149.9 20.2 %all-to-all-start.5 = ((f32[32,8,128]{2,1,0:T(8,128)}), f32[32,8,128]{2,1,0:T(8,128)S(1)}, u32[]{:S(2)}, u32[]{:S(2)}) async-start(f32[32,8,128]{2,1,0:T(8,128)} %broadcast_in_dim.3), calls=%async_computation.5 | async-start | bytes 262144 | tf_op jit(solution)/shard_map/all_to_all | solution.py:517
  159.1 0.7 collective-permute-start.12
  170.1 0.7 copy-start.10

commit v3 on v2

--- a/solution.py
+++ b/solution.py
@@ -61,9 +61,9 @@
 
 SMEM = pl.BlockSpec(memory_space=pltpu.SMEM)
 VMEM = pl.BlockSpec(memory_space=pltpu.VMEM)
-ANY = pl.BlockSpec(memory_space=pl.ANY)
-PARAMS = pltpu.CompilerParams(vmem_limit_bytes=40 * 1024 * 1024)
 WIDE = pltpu.CompilerParams(vmem_limit_bytes=60 * 1024 * 1024)
+HBM = pl.BlockSpec(memory_space=pltpu.HBM)
+PARAMS = pltpu.CompilerParams(vmem_limit_bytes=24 * 1024 * 1024)
 NT = (((1,), (1,)), ((), ()))
 
 
@@ -78,7 +78,7 @@
 
 
 def front_kernel(*refs):
-    out_ref, held, arrived = refs[9], refs[10:19], refs[19]
+    out_ref, factors_ref, held, arrived = refs[9], refs[10], refs[11:20], refs[20]
     copies = fetch(refs[:9], held, arrived)
     ids_ref, states_ref, gate_left_ref, up_left_ref, gate_ref, up_ref = held[:6]
     copies[0].wait()
@@ -103,6 +103,7 @@
             out_ref[x, kind * BANK : (kind + 1) * BANK] = part[:, x * CHUNK : (x + 1) * CHUNK]
     for kind in range(3):
         copies[6 + kind].wait()
+        factors_ref[kind * GROUP : (kind + 1) * GROUP] = held[6 + kind][...]
         start = 2 * BANK + kind * GROUP
         for x in range(NX):
             out_ref[x, start : start + GROUP] = held[6 + kind][
@@ -117,8 +118,11 @@
 def front(*arrays):
     return pl.pallas_call(
         front_kernel,
-        out_shape=jax.ShapeDtypeStruct((NX, 2 * BANK + 4 * GROUP, CHUNK), f32),
-        in_specs=[ANY] * 9,
+        out_shape=[
+            jax.ShapeDtypeStruct((NX, 2 * BANK + 4 * GROUP, CHUNK), f32),
+            jax.ShapeDtypeStruct((3 * GROUP, UNITS), bf16),
+        ],
+        in_specs=[HBM] * 9,
         scratch_shapes=[pltpu.VMEM(array.shape, array.dtype) for array in arrays]
         + [pltpu.SemaphoreType.DMA((9,))],
         compiler_params=WIDE,
@@ -270,14 +274,39 @@
     )(ids, got)
 
 
-def project_kernel(place_ref, hidden_ref, *refs):
-    out_ref, held, arrived = refs[2 * NX], refs[2 * NX + 1 : 4 * NX + 1], refs[4 * NX + 1]
-    own = list(refs[:NX])
-    own[1], own[3] = own[1].at[:, :KEPT], own[3].at[:, :KEPT]
-    other = [ref.at[:, :UNITS] for ref in refs[NX : 2 * NX]]
-    copies = fetch(own + other, held, arrived)
-    own_refs, other_refs = held[:NX], held[NX:]
+def project_kernel(place_ref, hidden_hbm, *refs):
+    out_ref, own_ref, other_ref, right_ref = refs[10:14]
+    arrived, hidden_ref = refs[14:16]
+    parts = [pl.ds(k * CHUNK, CHUNK) for k in range(8)]
+    rows = fetch(
+        [hidden_hbm.at[part] for part in parts],
+        [hidden_ref.at[part] for part in parts],
+        arrived.at[3],
+    )
+    half = WIDTH // 2
+    places = [(0, WIDTH), (WIDTH, WIDTH), (2 * WIDTH, half), (2 * WIDTH + half, half)]
+    places = [pl.ds(*spot) for spot in places + [(3 * WIDTH, WIDTH)]]
+    lanes = [slice(UNITS, KEPT)] * 2 + [slice(KEPT, KEPT + CHUNK)] * 2 + [slice(UNITS, KEPT)]
+    copies = [
+        fetch(
+            [ref.at[:, :UNITS] for ref in refs[:5]],
+            [own_ref.at[spot] for spot in places],
+            arrived.at[0],
+        ),
+        fetch(
+            [ref.at[:, lane] for ref, lane in zip(refs[:5], lanes)],
+            [right_ref.at[spot] for spot in places],
+            arrived.at[1],
+        ),
+        fetch(
+            [ref.at[:, :UNITS] for ref in refs[5:10]],
+            [other_ref.at[spot] for spot in places],
+            arrived.at[2],
+        ),
+    ]
     x_here, c_here = place_ref[0], place_ref[2]
+    for copy in rows:
+        copy.wait()
     dots = jnp.zeros((16, CHUNK), f32)
     for source in range(NC * NX * NYH):
         dots += hidden_ref[source * OWN : source * OWN + 16, PADDED - CHUNK :].astype(f32)
@@ -304,22 +333,23 @@
     other_rows = hidden_ref[pl.ds(start, UNITS), :].astype(f32)
     own_rows = jnp.transpose(own_rows)[:PART].astype(bf16)
     other_rows = jnp.transpose(other_rows)[:PART].astype(bf16)
+    for copy in copies[0]:
+        copy.wait()
+    total = lax.dot_general(own_rows, own_ref[...], NT, preferred_element_type=f32)
+    for copy in copies[1]:
+        copy.wait()
+    right = right_ref[...]
+    right = jnp.concatenate([right, right], axis=1)
+    total += lax.dot_general(shares, right, NT, preferred_element_type=f32)
+    for copy in copies[2]:
+        copy.wait()
+    total += lax.dot_general(other_rows, other_ref[...], NT, preferred_element_type=f32)
     for k in range(NX):
         x = lax.rem(x_here - k + NX, NX)
-        copies[k].wait()
-        copies[NX + k].wait()
-        total = lax.dot_general(
-            own_rows, own_refs[k][:, :UNITS], NT, preferred_element_type=f32
-        )
-        total += lax.dot_general(
-            other_rows, other_refs[k][...], NT, preferred_element_type=f32
-        )
-        right = own_refs[k][:, KEPT:] if k == 2 else own_refs[k][:, UNITS:KEPT]
-        right = jnp.concatenate([right, right], axis=1)
-        total += lax.dot_general(shares, right, NT, preferred_element_type=f32)
+        part = total[:, k * WIDTH : (k + 1) * WIDTH]
         for zh in range(NZH):
-            top = total[zh * BLOCK : zh * BLOCK + BLOCK // 2]
-            bottom = total[zh * BLOCK + BLOCK // 2 : (zh + 1) * BLOCK]
+            top = part[zh * BLOCK : zh * BLOCK + BLOCK // 2]
+            bottom = part[zh * BLOCK + BLOCK // 2 : (zh + 1) * BLOCK]
             out_ref[zh * NX + x] = jnp.concatenate([top, bottom], axis=1).astype(bf16)
 
 
@@ -327,12 +357,10 @@
     return pl.pallas_call(
         project_kernel,
         out_shape=jax.ShapeDtypeStruct((NZH * NX, BLOCK // 2, 2 * WIDTH), bf16),
-        in_specs=[SMEM, VMEM] + [ANY] * (2 * NX),
-        scratch_shapes=[
-            pltpu.VMEM((WIDTH, KEPT + CHUNK if k == 2 else KEPT), bf16) for k in range(NX)
-        ]
-        + [pltpu.VMEM((WIDTH, UNITS), bf16)] * NX
-        + [pltpu.SemaphoreType.DMA((2 * NX,))],
+        in_specs=[SMEM] + [HBM] * 11,
+        scratch_shapes=[pltpu.VMEM((NX * WIDTH, UNITS), bf16)] * 2
+        + [pltpu.VMEM((NX * WIDTH, CHUNK), bf16), pltpu.SemaphoreType.DMA((4, 8))]
+        + [pltpu.VMEM((NC * UNITS, PADDED), bf16)],
         compiler_params=WIDE,
     )(place, hidden, *own, *other)
 
@@ -417,13 +445,13 @@
     return pl.pallas_call(
         update_kernel,
         out_shape=[out] * 3,
-        in_specs=[SMEM, VMEM] + [ANY] * 3 + [VMEM] * NX,
-        out_specs=[ANY] * 3,
+        in_specs=[SMEM, VMEM] + [HBM] * 3 + [VMEM] * NX,
+        out_specs=[HBM] * 3,
         scratch_shapes=[pltpu.VMEM((3, MEMBERS, UNITS), bf16)]
         + [pltpu.VMEM((WIDTH, MEMBERS), bf16)] * 3
         + [pltpu.VMEM((WIDTH, UNITS), f32)] * 3
         + [pltpu.SemaphoreType.DMA((3,)), pltpu.SemaphoreType.DMA((6,))],
-        compiler_params=WIDE,
+        compiler_params=PARAMS,
     )(place, far, *lefts, *blocks)
 
 
@@ -455,11 +483,9 @@
     forth = to_owner()
     back = [(b, a) for a, b in forth]
 
-    own_factors = jnp.concatenate([gate_right, up_right, down_left], axis=0)
-    along = [shifted(own_factors, "yh", NYH, k) for k in (1, 2, 3)]
     columns = down_columns(place, down_matrix.T, down_right.T)
 
-    got = front(
+    got, own_factors = front(
         token_ids.T,
         states.T,
         gate_left.T,
@@ -470,30 +496,29 @@
         up_right,
         down_left,
     )
+    along = [shifted(own_factors, "yh", NYH, k) for k in (1, 2, 3)]
     sent = middle(lax.all_to_all(got, "x", 0, 0))
-    piece_target = lax.ppermute(target, EVERY, back)
-    partner = shifted(columns[0], "c", NC, 1)
-    sent, along[0], along[2], columns, piece_target, partner = lax.optimization_barrier(
-        (sent, along[0], along[2], columns, piece_target, partner)
-    )
+    sent, along, columns = lax.optimization_barrier((sent, along, columns))
     got = lax.all_to_all(sent, "yh", 0, 0)
 
     before = shifted(columns[1], "x", NX, 1)
     later = shifted(columns[2], "x", NX, 3)
+    partner = shifted(columns[0], "c", NC, 1)
+    (target,) = after(sent, target)
+    piece_target = lax.ppermute(target, EVERY, back)
     ids = token_ids.reshape(NX, NYH, GROUP * TOKENS).transpose(1, 0, 2).reshape(1, ROWS)
     outgoing = activate(ids, got)
-    outgoing, before, later, along[1] = lax.optimization_barrier(
-        (outgoing, before, later, along[1])
+    outgoing, before, later, partner, piece_target = lax.optimization_barrier(
+        (outgoing, before, later, partner, piece_target)
     )
 
     hidden = lax.all_to_all(
         outgoing.reshape(NC * NX * NYH * OWN, PADDED), ("c", "x", "yh"), 0, 0, tiled=True
     )
     half = WIDTH // 2
-    opposite = jnp.concatenate(
-        [shifted(before[:half], "x", NX, 1), shifted(later[half:], "x", NX, 3)], axis=0
-    )
-    columns = [columns[0], before, opposite, later]
+    ahead = shifted(before[:half], "x", NX, 1)
+    behind = shifted(later[half:], "x", NX, 3)
+    columns = [columns[0], before, ahead, behind, later]
     others = [partner] + [shifted(column, "c", NC, 1) for column in columns[1:]]
 
     pieces = project(place, hidden, columns, others)

time: 178 us -> 174 us (0.978)
  starting transfers between devices: 102 us -> 94.8 us
    all_to_all x1, waiting for transfers between devices: 0.01 us -> 6.09 us  [per_device(): got = lax.all_to_all(sent, 'yh', 0, 0)]
    all_to_all x1, starting transfers between devices: 15.5 us -> 11.1 us  [per_device(): got = lax.all_to_all(pieces, ('zh', 'zl', 'yl'), 0, 0)]
    ppermute x14 -> x15, starting transfers between devices: 55.2 us -> 51.7 us  [shifted(): return lax.ppermute(value, axis, [(i, (i + k) % size) for i in range(size)])]
    all_to_all x1, waiting for transfers between devices: 12.5 us -> 9.77 us  [per_device(): got = lax.all_to_all(pieces, ('zh', 'zl', 'yl'), 0, 0)]
    slice x2, local copies, waits for them, and re-layouts: 0.04 us -> 1.92 us  [the longest x1 0.96 us: per_device(): behind = shifted(later[half:], 'x', NX, 3)]
    ppermute x14 -> x15, waiting for transfers between devices: 11.2 us -> 10.1 us  [shifted(): return lax.ppermute(value, axis, [(i, (i + k) % size) for i in range(size)])]
    unnamed x57 -> x40, local copies, waits for them, and re-layouts: 4.51 us -> 3.59 us
  transfers between devices with their start and end apart: 21 -> 22, of which waited for: 7 -> 6; matrix products, arithmetic and copies ran while one was open for 1% -> 2% of each run, Pallas kernels for 3% -> 3%
where the time goes in v3:
time: 174 us; the launch traced here: 172 us
  starting transfers between devices  94.8 us (54%)
  waiting for transfers between devices  35.3 us (20%)
  Pallas kernels  19.8 us (11%)
  blocking collectives  12.9 us (7%)
  local copies, waits for them, and re-layouts  6.49 us (4%)
    ppermute x15, starting transfers between devices, shifted(): return lax.ppermute(value, axis, [(i, (i + k) % size) for i in range(size)])  51.7 us
    all_to_all x1, blocking collectives, per_device(): near = lax.all_to_all(sent, ('yh', 'zl', 'yl'), 0, 0)  12.9 us
    all_to_all x1, starting transfers between devices, per_device(): got = lax.all_to_all(pieces, ('zh', 'zl', 'yl'), 0, 0)  11.1 us
    ppermute x15, waiting for transfers between devices, shifted(): return lax.ppermute(value, axis, [(i, (i + k) % size) for i in range(size)])  10.1 us
    all_to_all x1, starting transfers between devices, per_device(): lax.all_to_all(outgoing.reshape(NC * NX * NYH * OWN, PADDED), ('c', 'x',...  10.1 us
    all_to_all x1, waiting for transfers between devices, per_device(): got = lax.all_to_all(pieces, ('zh', 'zl', 'yl'), 0, 0)  9.77 us
    all_to_all x1, waiting for transfers between devices, per_device(): far = lax.all_to_all(near, ('x', 'c', 'zh'), 0, 0)  9.37 us
    all_to_all x1, starting transfers between devices, per_device(): far = lax.all_to_all(near, ('x', 'c', 'zh'), 0, 0)  9.09 us
  transfers between devices with their start and end apart: 22, of which 6 were waited for; matrix products, arithmetic and copies ran while one was open for 2% of the time, Pallas kernels for 3%

profile of v3, /device:TPU:1, one launch (start us, length us, event | category | flops | bytes accessed | tf_op | source)
XLA Modules:
  0.0 171.7 jit_solution(9913344007046939289)
XLA Ops:
  0.6 4.3 %shard_map.147 = (f32[4,672,128]{2,1,0:T(8,128)}, bf16[120,512]{1,0:T(8,128)(2,1)}) custom-call(s32[4,640]{1,0:T(4,128)} %bitcast.36, bf16[320,256]{1,0:T(8,128)(2,1)} %bitcast.34, bf16[320,640]{1,0:T(8,128)(2,1)} %bitcast.26, bf16[320,640]{1,0:T(8,128)(2,1)} %bitcast.28, bf16[320,512]{1,0:T(8,128)(2,1)} %refs_4_.1, bf16[320,512]{1,0:T(8,128)(2,1)} %refs_5_.1, ...), custom_call_target="tpu_custom_call" | custom-call | tf_op jit(solution)/shard_map/pallas_call | solution.py:119
  5.0 5.0 %all-to-all-start = ((f32[4,672,128]{2,1,0:T(8,128)}), f32[4,672,128]{2,1,0:T(8,128)S(1)}, u32[]{:S(2)}, u32[]{:S(2)}) async-start(f32[4,672,128]{2,1,0:T(8,128)} %get-tuple-element.34), calls=%async_computation | async-start | bytes 2752512 | tf_op jit(solution)/shard_map/all_to_all | solution.py:500
  10.0 4.2 %collective-permute-start = (bf16[120,512]{1,0:T(8,128)(2,1)}, bf16[120,512]{1,0:T(8,128)(2,1)}, u32[]{:S(2)}, u32[]{:S(2)}) collective-permute-start(bf16[120,512]{1,0:T(8,128)(2,1)} %get-tuple-element.35), channel_id=1, source_target_pairs={{0,32},{32,64},{64,96},{96,0},{1,33},{33,65},{65,97},{97,1},{2,34}... | collective-permute-start | bytes 368648 | tf_op jit(solution)/shard_map/ppermute | solution.py:463
  14.2 5.7 %collective-permute-start.1 = (bf16[120,512]{1,0:T(8,128)(2,1)}, bf16[120,512]{1,0:T(8,128)(2,1)}, u32[]{:S(2)}, u32[]{:S(2)}) collective-permute-start(bf16[120,512]{1,0:T(8,128)(2,1)} %get-tuple-element.35), channel_id=1, source_target_pairs={{0,64},{32,96},{64,0},{96,32},{1,65},{33,97},{65,1},{97,33},{2,66}... | collective-permute-start | bytes 368648 | tf_op jit(solution)/shard_map/ppermute | solution.py:463
  19.9 5.0 %collective-permute-start.2 = (bf16[120,512]{1,0:T(8,128)(2,1)}, bf16[120,512]{1,0:T(8,128)(2,1)}, u32[]{:S(2)}, u32[]{:S(2)}) collective-permute-start(bf16[120,512]{1,0:T(8,128)(2,1)} %get-tuple-element.35), channel_id=1, source_target_pairs={{0,96},{32,0},{64,32},{96,64},{1,97},{33,1},{65,33},{97,65},{2,98}... | collective-permute-start | bytes 368648 | tf_op jit(solution)/shard_map/ppermute | solution.py:463
  24.9 1.2 shard_map.149
  26.2 1.0 shard_map.148
  27.2 5.6 %collective-permute-done.2 = bf16[120,512]{1,0:T(8,128)(2,1)} collective-permute-done((bf16[120,512]{1,0:T(8,128)(2,1)}, bf16[120,512]{1,0:T(8,128)(2,1)}, u32[]{:S(2)}, u32[]{:S(2)}) %collective-permute-start.2) | collective-permute-done | bytes 122912 | tf_op jit(solution)/shard_map/ppermute | solution.py:463
  32.8 5.6 %all-to-all-start.1 = ((f32[4,80,512]{2,1,0:T(8,128)}), f32[4,80,512]{2,1,0:T(8,128)S(1)}, u32[]{:S(2)}, u32[]{:S(2)}) async-start(f32[4,80,512]{2,1,0:T(8,128)} %shard_map.148), calls=%async_computation.1 | async-start | bytes 1310720 | tf_op jit(solution)/shard_map/all_to_all | solution.py:502
  38.4 3.4 %collective-permute-start.3 = (bf16[320,768]{1,0:T(8,128)(2,1)S(1)}, bf16[320,768]{1,0:T(8,128)(2,1)}, u32[]{:S(2)}, u32[]{:S(2)}) collective-permute-start(bf16[320,768]{1,0:T(8,128)(2,1)S(1)} %get-tuple-element.40), channel_id=1, source_target_pairs={{0,128},{128,256},{256,384},{384,0},{1,129},{129,257},{257,385},{3... | collective-permute-start | bytes 1474568 | tf_op jit(solution)/shard_map/ppermute | solution.py:463
  41.9 3.1 %collective-permute-start.4 = (bf16[320,768]{1,0:T(8,128)(2,1)S(1)}, bf16[320,768]{1,0:T(8,128)(2,1)}, u32[]{:S(2)}, u32[]{:S(2)}) collective-permute-start(bf16[320,768]{1,0:T(8,128)(2,1)S(1)} %get-tuple-element.41), channel_id=1, source_target_pairs={{0,384},{128,0},{256,128},{384,256},{1,385},{129,1},{257,129},{385... | collective-permute-start | bytes 1474568 | tf_op jit(solution)/shard_map/ppermute | solution.py:463
  45.0 3.2 %collective-permute-start.5 = (bf16[320,640]{1,0:T(8,128)(2,1)S(1)}, bf16[320,640]{1,0:T(8,128)(2,1)}, u32[]{:S(2)}, u32[]{:S(2)}) collective-permute-start(bf16[320,640]{1,0:T(8,128)(2,1)S(1)} %get-tuple-element.42.refs_0_), channel_id=1, source_target_pairs={{0,1},{1,0},{2,3},{3,2},{4,5},{5,4},{6,7},{7,6},{8,9},{9,8},{10,11... | collective-permute-start | bytes 1228808 | tf_op jit(solution)/shard_map/ppermute | solution.py:463
  48.2 0.7 collective-permute-start.6
  48.9 0.2 copy.16
  49.1 0.2 reshape.27
  49.3 6.1 %all-to-all-done.1.got_ref = f32[4,80,512]{2,1,0:T(8,128)S(1)} async-done(((f32[4,80,512]{2,1,0:T(8,128)}), f32[4,80,512]{2,1,0:T(8,128)S(1)}, u32[]{:S(2)}, u32[]{:S(2)}) %all-to-all-start.1) | async-done | bytes 655392 | tf_op jit(solution)/shard_map/all_to_all | solution.py:502
  55.4 2.5 %shard_map.150 = bf16[2,4,4,32,384]{4,3,2,1,0:T(8,128)(2,1)} custom-call(s32[1,2560]{1,0:T(1,128)S(1)} %reshape.28.ids_ref, f32[4,80,512]{2,1,0:T(8,128)S(1)} %all-to-all-done.1.got_ref), custom_call_target="tpu_custom_call" | custom-call | tf_op jit(solution)/shard_map/pallas_call | solution.py:269
  58.0 10.1 %all-to-all-start.2 = ((bf16[32,32,384]{2,1,0:T(8,128)(2,1)}), bf16[32,32,384]{2,1,0:T(8,128)(2,1)S(1)}, u32[]{:S(2)}, u32[]{:S(2)}) async-start(bf16[32,32,384]{2,1,0:T(8,128)(2,1)} %bitcast.11), calls=%async_computation.2 | async-start | bytes 1572864 | tf_op jit(solution)/shard_map/all_to_all | solution.py:515
  68.1 1.0 slice.6
  69.0 3.3 %collective-permute-start.7 = (bf16[160,768]{1,0:T(8,128)(2,1)S(1)}, bf16[160,768]{1,0:T(8,128)(2,1)S(1)}, u32[]{:S(2)}, u32[]{:S(2)}) collective-permute-start(bf16[160,768]{1,0:T(8,128)(2,1)S(1)} %slice.6), channel_id=1, source_target_pairs={{0,128},{128,256},{256,384},{384,0},{1,129},{129,257},{257,385},{3... | collective-permute-start | bytes 737288 | tf_op jit(solution)/shard_map/ppermute | solution.py:463
  72.3 1.0 slice.7
  73.3 3.2 %collective-permute-start.8 = (bf16[160,768]{1,0:T(8,128)(2,1)S(1)}, bf16[160,768]{1,0:T(8,128)(2,1)S(1)}, u32[]{:S(2)}, u32[]{:S(2)}) collective-permute-start(bf16[160,768]{1,0:T(8,128)(2,1)S(1)} %slice.7), channel_id=1, source_target_pairs={{0,384},{128,0},{256,128},{384,256},{1,385},{129,1},{257,129},{385... | collective-permute-start | bytes 737288 | tf_op jit(solution)/shard_map/ppermute | solution.py:463
  76.5 2.7 %collective-permute-start.9 = (bf16[320,768]{1,0:T(8,128)(2,1)}, bf16[320,768]{1,0:T(8,128)(2,1)S(1)}, u32[]{:S(2)}, u32[]{:S(2)}) collective-permute-start(bf16[320,768]{1,0:T(8,128)(2,1)} %collective-permute-done.3.refs_1_), channel_id=1, source_target_pairs={{0,1},{1,0},{2,3},{3,2},{4,5},{5,4},{6,7},{7,6},{8,9},{9,8},{10,11... | collective-permute-start | bytes 1474568 | tf_op jit(solution)/shard_map/ppermute | solution.py:463
  79.2 1.9 %collective-permute-start.12 = (bf16[320,768]{1,0:T(8,128)(2,1)}, bf16[320,768]{1,0:T(8,128)(2,1)S(1)}, u32[]{:S(2)}, u32[]{:S(2)}) collective-permute-start(bf16[320,768]{1,0:T(8,128)(2,1)} %collective-permute-done.4.refs_4_), channel_id=1, source_target_pairs={{0,1},{1,0},{2,3},{3,2},{4,5},{5,4},{6,7},{7,6},{8,9},{9,8},{10,11... | collective-permute-start | bytes 1474568 | tf_op jit(solution)/shard_map/ppermute | solution.py:463
  81.2 2.4 %collective-permute-start.10 = (bf16[160,768]{1,0:T(8,128)(2,1)S(1)}, bf16[160,768]{1,0:T(8,128)(2,1)S(1)}, u32[]{:S(2)}, u32[]{:S(2)}) collective-permute-start(bf16[160,768]{1,0:T(8,128)(2,1)S(1)} %collective-permute-done.7.refs_2_), channel_id=1, source_target_pairs={{0,1},{1,0},{2,3},{3,2},{4,5},{5,4},{6,7},{7,6},{8,9},{9,8},{10,11... | collective-permute-start | bytes 737288 | tf_op jit(solution)/shard_map/ppermute | solution.py:463
  83.6 3.4 %collective-permute-done.8.refs_3_ = bf16[160,768]{1,0:T(8,128)(2,1)S(1)} collective-permute-done((bf16[160,768]{1,0:T(8,128)(2,1)S(1)}, bf16[160,768]{1,0:T(8,128)(2,1)S(1)}, u32[]{:S(2)}, u32[]{:S(2)}) %collective-permute-start.8) | collective-permute-done | bytes 245792 | tf_op jit(solution)/shard_map/ppermute | solution.py:463
  87.0 3.2 %collective-permute-start.11 = (bf16[160,768]{1,0:T(8,128)(2,1)S(1)}, bf16[160,768]{1,0:T(8,128)(2,1)S(1)}, u32[]{:S(2)}, u32[]{:S(2)}) collective-permute-start(bf16[160,768]{1,0:T(8,128)(2,1)S(1)} %collective-permute-done.8.refs_3_), channel_id=1, source_target_pairs={{0,1},{1,0},{2,3},{3,2},{4,5},{5,4},{6,7},{7,6},{8,9},{9,8},{10,11... | collective-permute-start | bytes 737288 | tf_op jit(solution)/shard_map/ppermute | solution.py:463
  90.2 1.1 collective-permute-done.11.refs_8_
  91.4 0.6 copy-done.16
  92.2 0.2 copy-done.12
  92.3 0.3 copy-done.10
  92.6 5.2 %shard_map.151 = bf16[16,40,640]{2,1,0:T(8,128)(2,1)} custom-call(s32[4]{0:T(128)} %copy-done.7, bf16[1024,384]{1,0:T(8,128)(2,1)} %bitcast.33, bf16[320,640]{1,0:T(8,128)(2,1)} %copy-done.3, bf16[320,768]{1,0:T(8,128)(2,1)} %collective-permute-done.3.refs_1_, bf16[160,768]{1,0:T(8,128)(2,1)} %copy-done.13, bf16[160,768]{1,0:T(8,128)(2,1)} %copy-done.14, ...), custom_call_target="tpu_custom_call" | custom-call | tf_op jit(solution)/shard_map/pallas_call | solution.py:357
  97.8 11.1 %all-to-all-start.3 = ((bf16[16,40,640]{2,1,0:T(8,128)(2,1)}), bf16[16,40,640]{2,1,0:T(8,128)(2,1)S(1)}, u32[]{:S(2)}, u32[]{:S(2)}) async-start(bf16[16,40,640]{2,1,0:T(8,128)(2,1)} %shard_map.151), calls=%async_computation.3 | async-start | bytes 1638400 | tf_op jit(solution)/shard_map/all_to_all | solution.py:526
  109.0 1.1 pad_maximum_fusion
  110.2 3.2 %collective-permute-start.14 = (bf16[3,160,512]{2,1,0:T(8,128)(2,1)S(1)}, bf16[3,160,512]{2,1,0:T(8,128)(2,1)S(1)}, u32[]{:S(2)}, u32[]{:S(2)}) collective-permute-start(bf16[3,160,512]{2,1,0:T(8,128)(2,1)S(1)} %pad_maximum_fusion.1.refs_3_), channel_id=1, source_target_pairs={{0,128},{128,256},{256,384},{384,0},{1,129},{129,257},{257,385},{3... | collective-permute-start | bytes 1474568 | tf_op jit(solution)/shard_map/ppermute | solution.py:463
  113.4 3.7 %collective-permute-start.15 = (bf16[3,160,512]{2,1,0:T(8,128)(2,1)S(1)}, bf16[3,160,512]{2,1,0:T(8,128)(2,1)S(1)}, u32[]{:S(2)}, u32[]{:S(2)}) collective-permute-start(bf16[3,160,512]{2,1,0:T(8,128)(2,1)S(1)} %pad_maximum_fusion.1.refs_3_), channel_id=1, source_target_pairs={{0,256},{128,384},{256,0},{384,128},{1,257},{129,385},{257,1},{385... | collective-permute-start | bytes 1474568 | tf_op jit(solution)/shard_map/ppermute | solution.py:463
  117.1 3.4 %collective-permute-start.16 = (bf16[3,160,512]{2,1,0:T(8,128)(2,1)S(1)}, bf16[3,160,512]{2,1,0:T(8,128)(2,1)}, u32[]{:S(2)}, u32[]{:S(2)}) collective-permute-start(bf16[3,160,512]{2,1,0:T(8,128)(2,1)S(1)} %pad_maximum_fusion.1.refs_3_), channel_id=1, source_target_pairs={{0,384},{128,0},{256,128},{384,256},{1,385},{129,1},{257,129},{385... | collective-permute-start | bytes 1474568 | tf_op jit(solution)/shard_map/ppermute | solution.py:463
  120.6 9.8 %all-to-all-done.3.got_ref = bf16[16,40,640]{2,1,0:T(8,128)(2,1)S(1)} async-done(((bf16[16,40,640]{2,1,0:T(8,128)(2,1)}), bf16[16,40,640]{2,1,0:T(8,128)(2,1)S(1)}, u32[]{:S(2)}, u32[]{:S(2)}) %all-to-all-start.3) | async-done | bytes 819232 | tf_op jit(solution)/shard_map/all_to_all | solution.py:526
  130.4 0.8 copy-done.6
  131.2 0.8 shard_map.152
  132.0 0.6 copy-done.9
  132.6 12.9 %all_to_all.36 = f32[16,8,128]{2,1,0:T(8,128)S(1)} all-to-all(f32[16,8,128]{2,1,0:T(8,128)S(1)} %get-tuple-element.50), channel_id=1, replica_groups=mesh['x'=4,'yh'=4,'zh'=4,'zl'=2,'yl'=2,'c'=2] {'yh','zl','yl'}, dimensions={0} | all-to-all | bytes 131072 | tf_op jit(solution)/shard_map/all_to_all | solution.py:539
  145.6 0.7 broadcast_in_dim.3
  146.2 9.1 %all-to-all-start.5 = ((f32[32,8,128]{2,1,0:T(8,128)}), f32[32,8,128]{2,1,0:T(8,128)S(1)}, u32[]{:S(2)}, u32[]{:S(2)}) async-start(f32[32,8,128]{2,1,0:T(8,128)} %broadcast_in_dim.3), calls=%async_computation.5 | async-start | bytes 262144 | tf_op jit(solution)/shard_map/all_to_all | solution.py:542
  155.3 1.6 collective-permute-start.13
  156.9 9.4 %all-to-all-done.5.far_ref = f32[32,8,128]{2,1,0:T(8,128)S(1)} async-done(((f32[32,8,128]{2,1,0:T(8,128)}), f32[32,8,128]{2,1,0:T(8,128)S(1)}, u32[]{:S(2)}, u32[]{:S(2)}) %all-to-all-start.5) | async-done | bytes 131104 | tf_op jit(solution)/shard_map/all_to_all | solution.py:542
  166.3 4.8 %shard_map.153 = (f32[320,512]{1,0:T(8,128)}, f32[320,512]{1,0:T(8,128)}, f32[320,512]{1,0:T(8,128)}) custom-call(s32[4]{0:T(128)S(1)} %copy-done.8, f32[32,8,128]{2,1,0:T(8,128)S(1)} %all-to-all-done.5.far_ref, bf16[320,640]{1,0:T(8,128)(2,1)S(1)} %bitcast.27, bf16[320,640]{1,0:T(8,128)(2,1)S(1)} %bitcast.29, bf16[320,640]{1,0:T(8,128)(2,1)S(1)} %bitcast.31, ...), custom_call_target="tpu_custom_call" | custom-call | tf_op jit(solution)/shard_map/pallas_call | solution.py:445
  171.1 0.7 copy.19
  (55 shorter events, 0.6 us)
Async XLA Ops:
  5.0 20.0 %copy-start.2 = (bf16[640,320]{0,1:T(8,128)(2,1)S(1)}, bf16[640,320]{0,1:T(8,128)(2,1)}, u32[]{:S(2)}) copy-start(bf16[640,320]{0,1:T(8,128)(2,1)} %param.22) | copy-start | bytes 1228804
  5.0 20.0 %copy-start.4 = (bf16[512,320]{0,1:T(8,128)(2,1)S(1)}, bf16[512,320]{0,1:T(8,128)(2,1)}, u32[]{:S(2)}) copy-start(bf16[512,320]{0,1:T(8,128)(2,1)} %param.16) | copy-start | bytes 983044
  5.0 21.2 %all-to-all-start = ((f32[4,672,128]{2,1,0:T(8,128)}), f32[4,672,128]{2,1,0:T(8,128)S(1)}, u32[]{:S(2)}, u32[]{:S(2)}) async-start(f32[4,672,128]{2,1,0:T(8,128)} %get-tuple-element.34), calls=%async_computation | async-start | bytes 2752512 | tf_op jit(solution)/shard_map/all_to_all | solution.py:500
  10.0 17.2 %collective-permute-start = (bf16[120,512]{1,0:T(8,128)(2,1)}, bf16[120,512]{1,0:T(8,128)(2,1)}, u32[]{:S(2)}, u32[]{:S(2)}) collective-permute-start(bf16[120,512]{1,0:T(8,128)(2,1)} %get-tuple-element.35), channel_id=1, source_target_pairs={{0,32},{32,64},{64,96},{96,0},{1,33},{33,65},{65,97},{97,1},{2,34}... | collective-permute-start | bytes 368648 | tf_op jit(solution)/shard_map/ppermute | solution.py:463
  14.2 13.0 %collective-permute-start.1 = (bf16[120,512]{1,0:T(8,128)(2,1)}, bf16[120,512]{1,0:T(8,128)(2,1)}, u32[]{:S(2)}, u32[]{:S(2)}) collective-permute-start(bf16[120,512]{1,0:T(8,128)(2,1)} %get-tuple-element.35), channel_id=1, source_target_pairs={{0,64},{32,96},{64,0},{96,32},{1,65},{33,97},{65,1},{97,33},{2,66}... | collective-permute-start | bytes 368648 | tf_op jit(solution)/shard_map/ppermute | solution.py:463
  19.9 13.0 %collective-permute-start.2 = (bf16[120,512]{1,0:T(8,128)(2,1)}, bf16[120,512]{1,0:T(8,128)(2,1)}, u32[]{:S(2)}, u32[]{:S(2)}) collective-permute-start(bf16[120,512]{1,0:T(8,128)(2,1)} %get-tuple-element.35), channel_id=1, source_target_pairs={{0,96},{32,0},{64,32},{96,64},{1,97},{33,1},{65,33},{97,65},{2,98}... | collective-permute-start | bytes 368648 | tf_op jit(solution)/shard_map/ppermute | solution.py:463
  24.9 2.3 %copy-start.7 = (s32[4]{0:T(128)}, s32[4]{0:T(128)S(1)}, u32[]{:S(2)}) copy-start(s32[4]{0:T(128)S(1)} %pad_add_fusion.place_ref) | copy-start | bytes 52
  26.1 18.9 %copy-start.3 = (bf16[320,640]{1,0:T(8,128)(2,1)}, bf16[320,640]{1,0:T(8,128)(2,1)S(1)}, u32[]{:S(2)}) copy-start(bf16[320,640]{1,0:T(8,128)(2,1)S(1)} %get-tuple-element.42.refs_0_) | copy-start | bytes 1228804
  26.1 22.1 %copy-start.18 = (bf16[80,320]{1,0:T(8,128)(2,1)S(1)}, bf16[80,320]{1,0:T(8,128)(2,1)}, u32[]{:S(2)}) copy-start(bf16[80,320]{1,0:T(8,128)(2,1)} %param.23) | copy-start | bytes 153604
  26.1 22.7 %copy-start.17 = (s32[640,4]{0,1:T(4,128)S(1)}, s32[640,4]{0,1:T(4,128)}, u32[]{:S(2)}) copy-start(s32[640,4]{0,1:T(4,128)} %param.13) | copy-start | bytes 30724
  32.8 22.6 %all-to-all-start.1 = ((f32[4,80,512]{2,1,0:T(8,128)}), f32[4,80,512]{2,1,0:T(8,128)S(1)}, u32[]{:S(2)}, u32[]{:S(2)}) async-start(f32[4,80,512]{2,1,0:T(8,128)} %shard_map.148), calls=%async_computation.1 | async-start | bytes 1310720 | tf_op jit(solution)/shard_map/all_to_all | solution.py:502
  38.4 19.5 %collective-permute-start.3 = (bf16[320,768]{1,0:T(8,128)(2,1)S(1)}, bf16[320,768]{1,0:T(8,128)(2,1)}, u32[]{:S(2)}, u32[]{:S(2)}) collective-permute-start(bf16[320,768]{1,0:T(8,128)(2,1)S(1)} %get-tuple-element.40), channel_id=1, source_target_pairs={{0,128},{128,256},{256,384},{384,0},{1,129},{129,257},{257,385},{3... | collective-permute-start | bytes 1474568 | tf_op jit(solution)/shard_map/ppermute | solution.py:463
  41.9 16.1 %collective-permute-start.4 = (bf16[320,768]{1,0:T(8,128)(2,1)S(1)}, bf16[320,768]{1,0:T(8,128)(2,1)}, u32[]{:S(2)}, u32[]{:S(2)}) collective-permute-start(bf16[320,768]{1,0:T(8,128)(2,1)S(1)} %get-tuple-element.41), channel_id=1, source_target_pairs={{0,384},{128,0},{256,128},{384,256},{1,385},{129,1},{257,129},{385... | collective-permute-start | bytes 1474568 | tf_op jit(solution)/shard_map/ppermute | solution.py:463
  45.0 12.9 %collective-permute-start.5 = (bf16[320,640]{1,0:T(8,128)(2,1)S(1)}, bf16[320,640]{1,0:T(8,128)(2,1)}, u32[]{:S(2)}, u32[]{:S(2)}) collective-permute-start(bf16[320,640]{1,0:T(8,128)(2,1)S(1)} %get-tuple-element.42.refs_0_), channel_id=1, source_target_pairs={{0,1},{1,0},{2,3},{3,2},{4,5},{5,4},{6,7},{7,6},{8,9},{9,8},{10,11... | collective-permute-start | bytes 1228808 | tf_op jit(solution)/shard_map/ppermute | solution.py:463
  48.2 9.8 %collective-permute-start.6 = (bf16[80,320]{1,0:T(8,128)(2,1)S(1)}, bf16[80,320]{1,0:T(8,128)(2,1)S(1)}, u32[]{:S(2)}, u32[]{:S(2)}) collective-permute-start(bf16[80,320]{1,0:T(8,128)(2,1)S(1)} %copy-done.18), channel_id=1, source_target_pairs={{0,0},{1,1},{128,2},{129,3},{256,4},{257,5},{384,6},{385,7},{8,8},... | collective-permute-start | bytes 153608 | tf_op jit(solution)/shard_map/ppermute | solution.py:508
  58.0 39.8 %copy-start.5 = (bf16[80,320]{1,0:T(8,128)(2,1)}, bf16[80,320]{1,0:T(8,128)(2,1)S(1)}, u32[]{:S(2)}) copy-start(bf16[80,320]{1,0:T(8,128)(2,1)S(1)} %collective-permute-done.6.target_ref) | copy-start | bytes 153604
  58.0 33.4 %all-to-all-start.2 = ((bf16[32,32,384]{2,1,0:T(8,128)(2,1)}), bf16[32,32,384]{2,1,0:T(8,128)(2,1)S(1)}, u32[]{:S(2)}, u32[]{:S(2)}) async-start(bf16[32,32,384]{2,1,0:T(8,128)(2,1)} %bitcast.11), calls=%async_computation.2 | async-start | bytes 1572864 | tf_op jit(solution)/shard_map/all_to_all | solution.py:515
  69.0 12.1 %collective-permute-start.7 = (bf16[160,768]{1,0:T(8,128)(2,1)S(1)}, bf16[160,768]{1,0:T(8,128)(2,1)S(1)}, u32[]{:S(2)}, u32[]{:S(2)}) collective-permute-start(bf16[160,768]{1,0:T(8,128)(2,1)S(1)} %slice.6), channel_id=1, source_target_pairs={{0,128},{128,256},{256,384},{384,0},{1,129},{129,257},{257,385},{3... | collective-permute-start | bytes 737288 | tf_op jit(solution)/shard_map/ppermute | solution.py:463
  73.3 13.7 %collective-permute-start.8 = (bf16[160,768]{1,0:T(8,128)(2,1)S(1)}, bf16[160,768]{1,0:T(8,128)(2,1)S(1)}, u32[]{:S(2)}, u32[]{:S(2)}) collective-permute-start(bf16[160,768]{1,0:T(8,128)(2,1)S(1)} %slice.7), channel_id=1, source_target_pairs={{0,384},{128,0},{256,128},{384,256},{1,385},{129,1},{257,129},{385... | collective-permute-start | bytes 737288 | tf_op jit(solution)/shard_map/ppermute | solution.py:463
  76.5 14.8 %collective-permute-start.9 = (bf16[320,768]{1,0:T(8,128)(2,1)}, bf16[320,768]{1,0:T(8,128)(2,1)S(1)}, u32[]{:S(2)}, u32[]{:S(2)}) collective-permute-start(bf16[320,768]{1,0:T(8,128)(2,1)} %collective-permute-done.3.refs_1_), channel_id=1, source_target_pairs={{0,1},{1,0},{2,3},{3,2},{4,5},{5,4},{6,7},{7,6},{8,9},{9,8},{10,11... | collective-permute-start | bytes 1474568 | tf_op jit(solution)/shard_map/ppermute | solution.py:463
  79.2 12.1 %collective-permute-start.12 = (bf16[320,768]{1,0:T(8,128)(2,1)}, bf16[320,768]{1,0:T(8,128)(2,1)S(1)}, u32[]{:S(2)}, u32[]{:S(2)}) collective-permute-start(bf16[320,768]{1,0:T(8,128)(2,1)} %collective-permute-done.4.refs_4_), channel_id=1, source_target_pairs={{0,1},{1,0},{2,3},{3,2},{4,5},{5,4},{6,7},{7,6},{8,9},{9,8},{10,11... | collective-permute-start | bytes 1474568 | tf_op jit(solution)/shard_map/ppermute | solution.py:463
  81.1 10.2 %copy-start.13 = (bf16[160,768]{1,0:T(8,128)(2,1)}, bf16[160,768]{1,0:T(8,128)(2,1)S(1)}, u32[]{:S(2)}) copy-start(bf16[160,768]{1,0:T(8,128)(2,1)S(1)} %collective-permute-done.7.refs_2_) | copy-start | bytes 737284
  81.2 9.0 %collective-permute-start.10 = (bf16[160,768]{1,0:T(8,128)(2,1)S(1)}, bf16[160,768]{1,0:T(8,128)(2,1)S(1)}, u32[]{:S(2)}, u32[]{:S(2)}) collective-permute-start(bf16[160,768]{1,0:T(8,128)(2,1)S(1)} %collective-permute-done.7.refs_2_), channel_id=1, source_target_pairs={{0,1},{1,0},{2,3},{3,2},{4,5},{5,4},{6,7},{7,6},{8,9},{9,8},{10,11... | collective-permute-start | bytes 737288 | tf_op jit(solution)/shard_map/ppermute | solution.py:463
  87.0 4.4 %copy-start.14 = (bf16[160,768]{1,0:T(8,128)(2,1)}, bf16[160,768]{1,0:T(8,128)(2,1)S(1)}, u32[]{:S(2)}) copy-start(bf16[160,768]{1,0:T(8,128)(2,1)S(1)} %collective-permute-done.8.refs_3_) | copy-start | bytes 737284
  87.0 4.4 %collective-permute-start.11 = (bf16[160,768]{1,0:T(8,128)(2,1)S(1)}, bf16[160,768]{1,0:T(8,128)(2,1)S(1)}, u32[]{:S(2)}, u32[]{:S(2)}) collective-permute-start(bf16[160,768]{1,0:T(8,128)(2,1)S(1)} %collective-permute-done.8.refs_3_), channel_id=1, source_target_pairs={{0,1},{1,0},{2,3},{3,2},{4,5},{5,4},{6,7},{7,6},{8,9},{9,8},{10,11... | collective-permute-start | bytes 737288 | tf_op jit(solution)/shard_map/ppermute | solution.py:463
  90.2 1.2 copy-start.15
  91.3 0.7 copy-start.16
  91.3 0.9 copy-start.11
  91.3 1.0 copy-start.12
  91.4 1.3 copy-start.10
  97.8 32.6 %all-to-all-start.3 = ((bf16[16,40,640]{2,1,0:T(8,128)(2,1)}), bf16[16,40,640]{2,1,0:T(8,128)(2,1)S(1)}, u32[]{:S(2)}, u32[]{:S(2)}) async-start(bf16[16,40,640]{2,1,0:T(8,128)(2,1)} %shard_map.151), calls=%async_computation.3 | async-start | bytes 1638400 | tf_op jit(solution)/shard_map/all_to_all | solution.py:526
  108.9 21.4 %copy-start.8 = (s32[4]{0:T(128)S(1)}, s32[4]{0:T(128)}, u32[]{:S(2)}) copy-start(s32[4]{0:T(128)} %copy-done.7) | copy-start | bytes 52
  110.2 56.1 %copy-start = (bf16[640,320]{0,1:T(8,128)(2,1)S(1)}, bf16[640,320]{0,1:T(8,128)(2,1)}, u32[]{:S(2)}) copy-start(bf16[640,320]{0,1:T(8,128)(2,1)} %param.17) | copy-start | bytes 1228804
  110.2 56.1 %copy-start.1 = (bf16[640,320]{0,1:T(8,128)(2,1)S(1)}, bf16[640,320]{0,1:T(8,128)(2,1)}, u32[]{:S(2)}) copy-start(bf16[640,320]{0,1:T(8,128)(2,1)} %param.19) | copy-start | bytes 1228804
  110.2 35.3 %collective-permute-start.14 = (bf16[3,160,512]{2,1,0:T(8,128)(2,1)S(1)}, bf16[3,160,512]{2,1,0:T(8,128)(2,1)S(1)}, u32[]{:S(2)}, u32[]{:S(2)}) collective-permute-start(bf16[3,160,512]{2,1,0:T(8,128)(2,1)S(1)} %pad_maximum_fusion.1.refs_3_), channel_id=1, source_target_pairs={{0,128},{128,256},{256,384},{384,0},{1,129},{129,257},{257,385},{3... | collective-permute-start | bytes 1474568 | tf_op jit(solution)/shard_map/ppermute | solution.py:463
  113.4 32.1 %collective-permute-start.15 = (bf16[3,160,512]{2,1,0:T(8,128)(2,1)S(1)}, bf16[3,160,512]{2,1,0:T(8,128)(2,1)S(1)}, u32[]{:S(2)}, u32[]{:S(2)}) collective-permute-start(bf16[3,160,512]{2,1,0:T(8,128)(2,1)S(1)} %pad_maximum_fusion.1.refs_3_), channel_id=1, source_target_pairs={{0,256},{128,384},{256,0},{384,128},{1,257},{129,385},{257,1},{385... | collective-permute-start | bytes 1474568 | tf_op jit(solution)/shard_map/ppermute | solution.py:463
  117.1 28.4 %collective-permute-start.16 = (bf16[3,160,512]{2,1,0:T(8,128)(2,1)S(1)}, bf16[3,160,512]{2,1,0:T(8,128)(2,1)}, u32[]{:S(2)}, u32[]{:S(2)}) collective-permute-start(bf16[3,160,512]{2,1,0:T(8,128)(2,1)S(1)} %pad_maximum_fusion.1.refs_3_), channel_id=1, source_target_pairs={{0,384},{128,0},{256,128},{384,256},{1,385},{129,1},{257,129},{385... | collective-permute-start | bytes 1474568 | tf_op jit(solution)/shard_map/ppermute | solution.py:463
  130.4 0.8 copy-start.6
  132.0 0.7 copy-start.9
  146.2 20.0 %all-to-all-start.5 = ((f32[32,8,128]{2,1,0:T(8,128)}), f32[32,8,128]{2,1,0:T(8,128)S(1)}, u32[]{:S(2)}, u32[]{:S(2)}) async-start(f32[32,8,128]{2,1,0:T(8,128)} %broadcast_in_dim.3), calls=%async_computation.5 | async-start | bytes 262144 | tf_op jit(solution)/shard_map/all_to_all | solution.py:542
  155.3 1.6 collective-permute-start.13

commit v4 on v3

--- a/solution.py
+++ b/solution.py
@@ -101,14 +101,14 @@
         part = jnp.dot(states, matrix[...], preferred_element_type=f32)
         for x in range(NX):
             out_ref[x, kind * BANK : (kind + 1) * BANK] = part[:, x * CHUNK : (x + 1) * CHUNK]
+    rights = []
     for kind in range(3):
         copies[6 + kind].wait()
-        factors_ref[kind * GROUP : (kind + 1) * GROUP] = held[6 + kind][...]
+        rights.append(held[6 + kind][...].astype(f32))
         start = 2 * BANK + kind * GROUP
         for x in range(NX):
-            out_ref[x, start : start + GROUP] = held[6 + kind][
-                :, x * CHUNK : (x + 1) * CHUNK
-            ].astype(f32)
+            out_ref[x, start : start + GROUP] = rights[kind][:, x * CHUNK : (x + 1) * CHUNK]
+    factors_ref[...] = jnp.concatenate(rights, axis=0).astype(bf16)
     for x in range(NX):
         for k in range(CHUNKS):
             start = 2 * BANK + 3 * GROUP + 8 * k
@@ -277,7 +277,7 @@
 def project_kernel(place_ref, hidden_hbm, *refs):
     out_ref, own_ref, other_ref, right_ref = refs[10:14]
     arrived, hidden_ref = refs[14:16]
-    parts = [pl.ds(k * CHUNK, CHUNK) for k in range(8)]
+    parts = [pl.ds(k * UNITS, UNITS) for k in range(NC)]
     rows = fetch(
         [hidden_hbm.at[part] for part in parts],
         [hidden_ref.at[part] for part in parts],

time: 174 us -> 173 us (level)
  no operation moved by 1% of the time
where the time goes in v4:
time: 173 us; the launch traced here: 172 us
  starting transfers between devices  94.8 us (55%)
  waiting for transfers between devices  35.3 us (20%)
  Pallas kernels  19.7 us (11%)
  blocking collectives  12.9 us (7%)
  local copies, waits for them, and re-layouts  6.49 us (4%)
    ppermute x15, starting transfers between devices, shifted(): return lax.ppermute(value, axis, [(i, (i + k) % size) for i in range(size)])  51.7 us
    all_to_all x1, blocking collectives, per_device(): near = lax.all_to_all(sent, ('yh', 'zl', 'yl'), 0, 0)  12.9 us
    all_to_all x1, starting transfers between devices, per_device(): got = lax.all_to_all(pieces, ('zh', 'zl', 'yl'), 0, 0)  11.1 us
    ppermute x15, waiting for transfers between devices, shifted(): return lax.ppermute(value, axis, [(i, (i + k) % size) for i in range(size)])  10.1 us
    all_to_all x1, starting transfers between devices, per_device(): lax.all_to_all(outgoing.reshape(NC * NX * NYH * OWN, PADDED), ('c', 'x',...  10.1 us
    all_to_all x1, waiting for transfers between devices, per_device(): got = lax.all_to_all(pieces, ('zh', 'zl', 'yl'), 0, 0)  9.75 us
    all_to_all x1, waiting for transfers between devices, per_device(): far = lax.all_to_all(near, ('x', 'c', 'zh'), 0, 0)  9.37 us
    all_to_all x1, starting transfers between devices, per_device(): far = lax.all_to_all(near, ('x', 'c', 'zh'), 0, 0)  9.1 us
  transfers between devices with their start and end apart: 22, of which 6 were waited for; matrix products, arithmetic and copies ran while one was open for 2% of the time, Pallas kernels for 3%

profile of v4, /device:TPU:1, one launch (start us, length us, event | category | flops | bytes accessed | tf_op | source)
XLA Modules:
  0.0 171.6 jit_solution(7550361786068052573)
XLA Ops:
  0.6 4.3 %shard_map.147 = (f32[4,672,128]{2,1,0:T(8,128)}, bf16[120,512]{1,0:T(8,128)(2,1)}) custom-call(s32[4,640]{1,0:T(4,128)} %bitcast.36, bf16[320,256]{1,0:T(8,128)(2,1)} %bitcast.34, bf16[320,640]{1,0:T(8,128)(2,1)} %bitcast.26, bf16[320,640]{1,0:T(8,128)(2,1)} %bitcast.28, bf16[320,512]{1,0:T(8,128)(2,1)} %refs_4_.1, bf16[320,512]{1,0:T(8,128)(2,1)} %refs_5_.1, ...), custom_call_target="tpu_custom_call" | custom-call | tf_op jit(solution)/shard_map/pallas_call | solution.py:119
  5.0 5.0 %all-to-all-start = ((f32[4,672,128]{2,1,0:T(8,128)}), f32[4,672,128]{2,1,0:T(8,128)S(1)}, u32[]{:S(2)}, u32[]{:S(2)}) async-start(f32[4,672,128]{2,1,0:T(8,128)} %get-tuple-element.34), calls=%async_computation | async-start | bytes 2752512 | tf_op jit(solution)/shard_map/all_to_all | solution.py:500
  10.0 4.2 %collective-permute-start = (bf16[120,512]{1,0:T(8,128)(2,1)}, bf16[120,512]{1,0:T(8,128)(2,1)}, u32[]{:S(2)}, u32[]{:S(2)}) collective-permute-start(bf16[120,512]{1,0:T(8,128)(2,1)} %get-tuple-element.35), channel_id=1, source_target_pairs={{0,32},{32,64},{64,96},{96,0},{1,33},{33,65},{65,97},{97,1},{2,34}... | collective-permute-start | bytes 368648 | tf_op jit(solution)/shard_map/ppermute | solution.py:463
  14.2 5.7 %collective-permute-start.1 = (bf16[120,512]{1,0:T(8,128)(2,1)}, bf16[120,512]{1,0:T(8,128)(2,1)}, u32[]{:S(2)}, u32[]{:S(2)}) collective-permute-start(bf16[120,512]{1,0:T(8,128)(2,1)} %get-tuple-element.35), channel_id=1, source_target_pairs={{0,64},{32,96},{64,0},{96,32},{1,65},{33,97},{65,1},{97,33},{2,66}... | collective-permute-start | bytes 368648 | tf_op jit(solution)/shard_map/ppermute | solution.py:463
  19.9 5.0 %collective-permute-start.2 = (bf16[120,512]{1,0:T(8,128)(2,1)}, bf16[120,512]{1,0:T(8,128)(2,1)}, u32[]{:S(2)}, u32[]{:S(2)}) collective-permute-start(bf16[120,512]{1,0:T(8,128)(2,1)} %get-tuple-element.35), channel_id=1, source_target_pairs={{0,96},{32,0},{64,32},{96,64},{1,97},{33,1},{65,33},{97,65},{2,98}... | collective-permute-start | bytes 368648 | tf_op jit(solution)/shard_map/ppermute | solution.py:463
  24.9 1.2 shard_map.149
  26.2 1.0 shard_map.148
  27.2 5.6 %collective-permute-done.2 = bf16[120,512]{1,0:T(8,128)(2,1)} collective-permute-done((bf16[120,512]{1,0:T(8,128)(2,1)}, bf16[120,512]{1,0:T(8,128)(2,1)}, u32[]{:S(2)}, u32[]{:S(2)}) %collective-permute-start.2) | collective-permute-done | bytes 122912 | tf_op jit(solution)/shard_map/ppermute | solution.py:463
  32.8 5.6 %all-to-all-start.1 = ((f32[4,80,512]{2,1,0:T(8,128)}), f32[4,80,512]{2,1,0:T(8,128)S(1)}, u32[]{:S(2)}, u32[]{:S(2)}) async-start(f32[4,80,512]{2,1,0:T(8,128)} %shard_map.148), calls=%async_computation.1 | async-start | bytes 1310720 | tf_op jit(solution)/shard_map/all_to_all | solution.py:502
  38.4 3.4 %collective-permute-start.3 = (bf16[320,768]{1,0:T(8,128)(2,1)S(1)}, bf16[320,768]{1,0:T(8,128)(2,1)}, u32[]{:S(2)}, u32[]{:S(2)}) collective-permute-start(bf16[320,768]{1,0:T(8,128)(2,1)S(1)} %get-tuple-element.40), channel_id=1, source_target_pairs={{0,128},{128,256},{256,384},{384,0},{1,129},{129,257},{257,385},{3... | collective-permute-start | bytes 1474568 | tf_op jit(solution)/shard_map/ppermute | solution.py:463
  41.9 3.1 %collective-permute-start.4 = (bf16[320,768]{1,0:T(8,128)(2,1)S(1)}, bf16[320,768]{1,0:T(8,128)(2,1)}, u32[]{:S(2)}, u32[]{:S(2)}) collective-permute-start(bf16[320,768]{1,0:T(8,128)(2,1)S(1)} %get-tuple-element.41), channel_id=1, source_target_pairs={{0,384},{128,0},{256,128},{384,256},{1,385},{129,1},{257,129},{385... | collective-permute-start | bytes 1474568 | tf_op jit(solution)/shard_map/ppermute | solution.py:463
  45.0 3.2 %collective-permute-start.5 = (bf16[320,640]{1,0:T(8,128)(2,1)S(1)}, bf16[320,640]{1,0:T(8,128)(2,1)}, u32[]{:S(2)}, u32[]{:S(2)}) collective-permute-start(bf16[320,640]{1,0:T(8,128)(2,1)S(1)} %get-tuple-element.42.refs_0_), channel_id=1, source_target_pairs={{0,1},{1,0},{2,3},{3,2},{4,5},{5,4},{6,7},{7,6},{8,9},{9,8},{10,11... | collective-permute-start | bytes 1228808 | tf_op jit(solution)/shard_map/ppermute | solution.py:463
  48.2 0.7 collective-permute-start.6
  48.9 0.2 copy.16
  49.1 0.2 reshape.27
  49.3 6.1 %all-to-all-done.1.got_ref = f32[4,80,512]{2,1,0:T(8,128)S(1)} async-done(((f32[4,80,512]{2,1,0:T(8,128)}), f32[4,80,512]{2,1,0:T(8,128)S(1)}, u32[]{:S(2)}, u32[]{:S(2)}) %all-to-all-start.1) | async-done | bytes 655392 | tf_op jit(solution)/shard_map/all_to_all | solution.py:502
  55.4 2.5 %shard_map.150 = bf16[2,4,4,32,384]{4,3,2,1,0:T(8,128)(2,1)} custom-call(s32[1,2560]{1,0:T(1,128)S(1)} %reshape.28.ids_ref, f32[4,80,512]{2,1,0:T(8,128)S(1)} %all-to-all-done.1.got_ref), custom_call_target="tpu_custom_call" | custom-call | tf_op jit(solution)/shard_map/pallas_call | solution.py:269
  58.0 10.1 %all-to-all-start.2 = ((bf16[32,32,384]{2,1,0:T(8,128)(2,1)}), bf16[32,32,384]{2,1,0:T(8,128)(2,1)S(1)}, u32[]{:S(2)}, u32[]{:S(2)}) async-start(bf16[32,32,384]{2,1,0:T(8,128)(2,1)} %bitcast.11), calls=%async_computation.2 | async-start | bytes 1572864 | tf_op jit(solution)/shard_map/all_to_all | solution.py:515
  68.1 1.0 slice.6
  69.0 3.3 %collective-permute-start.7 = (bf16[160,768]{1,0:T(8,128)(2,1)S(1)}, bf16[160,768]{1,0:T(8,128)(2,1)S(1)}, u32[]{:S(2)}, u32[]{:S(2)}) collective-permute-start(bf16[160,768]{1,0:T(8,128)(2,1)S(1)} %slice.6), channel_id=1, source_target_pairs={{0,128},{128,256},{256,384},{384,0},{1,129},{129,257},{257,385},{3... | collective-permute-start | bytes 737288 | tf_op jit(solution)/shard_map/ppermute | solution.py:463
  72.3 1.0 slice.7
  73.3 3.2 %collective-permute-start.8 = (bf16[160,768]{1,0:T(8,128)(2,1)S(1)}, bf16[160,768]{1,0:T(8,128)(2,1)S(1)}, u32[]{:S(2)}, u32[]{:S(2)}) collective-permute-start(bf16[160,768]{1,0:T(8,128)(2,1)S(1)} %slice.7), channel_id=1, source_target_pairs={{0,384},{128,0},{256,128},{384,256},{1,385},{129,1},{257,129},{385... | collective-permute-start | bytes 737288 | tf_op jit(solution)/shard_map/ppermute | solution.py:463
  76.5 2.7 %collective-permute-start.9 = (bf16[320,768]{1,0:T(8,128)(2,1)}, bf16[320,768]{1,0:T(8,128)(2,1)S(1)}, u32[]{:S(2)}, u32[]{:S(2)}) collective-permute-start(bf16[320,768]{1,0:T(8,128)(2,1)} %collective-permute-done.3.refs_1_), channel_id=1, source_target_pairs={{0,1},{1,0},{2,3},{3,2},{4,5},{5,4},{6,7},{7,6},{8,9},{9,8},{10,11... | collective-permute-start | bytes 1474568 | tf_op jit(solution)/shard_map/ppermute | solution.py:463
  79.2 1.9 %collective-permute-start.12 = (bf16[320,768]{1,0:T(8,128)(2,1)}, bf16[320,768]{1,0:T(8,128)(2,1)S(1)}, u32[]{:S(2)}, u32[]{:S(2)}) collective-permute-start(bf16[320,768]{1,0:T(8,128)(2,1)} %collective-permute-done.4.refs_4_), channel_id=1, source_target_pairs={{0,1},{1,0},{2,3},{3,2},{4,5},{5,4},{6,7},{7,6},{8,9},{9,8},{10,11... | collective-permute-start | bytes 1474568 | tf_op jit(solution)/shard_map/ppermute | solution.py:463
  81.2 2.4 %collective-permute-start.10 = (bf16[160,768]{1,0:T(8,128)(2,1)S(1)}, bf16[160,768]{1,0:T(8,128)(2,1)S(1)}, u32[]{:S(2)}, u32[]{:S(2)}) collective-permute-start(bf16[160,768]{1,0:T(8,128)(2,1)S(1)} %collective-permute-done.7.refs_2_), channel_id=1, source_target_pairs={{0,1},{1,0},{2,3},{3,2},{4,5},{5,4},{6,7},{7,6},{8,9},{9,8},{10,11... | collective-permute-start | bytes 737288 | tf_op jit(solution)/shard_map/ppermute | solution.py:463
  83.6 3.4 %collective-permute-done.8.refs_3_ = bf16[160,768]{1,0:T(8,128)(2,1)S(1)} collective-permute-done((bf16[160,768]{1,0:T(8,128)(2,1)S(1)}, bf16[160,768]{1,0:T(8,128)(2,1)S(1)}, u32[]{:S(2)}, u32[]{:S(2)}) %collective-permute-start.8) | collective-permute-done | bytes 245792 | tf_op jit(solution)/shard_map/ppermute | solution.py:463
  87.0 3.2 %collective-permute-start.11 = (bf16[160,768]{1,0:T(8,128)(2,1)S(1)}, bf16[160,768]{1,0:T(8,128)(2,1)S(1)}, u32[]{:S(2)}, u32[]{:S(2)}) collective-permute-start(bf16[160,768]{1,0:T(8,128)(2,1)S(1)} %collective-permute-done.8.refs_3_), channel_id=1, source_target_pairs={{0,1},{1,0},{2,3},{3,2},{4,5},{5,4},{6,7},{7,6},{8,9},{9,8},{10,11... | collective-permute-start | bytes 737288 | tf_op jit(solution)/shard_map/ppermute | solution.py:463
  90.2 1.1 collective-permute-done.11.refs_8_
  91.4 0.6 copy-done.16
  92.2 0.2 copy-done.12
  92.3 0.3 copy-done.10
  92.6 5.1 %shard_map.151 = bf16[16,40,640]{2,1,0:T(8,128)(2,1)} custom-call(s32[4]{0:T(128)} %copy-done.7, bf16[1024,384]{1,0:T(8,128)(2,1)} %bitcast.33, bf16[320,640]{1,0:T(8,128)(2,1)} %copy-done.3, bf16[320,768]{1,0:T(8,128)(2,1)} %collective-permute-done.3.refs_1_, bf16[160,768]{1,0:T(8,128)(2,1)} %copy-done.13, bf16[160,768]{1,0:T(8,128)(2,1)} %copy-done.14, ...), custom_call_target="tpu_custom_call" | custom-call | tf_op jit(solution)/shard_map/pallas_call | solution.py:357
  97.7 11.1 %all-to-all-start.3 = ((bf16[16,40,640]{2,1,0:T(8,128)(2,1)}), bf16[16,40,640]{2,1,0:T(8,128)(2,1)S(1)}, u32[]{:S(2)}, u32[]{:S(2)}) async-start(bf16[16,40,640]{2,1,0:T(8,128)(2,1)} %shard_map.151), calls=%async_computation.3 | async-start | bytes 1638400 | tf_op jit(solution)/shard_map/all_to_all | solution.py:526
  108.9 1.1 pad_maximum_fusion
  110.1 3.2 %collective-permute-start.14 = (bf16[3,160,512]{2,1,0:T(8,128)(2,1)S(1)}, bf16[3,160,512]{2,1,0:T(8,128)(2,1)S(1)}, u32[]{:S(2)}, u32[]{:S(2)}) collective-permute-start(bf16[3,160,512]{2,1,0:T(8,128)(2,1)S(1)} %pad_maximum_fusion.1.refs_3_), channel_id=1, source_target_pairs={{0,128},{128,256},{256,384},{384,0},{1,129},{129,257},{257,385},{3... | collective-permute-start | bytes 1474568 | tf_op jit(solution)/shard_map/ppermute | solution.py:463
  113.3 3.7 %collective-permute-start.15 = (bf16[3,160,512]{2,1,0:T(8,128)(2,1)S(1)}, bf16[3,160,512]{2,1,0:T(8,128)(2,1)S(1)}, u32[]{:S(2)}, u32[]{:S(2)}) collective-permute-start(bf16[3,160,512]{2,1,0:T(8,128)(2,1)S(1)} %pad_maximum_fusion.1.refs_3_), channel_id=1, source_target_pairs={{0,256},{128,384},{256,0},{384,128},{1,257},{129,385},{257,1},{385... | collective-permute-start | bytes 1474568 | tf_op jit(solution)/shard_map/ppermute | solution.py:463
  117.0 3.4 %collective-permute-start.16 = (bf16[3,160,512]{2,1,0:T(8,128)(2,1)S(1)}, bf16[3,160,512]{2,1,0:T(8,128)(2,1)}, u32[]{:S(2)}, u32[]{:S(2)}) collective-permute-start(bf16[3,160,512]{2,1,0:T(8,128)(2,1)S(1)} %pad_maximum_fusion.1.refs_3_), channel_id=1, source_target_pairs={{0,384},{128,0},{256,128},{384,256},{1,385},{129,1},{257,129},{385... | collective-permute-start | bytes 1474568 | tf_op jit(solution)/shard_map/ppermute | solution.py:463
  120.5 9.8 %all-to-all-done.3.got_ref = bf16[16,40,640]{2,1,0:T(8,128)(2,1)S(1)} async-done(((bf16[16,40,640]{2,1,0:T(8,128)(2,1)}), bf16[16,40,640]{2,1,0:T(8,128)(2,1)S(1)}, u32[]{:S(2)}, u32[]{:S(2)}) %all-to-all-start.3) | async-done | bytes 819232 | tf_op jit(solution)/shard_map/all_to_all | solution.py:526
  130.3 0.8 copy-done.6
  131.1 0.8 shard_map.152
  131.9 0.6 copy-done.9
  132.5 12.9 %all_to_all.36 = f32[16,8,128]{2,1,0:T(8,128)S(1)} all-to-all(f32[16,8,128]{2,1,0:T(8,128)S(1)} %get-tuple-element.50), channel_id=1, replica_groups=mesh['x'=4,'yh'=4,'zh'=4,'zl'=2,'yl'=2,'c'=2] {'yh','zl','yl'}, dimensions={0} | all-to-all | bytes 131072 | tf_op jit(solution)/shard_map/all_to_all | solution.py:539
  145.5 0.7 broadcast_in_dim.3
  146.1 9.1 %all-to-all-start.5 = ((f32[32,8,128]{2,1,0:T(8,128)}), f32[32,8,128]{2,1,0:T(8,128)S(1)}, u32[]{:S(2)}, u32[]{:S(2)}) async-start(f32[32,8,128]{2,1,0:T(8,128)} %broadcast_in_dim.3), calls=%async_computation.5 | async-start | bytes 262144 | tf_op jit(solution)/shard_map/all_to_all | solution.py:542
  155.2 1.6 collective-permute-start.13
  156.8 9.4 %all-to-all-done.5.far_ref = f32[32,8,128]{2,1,0:T(8,128)S(1)} async-done(((f32[32,8,128]{2,1,0:T(8,128)}), f32[32,8,128]{2,1,0:T(8,128)S(1)}, u32[]{:S(2)}, u32[]{:S(2)}) %all-to-all-start.5) | async-done | bytes 131104 | tf_op jit(solution)/shard_map/all_to_all | solution.py:542
  166.2 4.8 %shard_map.153 = (f32[320,512]{1,0:T(8,128)}, f32[320,512]{1,0:T(8,128)}, f32[320,512]{1,0:T(8,128)}) custom-call(s32[4]{0:T(128)S(1)} %copy-done.8, f32[32,8,128]{2,1,0:T(8,128)S(1)} %all-to-all-done.5.far_ref, bf16[320,640]{1,0:T(8,128)(2,1)S(1)} %bitcast.27, bf16[320,640]{1,0:T(8,128)(2,1)S(1)} %bitcast.29, bf16[320,640]{1,0:T(8,128)(2,1)S(1)} %bitcast.31, ...), custom_call_target="tpu_custom_call" | custom-call | tf_op jit(solution)/shard_map/pallas_call | solution.py:445
  171.0 0.7 copy.19
  (55 shorter events, 0.6 us)
Async XLA Ops:
  5.0 20.0 %copy-start.2 = (bf16[640,320]{0,1:T(8,128)(2,1)S(1)}, bf16[640,320]{0,1:T(8,128)(2,1)}, u32[]{:S(2)}) copy-start(bf16[640,320]{0,1:T(8,128)(2,1)} %param.22) | copy-start | bytes 1228804
  5.0 20.0 %copy-start.4 = (bf16[512,320]{0,1:T(8,128)(2,1)S(1)}, bf16[512,320]{0,1:T(8,128)(2,1)}, u32[]{:S(2)}) copy-start(bf16[512,320]{0,1:T(8,128)(2,1)} %param.16) | copy-start | bytes 983044
  5.0 21.2 %all-to-all-start = ((f32[4,672,128]{2,1,0:T(8,128)}), f32[4,672,128]{2,1,0:T(8,128)S(1)}, u32[]{:S(2)}, u32[]{:S(2)}) async-start(f32[4,672,128]{2,1,0:T(8,128)} %get-tuple-element.34), calls=%async_computation | async-start | bytes 2752512 | tf_op jit(solution)/shard_map/all_to_all | solution.py:500
  10.0 17.2 %collective-permute-start = (bf16[120,512]{1,0:T(8,128)(2,1)}, bf16[120,512]{1,0:T(8,128)(2,1)}, u32[]{:S(2)}, u32[]{:S(2)}) collective-permute-start(bf16[120,512]{1,0:T(8,128)(2,1)} %get-tuple-element.35), channel_id=1, source_target_pairs={{0,32},{32,64},{64,96},{96,0},{1,33},{33,65},{65,97},{97,1},{2,34}... | collective-permute-start | bytes 368648 | tf_op jit(solution)/shard_map/ppermute | solution.py:463
  14.2 13.0 %collective-permute-start.1 = (bf16[120,512]{1,0:T(8,128)(2,1)}, bf16[120,512]{1,0:T(8,128)(2,1)}, u32[]{:S(2)}, u32[]{:S(2)}) collective-permute-start(bf16[120,512]{1,0:T(8,128)(2,1)} %get-tuple-element.35), channel_id=1, source_target_pairs={{0,64},{32,96},{64,0},{96,32},{1,65},{33,97},{65,1},{97,33},{2,66}... | collective-permute-start | bytes 368648 | tf_op jit(solution)/shard_map/ppermute | solution.py:463
  19.9 13.0 %collective-permute-start.2 = (bf16[120,512]{1,0:T(8,128)(2,1)}, bf16[120,512]{1,0:T(8,128)(2,1)}, u32[]{:S(2)}, u32[]{:S(2)}) collective-permute-start(bf16[120,512]{1,0:T(8,128)(2,1)} %get-tuple-element.35), channel_id=1, source_target_pairs={{0,96},{32,0},{64,32},{96,64},{1,97},{33,1},{65,33},{97,65},{2,98}... | collective-permute-start | bytes 368648 | tf_op jit(solution)/shard_map/ppermute | solution.py:463
  24.9 2.3 %copy-start.7 = (s32[4]{0:T(128)}, s32[4]{0:T(128)S(1)}, u32[]{:S(2)}) copy-start(s32[4]{0:T(128)S(1)} %pad_add_fusion.place_ref) | copy-start | bytes 52
  26.1 18.9 %copy-start.3 = (bf16[320,640]{1,0:T(8,128)(2,1)}, bf16[320,640]{1,0:T(8,128)(2,1)S(1)}, u32[]{:S(2)}) copy-start(bf16[320,640]{1,0:T(8,128)(2,1)S(1)} %get-tuple-element.42.refs_0_) | copy-start | bytes 1228804
  26.1 22.1 %copy-start.18 = (bf16[80,320]{1,0:T(8,128)(2,1)S(1)}, bf16[80,320]{1,0:T(8,128)(2,1)}, u32[]{:S(2)}) copy-start(bf16[80,320]{1,0:T(8,128)(2,1)} %param.23) | copy-start | bytes 153604
  26.1 22.7 %copy-start.17 = (s32[640,4]{0,1:T(4,128)S(1)}, s32[640,4]{0,1:T(4,128)}, u32[]{:S(2)}) copy-start(s32[640,4]{0,1:T(4,128)} %param.13) | copy-start | bytes 30724
  32.8 22.6 %all-to-all-start.1 = ((f32[4,80,512]{2,1,0:T(8,128)}), f32[4,80,512]{2,1,0:T(8,128)S(1)}, u32[]{:S(2)}, u32[]{:S(2)}) async-start(f32[4,80,512]{2,1,0:T(8,128)} %shard_map.148), calls=%async_computation.1 | async-start | bytes 1310720 | tf_op jit(solution)/shard_map/all_to_all | solution.py:502
  38.4 19.5 %collective-permute-start.3 = (bf16[320,768]{1,0:T(8,128)(2,1)S(1)}, bf16[320,768]{1,0:T(8,128)(2,1)}, u32[]{:S(2)}, u32[]{:S(2)}) collective-permute-start(bf16[320,768]{1,0:T(8,128)(2,1)S(1)} %get-tuple-element.40), channel_id=1, source_target_pairs={{0,128},{128,256},{256,384},{384,0},{1,129},{129,257},{257,385},{3... | collective-permute-start | bytes 1474568 | tf_op jit(solution)/shard_map/ppermute | solution.py:463
  41.9 16.1 %collective-permute-start.4 = (bf16[320,768]{1,0:T(8,128)(2,1)S(1)}, bf16[320,768]{1,0:T(8,128)(2,1)}, u32[]{:S(2)}, u32[]{:S(2)}) collective-permute-start(bf16[320,768]{1,0:T(8,128)(2,1)S(1)} %get-tuple-element.41), channel_id=1, source_target_pairs={{0,384},{128,0},{256,128},{384,256},{1,385},{129,1},{257,129},{385... | collective-permute-start | bytes 1474568 | tf_op jit(solution)/shard_map/ppermute | solution.py:463
  45.0 13.0 %collective-permute-start.5 = (bf16[320,640]{1,0:T(8,128)(2,1)S(1)}, bf16[320,640]{1,0:T(8,128)(2,1)}, u32[]{:S(2)}, u32[]{:S(2)}) collective-permute-start(bf16[320,640]{1,0:T(8,128)(2,1)S(1)} %get-tuple-element.42.refs_0_), channel_id=1, source_target_pairs={{0,1},{1,0},{2,3},{3,2},{4,5},{5,4},{6,7},{7,6},{8,9},{9,8},{10,11... | collective-permute-start | bytes 1228808 | tf_op jit(solution)/shard_map/ppermute | solution.py:463
  48.2 9.8 %collective-permute-start.6 = (bf16[80,320]{1,0:T(8,128)(2,1)S(1)}, bf16[80,320]{1,0:T(8,128)(2,1)S(1)}, u32[]{:S(2)}, u32[]{:S(2)}) collective-permute-start(bf16[80,320]{1,0:T(8,128)(2,1)S(1)} %copy-done.18), channel_id=1, source_target_pairs={{0,0},{1,1},{128,2},{129,3},{256,4},{257,5},{384,6},{385,7},{8,8},... | collective-permute-start | bytes 153608 | tf_op jit(solution)/shard_map/ppermute | solution.py:508
  58.0 39.7 %copy-start.5 = (bf16[80,320]{1,0:T(8,128)(2,1)}, bf16[80,320]{1,0:T(8,128)(2,1)S(1)}, u32[]{:S(2)}) copy-start(bf16[80,320]{1,0:T(8,128)(2,1)S(1)} %collective-permute-done.6.target_ref) | copy-start | bytes 153604
  58.0 33.4 %all-to-all-start.2 = ((bf16[32,32,384]{2,1,0:T(8,128)(2,1)}), bf16[32,32,384]{2,1,0:T(8,128)(2,1)S(1)}, u32[]{:S(2)}, u32[]{:S(2)}) async-start(bf16[32,32,384]{2,1,0:T(8,128)(2,1)} %bitcast.11), calls=%async_computation.2 | async-start | bytes 1572864 | tf_op jit(solution)/shard_map/all_to_all | solution.py:515
  69.0 12.1 %collective-permute-start.7 = (bf16[160,768]{1,0:T(8,128)(2,1)S(1)}, bf16[160,768]{1,0:T(8,128)(2,1)S(1)}, u32[]{:S(2)}, u32[]{:S(2)}) collective-permute-start(bf16[160,768]{1,0:T(8,128)(2,1)S(1)} %slice.6), channel_id=1, source_target_pairs={{0,128},{128,256},{256,384},{384,0},{1,129},{129,257},{257,385},{3... | collective-permute-start | bytes 737288 | tf_op jit(solution)/shard_map/ppermute | solution.py:463
  73.3 13.7 %collective-permute-start.8 = (bf16[160,768]{1,0:T(8,128)(2,1)S(1)}, bf16[160,768]{1,0:T(8,128)(2,1)S(1)}, u32[]{:S(2)}, u32[]{:S(2)}) collective-permute-start(bf16[160,768]{1,0:T(8,128)(2,1)S(1)} %slice.7), channel_id=1, source_target_pairs={{0,384},{128,0},{256,128},{384,256},{1,385},{129,1},{257,129},{385... | collective-permute-start | bytes 737288 | tf_op jit(solution)/shard_map/ppermute | solution.py:463
  76.5 14.8 %collective-permute-start.9 = (bf16[320,768]{1,0:T(8,128)(2,1)}, bf16[320,768]{1,0:T(8,128)(2,1)S(1)}, u32[]{:S(2)}, u32[]{:S(2)}) collective-permute-start(bf16[320,768]{1,0:T(8,128)(2,1)} %collective-permute-done.3.refs_1_), channel_id=1, source_target_pairs={{0,1},{1,0},{2,3},{3,2},{4,5},{5,4},{6,7},{7,6},{8,9},{9,8},{10,11... | collective-permute-start | bytes 1474568 | tf_op jit(solution)/shard_map/ppermute | solution.py:463
  79.2 12.1 %collective-permute-start.12 = (bf16[320,768]{1,0:T(8,128)(2,1)}, bf16[320,768]{1,0:T(8,128)(2,1)S(1)}, u32[]{:S(2)}, u32[]{:S(2)}) collective-permute-start(bf16[320,768]{1,0:T(8,128)(2,1)} %collective-permute-done.4.refs_4_), channel_id=1, source_target_pairs={{0,1},{1,0},{2,3},{3,2},{4,5},{5,4},{6,7},{7,6},{8,9},{9,8},{10,11... | collective-permute-start | bytes 1474568 | tf_op jit(solution)/shard_map/ppermute | solution.py:463
  81.1 10.2 %copy-start.13 = (bf16[160,768]{1,0:T(8,128)(2,1)}, bf16[160,768]{1,0:T(8,128)(2,1)S(1)}, u32[]{:S(2)}) copy-start(bf16[160,768]{1,0:T(8,128)(2,1)S(1)} %collective-permute-done.7.refs_2_) | copy-start | bytes 737284
  81.2 9.0 %collective-permute-start.10 = (bf16[160,768]{1,0:T(8,128)(2,1)S(1)}, bf16[160,768]{1,0:T(8,128)(2,1)S(1)}, u32[]{:S(2)}, u32[]{:S(2)}) collective-permute-start(bf16[160,768]{1,0:T(8,128)(2,1)S(1)} %collective-permute-done.7.refs_2_), channel_id=1, source_target_pairs={{0,1},{1,0},{2,3},{3,2},{4,5},{5,4},{6,7},{7,6},{8,9},{9,8},{10,11... | collective-permute-start | bytes 737288 | tf_op jit(solution)/shard_map/ppermute | solution.py:463
  87.0 4.4 %copy-start.14 = (bf16[160,768]{1,0:T(8,128)(2,1)}, bf16[160,768]{1,0:T(8,128)(2,1)S(1)}, u32[]{:S(2)}) copy-start(bf16[160,768]{1,0:T(8,128)(2,1)S(1)} %collective-permute-done.8.refs_3_) | copy-start | bytes 737284
  87.0 4.4 %collective-permute-start.11 = (bf16[160,768]{1,0:T(8,128)(2,1)S(1)}, bf16[160,768]{1,0:T(8,128)(2,1)S(1)}, u32[]{:S(2)}, u32[]{:S(2)}) collective-permute-start(bf16[160,768]{1,0:T(8,128)(2,1)S(1)} %collective-permute-done.8.refs_3_), channel_id=1, source_target_pairs={{0,1},{1,0},{2,3},{3,2},{4,5},{5,4},{6,7},{7,6},{8,9},{9,8},{10,11... | collective-permute-start | bytes 737288 | tf_op jit(solution)/shard_map/ppermute | solution.py:463
  90.2 1.2 copy-start.15
  91.3 0.7 copy-start.16
  91.3 0.9 copy-start.11
  91.3 1.0 copy-start.12
  91.4 1.3 copy-start.10
  97.7 32.5 %all-to-all-start.3 = ((bf16[16,40,640]{2,1,0:T(8,128)(2,1)}), bf16[16,40,640]{2,1,0:T(8,128)(2,1)S(1)}, u32[]{:S(2)}, u32[]{:S(2)}) async-start(bf16[16,40,640]{2,1,0:T(8,128)(2,1)} %shard_map.151), calls=%async_computation.3 | async-start | bytes 1638400 | tf_op jit(solution)/shard_map/all_to_all | solution.py:526
  108.8 21.4 %copy-start.8 = (s32[4]{0:T(128)S(1)}, s32[4]{0:T(128)}, u32[]{:S(2)}) copy-start(s32[4]{0:T(128)} %copy-done.7) | copy-start | bytes 52
  110.1 56.1 %copy-start = (bf16[640,320]{0,1:T(8,128)(2,1)S(1)}, bf16[640,320]{0,1:T(8,128)(2,1)}, u32[]{:S(2)}) copy-start(bf16[640,320]{0,1:T(8,128)(2,1)} %param.17) | copy-start | bytes 1228804
  110.1 56.1 %copy-start.1 = (bf16[640,320]{0,1:T(8,128)(2,1)S(1)}, bf16[640,320]{0,1:T(8,128)(2,1)}, u32[]{:S(2)}) copy-start(bf16[640,320]{0,1:T(8,128)(2,1)} %param.19) | copy-start | bytes 1228804
  110.1 35.3 %collective-permute-start.14 = (bf16[3,160,512]{2,1,0:T(8,128)(2,1)S(1)}, bf16[3,160,512]{2,1,0:T(8,128)(2,1)S(1)}, u32[]{:S(2)}, u32[]{:S(2)}) collective-permute-start(bf16[3,160,512]{2,1,0:T(8,128)(2,1)S(1)} %pad_maximum_fusion.1.refs_3_), channel_id=1, source_target_pairs={{0,128},{128,256},{256,384},{384,0},{1,129},{129,257},{257,385},{3... | collective-permute-start | bytes 1474568 | tf_op jit(solution)/shard_map/ppermute | solution.py:463
  113.3 32.1 %collective-permute-start.15 = (bf16[3,160,512]{2,1,0:T(8,128)(2,1)S(1)}, bf16[3,160,512]{2,1,0:T(8,128)(2,1)S(1)}, u32[]{:S(2)}, u32[]{:S(2)}) collective-permute-start(bf16[3,160,512]{2,1,0:T(8,128)(2,1)S(1)} %pad_maximum_fusion.1.refs_3_), channel_id=1, source_target_pairs={{0,256},{128,384},{256,0},{384,128},{1,257},{129,385},{257,1},{385... | collective-permute-start | bytes 1474568 | tf_op jit(solution)/shard_map/ppermute | solution.py:463
  117.0 28.4 %collective-permute-start.16 = (bf16[3,160,512]{2,1,0:T(8,128)(2,1)S(1)}, bf16[3,160,512]{2,1,0:T(8,128)(2,1)}, u32[]{:S(2)}, u32[]{:S(2)}) collective-permute-start(bf16[3,160,512]{2,1,0:T(8,128)(2,1)S(1)} %pad_maximum_fusion.1.refs_3_), channel_id=1, source_target_pairs={{0,384},{128,0},{256,128},{384,256},{1,385},{129,1},{257,129},{385... | collective-permute-start | bytes 1474568 | tf_op jit(solution)/shard_map/ppermute | solution.py:463
  130.3 0.8 copy-start.6
  131.9 0.7 copy-start.9
  146.1 20.0 %all-to-all-start.5 = ((f32[32,8,128]{2,1,0:T(8,128)}), f32[32,8,128]{2,1,0:T(8,128)S(1)}, u32[]{:S(2)}, u32[]{:S(2)}) async-start(f32[32,8,128]{2,1,0:T(8,128)} %broadcast_in_dim.3), calls=%async_computation.5 | async-start | bytes 262144 | tf_op jit(solution)/shard_map/all_to_all | solution.py:542
  155.2 1.6 collective-permute-start.13

commit v5 on v4

--- a/solution.py
+++ b/solution.py
@@ -365,12 +365,17 @@
     )(place, hidden, *own, *other)
 
 
-def loss_kernel(place_ref, got_ref, target_ref, raw_ref, out_ref):
+def loss_kernel(place_ref, got_ref, target_hbm, raw_hbm, out_ref, target_ref, raw_ref, moved):
+    arriving = pltpu.make_async_copy(target_hbm, target_ref, moved.at[0])
+    arriving.start()
     total = got_ref[0].astype(f32)
     for source in range(1, NZH * NX):
         total += got_ref[source].astype(f32)
     raw = jnp.concatenate([total[:, :WIDTH], total[:, WIDTH:]], axis=0)
     raw_ref[...] = raw
+    leaving = pltpu.make_async_copy(raw_ref, raw_hbm, moved.at[1])
+    leaving.start()
+    arriving.wait()
     error = raw - target_ref[...].astype(f32)
     squares = jnp.sum(error * error, axis=1, keepdims=True)
     member = (
@@ -385,6 +390,7 @@
         placed = jnp.where(line == k, here, placed)
     for k in range(NYH * NZL * NYL):
         out_ref[k] = placed
+    leaving.wait()
 
 
 def piece_losses(place, got, target):
@@ -394,7 +400,13 @@
             jax.ShapeDtypeStruct((BLOCK, WIDTH), f32),
             jax.ShapeDtypeStruct((NYH * NZL * NYL, 8, CHUNK), f32),
         ],
-        in_specs=[SMEM] + [VMEM] * 2,
+        in_specs=[SMEM, VMEM, HBM],
+        out_specs=[HBM, VMEM],
+        scratch_shapes=[
+            pltpu.VMEM((BLOCK, WIDTH), bf16),
+            pltpu.VMEM((BLOCK, WIDTH), f32),
+            pltpu.SemaphoreType.DMA((2,)),
+        ],
         compiler_params=PARAMS,
     )(place, got, target)
 

time: 173 us -> 174 us (level)
  no operation moved by 1% of the time
where the time goes in v5:
time: 174 us; the launch traced here: 172 us
  starting transfers between devices  94.8 us (54%)
  waiting for transfers between devices  35.3 us (20%)
  Pallas kernels  20 us (11%)
  blocking collectives  12.9 us (7%)
  local copies, waits for them, and re-layouts  6.49 us (4%)
    ppermute x15, starting transfers between devices, shifted(): return lax.ppermute(value, axis, [(i, (i + k) % size) for i in range(size)])  51.7 us
    all_to_all x1, blocking collectives, per_device(): near = lax.all_to_all(sent, ('yh', 'zl', 'yl'), 0, 0)  12.9 us
    all_to_all x1, starting transfers between devices, per_device(): got = lax.all_to_all(pieces, ('zh', 'zl', 'yl'), 0, 0)  11.1 us
    ppermute x15, waiting for transfers between devices, shifted(): return lax.ppermute(value, axis, [(i, (i + k) % size) for i in range(size)])  10.1 us
    all_to_all x1, starting transfers between devices, per_device(): lax.all_to_all(outgoing.reshape(NC * NX * NYH * OWN, PADDED), ('c', 'x',...  10.1 us
    all_to_all x1, waiting for transfers between devices, per_device(): got = lax.all_to_all(pieces, ('zh', 'zl', 'yl'), 0, 0)  9.75 us
    all_to_all x1, waiting for transfers between devices, per_device(): far = lax.all_to_all(near, ('x', 'c', 'zh'), 0, 0)  9.37 us
    all_to_all x1, starting transfers between devices, per_device(): far = lax.all_to_all(near, ('x', 'c', 'zh'), 0, 0)  9.1 us
  transfers between devices with their start and end apart: 22, of which 6 were waited for; matrix products, arithmetic and copies ran while one was open for 2% of the time, Pallas kernels for 3%

profile of v5, /device:TPU:1, one launch (start us, length us, event | category | flops | bytes accessed | tf_op | source)
XLA Modules:
  0.0 171.9 jit_solution(12099482478857247304)
XLA Ops:
  0.6 4.3 %shard_map.147 = (f32[4,672,128]{2,1,0:T(8,128)}, bf16[120,512]{1,0:T(8,128)(2,1)}) custom-call(s32[4,640]{1,0:T(4,128)} %bitcast.36, bf16[320,256]{1,0:T(8,128)(2,1)} %bitcast.34, bf16[320,640]{1,0:T(8,128)(2,1)} %bitcast.26, bf16[320,640]{1,0:T(8,128)(2,1)} %bitcast.28, bf16[320,512]{1,0:T(8,128)(2,1)} %refs_4_.1, bf16[320,512]{1,0:T(8,128)(2,1)} %refs_5_.1, ...), custom_call_target="tpu_custom_call" | custom-call | tf_op jit(solution)/shard_map/pallas_call | solution.py:119
  5.0 5.0 %all-to-all-start = ((f32[4,672,128]{2,1,0:T(8,128)}), f32[4,672,128]{2,1,0:T(8,128)S(1)}, u32[]{:S(2)}, u32[]{:S(2)}) async-start(f32[4,672,128]{2,1,0:T(8,128)} %get-tuple-element.34), calls=%async_computation | async-start | bytes 2752512 | tf_op jit(solution)/shard_map/all_to_all | solution.py:512
  10.0 4.2 %collective-permute-start = (bf16[120,512]{1,0:T(8,128)(2,1)}, bf16[120,512]{1,0:T(8,128)(2,1)}, u32[]{:S(2)}, u32[]{:S(2)}) collective-permute-start(bf16[120,512]{1,0:T(8,128)(2,1)} %get-tuple-element.35), channel_id=1, source_target_pairs={{0,32},{32,64},{64,96},{96,0},{1,33},{33,65},{65,97},{97,1},{2,34}... | collective-permute-start | bytes 368648 | tf_op jit(solution)/shard_map/ppermute | solution.py:475
  14.2 5.7 %collective-permute-start.1 = (bf16[120,512]{1,0:T(8,128)(2,1)}, bf16[120,512]{1,0:T(8,128)(2,1)}, u32[]{:S(2)}, u32[]{:S(2)}) collective-permute-start(bf16[120,512]{1,0:T(8,128)(2,1)} %get-tuple-element.35), channel_id=1, source_target_pairs={{0,64},{32,96},{64,0},{96,32},{1,65},{33,97},{65,1},{97,33},{2,66}... | collective-permute-start | bytes 368648 | tf_op jit(solution)/shard_map/ppermute | solution.py:475
  19.9 5.0 %collective-permute-start.2 = (bf16[120,512]{1,0:T(8,128)(2,1)}, bf16[120,512]{1,0:T(8,128)(2,1)}, u32[]{:S(2)}, u32[]{:S(2)}) collective-permute-start(bf16[120,512]{1,0:T(8,128)(2,1)} %get-tuple-element.35), channel_id=1, source_target_pairs={{0,96},{32,0},{64,32},{96,64},{1,97},{33,1},{65,33},{97,65},{2,98}... | collective-permute-start | bytes 368648 | tf_op jit(solution)/shard_map/ppermute | solution.py:475
  24.9 1.2 shard_map.149
  26.2 1.0 shard_map.148
  27.2 5.6 %collective-permute-done.2 = bf16[120,512]{1,0:T(8,128)(2,1)} collective-permute-done((bf16[120,512]{1,0:T(8,128)(2,1)}, bf16[120,512]{1,0:T(8,128)(2,1)}, u32[]{:S(2)}, u32[]{:S(2)}) %collective-permute-start.2) | collective-permute-done | bytes 122912 | tf_op jit(solution)/shard_map/ppermute | solution.py:475
  32.8 5.6 %all-to-all-start.1 = ((f32[4,80,512]{2,1,0:T(8,128)}), f32[4,80,512]{2,1,0:T(8,128)S(1)}, u32[]{:S(2)}, u32[]{:S(2)}) async-start(f32[4,80,512]{2,1,0:T(8,128)} %shard_map.148), calls=%async_computation.1 | async-start | bytes 1310720 | tf_op jit(solution)/shard_map/all_to_all | solution.py:514
  38.4 3.4 %collective-permute-start.3 = (bf16[320,768]{1,0:T(8,128)(2,1)S(1)}, bf16[320,768]{1,0:T(8,128)(2,1)}, u32[]{:S(2)}, u32[]{:S(2)}) collective-permute-start(bf16[320,768]{1,0:T(8,128)(2,1)S(1)} %get-tuple-element.40), channel_id=1, source_target_pairs={{0,128},{128,256},{256,384},{384,0},{1,129},{129,257},{257,385},{3... | collective-permute-start | bytes 1474568 | tf_op jit(solution)/shard_map/ppermute | solution.py:475
  41.9 3.1 %collective-permute-start.4 = (bf16[320,768]{1,0:T(8,128)(2,1)S(1)}, bf16[320,768]{1,0:T(8,128)(2,1)}, u32[]{:S(2)}, u32[]{:S(2)}) collective-permute-start(bf16[320,768]{1,0:T(8,128)(2,1)S(1)} %get-tuple-element.41), channel_id=1, source_target_pairs={{0,384},{128,0},{256,128},{384,256},{1,385},{129,1},{257,129},{385... | collective-permute-start | bytes 1474568 | tf_op jit(solution)/shard_map/ppermute | solution.py:475
  45.0 3.2 %collective-permute-start.5 = (bf16[320,640]{1,0:T(8,128)(2,1)S(1)}, bf16[320,640]{1,0:T(8,128)(2,1)}, u32[]{:S(2)}, u32[]{:S(2)}) collective-permute-start(bf16[320,640]{1,0:T(8,128)(2,1)S(1)} %get-tuple-element.42.refs_0_), channel_id=1, source_target_pairs={{0,1},{1,0},{2,3},{3,2},{4,5},{5,4},{6,7},{7,6},{8,9},{9,8},{10,11... | collective-permute-start | bytes 1228808 | tf_op jit(solution)/shard_map/ppermute | solution.py:475
  48.2 0.7 collective-permute-start.6
  48.9 0.2 copy.16
  49.1 0.2 reshape.27
  49.3 6.1 %all-to-all-done.1.got_ref = f32[4,80,512]{2,1,0:T(8,128)S(1)} async-done(((f32[4,80,512]{2,1,0:T(8,128)}), f32[4,80,512]{2,1,0:T(8,128)S(1)}, u32[]{:S(2)}, u32[]{:S(2)}) %all-to-all-start.1) | async-done | bytes 655392 | tf_op jit(solution)/shard_map/all_to_all | solution.py:514
  55.4 2.5 %shard_map.150 = bf16[2,4,4,32,384]{4,3,2,1,0:T(8,128)(2,1)} custom-call(s32[1,2560]{1,0:T(1,128)S(1)} %reshape.28.ids_ref, f32[4,80,512]{2,1,0:T(8,128)S(1)} %all-to-all-done.1.got_ref), custom_call_target="tpu_custom_call" | custom-call | tf_op jit(solution)/shard_map/pallas_call | solution.py:269
  58.0 10.1 %all-to-all-start.2 = ((bf16[32,32,384]{2,1,0:T(8,128)(2,1)}), bf16[32,32,384]{2,1,0:T(8,128)(2,1)S(1)}, u32[]{:S(2)}, u32[]{:S(2)}) async-start(bf16[32,32,384]{2,1,0:T(8,128)(2,1)} %bitcast.11), calls=%async_computation.2 | async-start | bytes 1572864 | tf_op jit(solution)/shard_map/all_to_all | solution.py:527
  68.1 1.0 slice.6
  69.0 3.3 %collective-permute-start.7 = (bf16[160,768]{1,0:T(8,128)(2,1)S(1)}, bf16[160,768]{1,0:T(8,128)(2,1)S(1)}, u32[]{:S(2)}, u32[]{:S(2)}) collective-permute-start(bf16[160,768]{1,0:T(8,128)(2,1)S(1)} %slice.6), channel_id=1, source_target_pairs={{0,128},{128,256},{256,384},{384,0},{1,129},{129,257},{257,385},{3... | collective-permute-start | bytes 737288 | tf_op jit(solution)/shard_map/ppermute | solution.py:475
  72.3 1.0 slice.7
  73.3 3.2 %collective-permute-start.8 = (bf16[160,768]{1,0:T(8,128)(2,1)S(1)}, bf16[160,768]{1,0:T(8,128)(2,1)S(1)}, u32[]{:S(2)}, u32[]{:S(2)}) collective-permute-start(bf16[160,768]{1,0:T(8,128)(2,1)S(1)} %slice.7), channel_id=1, source_target_pairs={{0,384},{128,0},{256,128},{384,256},{1,385},{129,1},{257,129},{385... | collective-permute-start | bytes 737288 | tf_op jit(solution)/shard_map/ppermute | solution.py:475
  76.5 2.7 %collective-permute-start.9 = (bf16[320,768]{1,0:T(8,128)(2,1)}, bf16[320,768]{1,0:T(8,128)(2,1)S(1)}, u32[]{:S(2)}, u32[]{:S(2)}) collective-permute-start(bf16[320,768]{1,0:T(8,128)(2,1)} %collective-permute-done.3.refs_1_), channel_id=1, source_target_pairs={{0,1},{1,0},{2,3},{3,2},{4,5},{5,4},{6,7},{7,6},{8,9},{9,8},{10,11... | collective-permute-start | bytes 1474568 | tf_op jit(solution)/shard_map/ppermute | solution.py:475
  79.2 1.9 %collective-permute-start.12 = (bf16[320,768]{1,0:T(8,128)(2,1)}, bf16[320,768]{1,0:T(8,128)(2,1)S(1)}, u32[]{:S(2)}, u32[]{:S(2)}) collective-permute-start(bf16[320,768]{1,0:T(8,128)(2,1)} %collective-permute-done.4.refs_4_), channel_id=1, source_target_pairs={{0,1},{1,0},{2,3},{3,2},{4,5},{5,4},{6,7},{7,6},{8,9},{9,8},{10,11... | collective-permute-start | bytes 1474568 | tf_op jit(solution)/shard_map/ppermute | solution.py:475
  81.2 2.4 %collective-permute-start.10 = (bf16[160,768]{1,0:T(8,128)(2,1)S(1)}, bf16[160,768]{1,0:T(8,128)(2,1)S(1)}, u32[]{:S(2)}, u32[]{:S(2)}) collective-permute-start(bf16[160,768]{1,0:T(8,128)(2,1)S(1)} %collective-permute-done.7.refs_2_), channel_id=1, source_target_pairs={{0,1},{1,0},{2,3},{3,2},{4,5},{5,4},{6,7},{7,6},{8,9},{9,8},{10,11... | collective-permute-start | bytes 737288 | tf_op jit(solution)/shard_map/ppermute | solution.py:475
  83.6 3.4 %collective-permute-done.8.refs_3_ = bf16[160,768]{1,0:T(8,128)(2,1)S(1)} collective-permute-done((bf16[160,768]{1,0:T(8,128)(2,1)S(1)}, bf16[160,768]{1,0:T(8,128)(2,1)S(1)}, u32[]{:S(2)}, u32[]{:S(2)}) %collective-permute-start.8) | collective-permute-done | bytes 245792 | tf_op jit(solution)/shard_map/ppermute | solution.py:475
  87.0 3.2 %collective-permute-start.11 = (bf16[160,768]{1,0:T(8,128)(2,1)S(1)}, bf16[160,768]{1,0:T(8,128)(2,1)S(1)}, u32[]{:S(2)}, u32[]{:S(2)}) collective-permute-start(bf16[160,768]{1,0:T(8,128)(2,1)S(1)} %collective-permute-done.8.refs_3_), channel_id=1, source_target_pairs={{0,1},{1,0},{2,3},{3,2},{4,5},{5,4},{6,7},{7,6},{8,9},{9,8},{10,11... | collective-permute-start | bytes 737288 | tf_op jit(solution)/shard_map/ppermute | solution.py:475
  90.2 1.1 collective-permute-done.11.refs_8_
  91.4 0.6 copy-done.16
  92.2 0.2 copy-done.12
  92.3 0.3 copy-done.10
  92.6 5.1 %shard_map.151 = bf16[16,40,640]{2,1,0:T(8,128)(2,1)} custom-call(s32[4]{0:T(128)} %copy-done.7, bf16[1024,384]{1,0:T(8,128)(2,1)} %bitcast.33, bf16[320,640]{1,0:T(8,128)(2,1)} %copy-done.3, bf16[320,768]{1,0:T(8,128)(2,1)} %collective-permute-done.3.refs_1_, bf16[160,768]{1,0:T(8,128)(2,1)} %copy-done.13, bf16[160,768]{1,0:T(8,128)(2,1)} %copy-done.14, ...), custom_call_target="tpu_custom_call" | custom-call | tf_op jit(solution)/shard_map/pallas_call | solution.py:357
  97.7 11.1 %all-to-all-start.3 = ((bf16[16,40,640]{2,1,0:T(8,128)(2,1)}), bf16[16,40,640]{2,1,0:T(8,128)(2,1)S(1)}, u32[]{:S(2)}, u32[]{:S(2)}) async-start(bf16[16,40,640]{2,1,0:T(8,128)(2,1)} %shard_map.151), calls=%async_computation.3 | async-start | bytes 1638400 | tf_op jit(solution)/shard_map/all_to_all | solution.py:538
  108.9 1.1 pad_maximum_fusion
  110.1 3.2 %collective-permute-start.14 = (bf16[3,160,512]{2,1,0:T(8,128)(2,1)S(1)}, bf16[3,160,512]{2,1,0:T(8,128)(2,1)S(1)}, u32[]{:S(2)}, u32[]{:S(2)}) collective-permute-start(bf16[3,160,512]{2,1,0:T(8,128)(2,1)S(1)} %pad_maximum_fusion.1.refs_3_), channel_id=1, source_target_pairs={{0,128},{128,256},{256,384},{384,0},{1,129},{129,257},{257,385},{3... | collective-permute-start | bytes 1474568 | tf_op jit(solution)/shard_map/ppermute | solution.py:475
  113.3 3.7 %collective-permute-start.15 = (bf16[3,160,512]{2,1,0:T(8,128)(2,1)S(1)}, bf16[3,160,512]{2,1,0:T(8,128)(2,1)S(1)}, u32[]{:S(2)}, u32[]{:S(2)}) collective-permute-start(bf16[3,160,512]{2,1,0:T(8,128)(2,1)S(1)} %pad_maximum_fusion.1.refs_3_), channel_id=1, source_target_pairs={{0,256},{128,384},{256,0},{384,128},{1,257},{129,385},{257,1},{385... | collective-permute-start | bytes 1474568 | tf_op jit(solution)/shard_map/ppermute | solution.py:475
  117.0 3.4 %collective-permute-start.16 = (bf16[3,160,512]{2,1,0:T(8,128)(2,1)S(1)}, bf16[3,160,512]{2,1,0:T(8,128)(2,1)}, u32[]{:S(2)}, u32[]{:S(2)}) collective-permute-start(bf16[3,160,512]{2,1,0:T(8,128)(2,1)S(1)} %pad_maximum_fusion.1.refs_3_), channel_id=1, source_target_pairs={{0,384},{128,0},{256,128},{384,256},{1,385},{129,1},{257,129},{385... | collective-permute-start | bytes 1474568 | tf_op jit(solution)/shard_map/ppermute | solution.py:475
  120.5 9.8 %all-to-all-done.3.got_ref = bf16[16,40,640]{2,1,0:T(8,128)(2,1)S(1)} async-done(((bf16[16,40,640]{2,1,0:T(8,128)(2,1)}), bf16[16,40,640]{2,1,0:T(8,128)(2,1)S(1)}, u32[]{:S(2)}, u32[]{:S(2)}) %all-to-all-start.3) | async-done | bytes 819232 | tf_op jit(solution)/shard_map/all_to_all | solution.py:538
  130.3 0.8 copy-done.6
  131.1 1.0 shard_map.152
  132.1 0.6 copy-done.9
  132.8 12.9 %all_to_all.36 = f32[16,8,128]{2,1,0:T(8,128)S(1)} all-to-all(f32[16,8,128]{2,1,0:T(8,128)S(1)} %get-tuple-element.50), channel_id=1, replica_groups=mesh['x'=4,'yh'=4,'zh'=4,'zl'=2,'yl'=2,'c'=2] {'yh','zl','yl'}, dimensions={0} | all-to-all | bytes 131072 | tf_op jit(solution)/shard_map/all_to_all | solution.py:551
  145.7 0.7 broadcast_in_dim.3
  146.4 9.1 %all-to-all-start.5 = ((f32[32,8,128]{2,1,0:T(8,128)}), f32[32,8,128]{2,1,0:T(8,128)S(1)}, u32[]{:S(2)}, u32[]{:S(2)}) async-start(f32[32,8,128]{2,1,0:T(8,128)} %broadcast_in_dim.3), calls=%async_computation.5 | async-start | bytes 262144 | tf_op jit(solution)/shard_map/all_to_all | solution.py:554
  155.5 1.6 collective-permute-start.13
  157.1 9.4 %all-to-all-done.5.far_ref = f32[32,8,128]{2,1,0:T(8,128)S(1)} async-done(((f32[32,8,128]{2,1,0:T(8,128)}), f32[32,8,128]{2,1,0:T(8,128)S(1)}, u32[]{:S(2)}, u32[]{:S(2)}) %all-to-all-start.5) | async-done | bytes 131104 | tf_op jit(solution)/shard_map/all_to_all | solution.py:554
  166.4 4.8 %shard_map.153 = (f32[320,512]{1,0:T(8,128)}, f32[320,512]{1,0:T(8,128)}, f32[320,512]{1,0:T(8,128)}) custom-call(s32[4]{0:T(128)S(1)} %copy-done.8, f32[32,8,128]{2,1,0:T(8,128)S(1)} %all-to-all-done.5.far_ref, bf16[320,640]{1,0:T(8,128)(2,1)S(1)} %bitcast.27, bf16[320,640]{1,0:T(8,128)(2,1)S(1)} %bitcast.29, bf16[320,640]{1,0:T(8,128)(2,1)S(1)} %bitcast.31, ...), custom_call_target="tpu_custom_call" | custom-call | tf_op jit(solution)/shard_map/pallas_call | solution.py:457
  171.2 0.7 copy.19
  (55 shorter events, 0.6 us)
Async XLA Ops:
  5.0 20.0 %copy-start.2 = (bf16[640,320]{0,1:T(8,128)(2,1)S(1)}, bf16[640,320]{0,1:T(8,128)(2,1)}, u32[]{:S(2)}) copy-start(bf16[640,320]{0,1:T(8,128)(2,1)} %param.22) | copy-start | bytes 1228804
  5.0 20.0 %copy-start.4 = (bf16[512,320]{0,1:T(8,128)(2,1)S(1)}, bf16[512,320]{0,1:T(8,128)(2,1)}, u32[]{:S(2)}) copy-start(bf16[512,320]{0,1:T(8,128)(2,1)} %param.16) | copy-start | bytes 983044
  5.0 21.2 %all-to-all-start = ((f32[4,672,128]{2,1,0:T(8,128)}), f32[4,672,128]{2,1,0:T(8,128)S(1)}, u32[]{:S(2)}, u32[]{:S(2)}) async-start(f32[4,672,128]{2,1,0:T(8,128)} %get-tuple-element.34), calls=%async_computation | async-start | bytes 2752512 | tf_op jit(solution)/shard_map/all_to_all | solution.py:512
  10.0 17.2 %collective-permute-start = (bf16[120,512]{1,0:T(8,128)(2,1)}, bf16[120,512]{1,0:T(8,128)(2,1)}, u32[]{:S(2)}, u32[]{:S(2)}) collective-permute-start(bf16[120,512]{1,0:T(8,128)(2,1)} %get-tuple-element.35), channel_id=1, source_target_pairs={{0,32},{32,64},{64,96},{96,0},{1,33},{33,65},{65,97},{97,1},{2,34}... | collective-permute-start | bytes 368648 | tf_op jit(solution)/shard_map/ppermute | solution.py:475
  14.2 13.0 %collective-permute-start.1 = (bf16[120,512]{1,0:T(8,128)(2,1)}, bf16[120,512]{1,0:T(8,128)(2,1)}, u32[]{:S(2)}, u32[]{:S(2)}) collective-permute-start(bf16[120,512]{1,0:T(8,128)(2,1)} %get-tuple-element.35), channel_id=1, source_target_pairs={{0,64},{32,96},{64,0},{96,32},{1,65},{33,97},{65,1},{97,33},{2,66}... | collective-permute-start | bytes 368648 | tf_op jit(solution)/shard_map/ppermute | solution.py:475
  19.9 13.0 %collective-permute-start.2 = (bf16[120,512]{1,0:T(8,128)(2,1)}, bf16[120,512]{1,0:T(8,128)(2,1)}, u32[]{:S(2)}, u32[]{:S(2)}) collective-permute-start(bf16[120,512]{1,0:T(8,128)(2,1)} %get-tuple-element.35), channel_id=1, source_target_pairs={{0,96},{32,0},{64,32},{96,64},{1,97},{33,1},{65,33},{97,65},{2,98}... | collective-permute-start | bytes 368648 | tf_op jit(solution)/shard_map/ppermute | solution.py:475
  24.9 2.3 %copy-start.7 = (s32[4]{0:T(128)}, s32[4]{0:T(128)S(1)}, u32[]{:S(2)}) copy-start(s32[4]{0:T(128)S(1)} %pad_add_fusion.place_ref) | copy-start | bytes 52
  26.1 18.9 %copy-start.3 = (bf16[320,640]{1,0:T(8,128)(2,1)}, bf16[320,640]{1,0:T(8,128)(2,1)S(1)}, u32[]{:S(2)}) copy-start(bf16[320,640]{1,0:T(8,128)(2,1)S(1)} %get-tuple-element.42.refs_0_) | copy-start | bytes 1228804
  26.1 22.1 %copy-start.18 = (bf16[80,320]{1,0:T(8,128)(2,1)S(1)}, bf16[80,320]{1,0:T(8,128)(2,1)}, u32[]{:S(2)}) copy-start(bf16[80,320]{1,0:T(8,128)(2,1)} %param.23) | copy-start | bytes 153604
  26.1 22.7 %copy-start.17 = (s32[640,4]{0,1:T(4,128)S(1)}, s32[640,4]{0,1:T(4,128)}, u32[]{:S(2)}) copy-start(s32[640,4]{0,1:T(4,128)} %param.13) | copy-start | bytes 30724
  32.8 22.6 %all-to-all-start.1 = ((f32[4,80,512]{2,1,0:T(8,128)}), f32[4,80,512]{2,1,0:T(8,128)S(1)}, u32[]{:S(2)}, u32[]{:S(2)}) async-start(f32[4,80,512]{2,1,0:T(8,128)} %shard_map.148), calls=%async_computation.1 | async-start | bytes 1310720 | tf_op jit(solution)/shard_map/all_to_all | solution.py:514
  38.4 19.5 %collective-permute-start.3 = (bf16[320,768]{1,0:T(8,128)(2,1)S(1)}, bf16[320,768]{1,0:T(8,128)(2,1)}, u32[]{:S(2)}, u32[]{:S(2)}) collective-permute-start(bf16[320,768]{1,0:T(8,128)(2,1)S(1)} %get-tuple-element.40), channel_id=1, source_target_pairs={{0,128},{128,256},{256,384},{384,0},{1,129},{129,257},{257,385},{3... | collective-permute-start | bytes 1474568 | tf_op jit(solution)/shard_map/ppermute | solution.py:475
  41.9 16.1 %collective-permute-start.4 = (bf16[320,768]{1,0:T(8,128)(2,1)S(1)}, bf16[320,768]{1,0:T(8,128)(2,1)}, u32[]{:S(2)}, u32[]{:S(2)}) collective-permute-start(bf16[320,768]{1,0:T(8,128)(2,1)S(1)} %get-tuple-element.41), channel_id=1, source_target_pairs={{0,384},{128,0},{256,128},{384,256},{1,385},{129,1},{257,129},{385... | collective-permute-start | bytes 1474568 | tf_op jit(solution)/shard_map/ppermute | solution.py:475
  45.0 13.0 %collective-permute-start.5 = (bf16[320,640]{1,0:T(8,128)(2,1)S(1)}, bf16[320,640]{1,0:T(8,128)(2,1)}, u32[]{:S(2)}, u32[]{:S(2)}) collective-permute-start(bf16[320,640]{1,0:T(8,128)(2,1)S(1)} %get-tuple-element.42.refs_0_), channel_id=1, source_target_pairs={{0,1},{1,0},{2,3},{3,2},{4,5},{5,4},{6,7},{7,6},{8,9},{9,8},{10,11... | collective-permute-start | bytes 1228808 | tf_op jit(solution)/shard_map/ppermute | solution.py:475
  48.2 9.8 %collective-permute-start.6 = (bf16[80,320]{1,0:T(8,128)(2,1)S(1)}, bf16[80,320]{1,0:T(8,128)(2,1)S(1)}, u32[]{:S(2)}, u32[]{:S(2)}) collective-permute-start(bf16[80,320]{1,0:T(8,128)(2,1)S(1)} %copy-done.18), channel_id=1, source_target_pairs={{0,0},{1,1},{128,2},{129,3},{256,4},{257,5},{384,6},{385,7},{8,8},... | collective-permute-start | bytes 153608 | tf_op jit(solution)/shard_map/ppermute | solution.py:520
  58.0 39.7 %copy-start.5 = (bf16[80,320]{1,0:T(8,128)(2,1)}, bf16[80,320]{1,0:T(8,128)(2,1)S(1)}, u32[]{:S(2)}) copy-start(bf16[80,320]{1,0:T(8,128)(2,1)S(1)} %collective-permute-done.6.target_hbm) | copy-start | bytes 153604
  58.0 33.4 %all-to-all-start.2 = ((bf16[32,32,384]{2,1,0:T(8,128)(2,1)}), bf16[32,32,384]{2,1,0:T(8,128)(2,1)S(1)}, u32[]{:S(2)}, u32[]{:S(2)}) async-start(bf16[32,32,384]{2,1,0:T(8,128)(2,1)} %bitcast.11), calls=%async_computation.2 | async-start | bytes 1572864 | tf_op jit(solution)/shard_map/all_to_all | solution.py:527
  69.0 12.1 %collective-permute-start.7 = (bf16[160,768]{1,0:T(8,128)(2,1)S(1)}, bf16[160,768]{1,0:T(8,128)(2,1)S(1)}, u32[]{:S(2)}, u32[]{:S(2)}) collective-permute-start(bf16[160,768]{1,0:T(8,128)(2,1)S(1)} %slice.6), channel_id=1, source_target_pairs={{0,128},{128,256},{256,384},{384,0},{1,129},{129,257},{257,385},{3... | collective-permute-start | bytes 737288 | tf_op jit(solution)/shard_map/ppermute | solution.py:475
  73.3 13.7 %collective-permute-start.8 = (bf16[160,768]{1,0:T(8,128)(2,1)S(1)}, bf16[160,768]{1,0:T(8,128)(2,1)S(1)}, u32[]{:S(2)}, u32[]{:S(2)}) collective-permute-start(bf16[160,768]{1,0:T(8,128)(2,1)S(1)} %slice.7), channel_id=1, source_target_pairs={{0,384},{128,0},{256,128},{384,256},{1,385},{129,1},{257,129},{385... | collective-permute-start | bytes 737288 | tf_op jit(solution)/shard_map/ppermute | solution.py:475
  76.5 14.8 %collective-permute-start.9 = (bf16[320,768]{1,0:T(8,128)(2,1)}, bf16[320,768]{1,0:T(8,128)(2,1)S(1)}, u32[]{:S(2)}, u32[]{:S(2)}) collective-permute-start(bf16[320,768]{1,0:T(8,128)(2,1)} %collective-permute-done.3.refs_1_), channel_id=1, source_target_pairs={{0,1},{1,0},{2,3},{3,2},{4,5},{5,4},{6,7},{7,6},{8,9},{9,8},{10,11... | collective-permute-start | bytes 1474568 | tf_op jit(solution)/shard_map/ppermute | solution.py:475
  79.2 12.1 %collective-permute-start.12 = (bf16[320,768]{1,0:T(8,128)(2,1)}, bf16[320,768]{1,0:T(8,128)(2,1)S(1)}, u32[]{:S(2)}, u32[]{:S(2)}) collective-permute-start(bf16[320,768]{1,0:T(8,128)(2,1)} %collective-permute-done.4.refs_4_), channel_id=1, source_target_pairs={{0,1},{1,0},{2,3},{3,2},{4,5},{5,4},{6,7},{7,6},{8,9},{9,8},{10,11... | collective-permute-start | bytes 1474568 | tf_op jit(solution)/shard_map/ppermute | solution.py:475
  81.1 10.2 %copy-start.13 = (bf16[160,768]{1,0:T(8,128)(2,1)}, bf16[160,768]{1,0:T(8,128)(2,1)S(1)}, u32[]{:S(2)}) copy-start(bf16[160,768]{1,0:T(8,128)(2,1)S(1)} %collective-permute-done.7.refs_2_) | copy-start | bytes 737284
  81.2 9.0 %collective-permute-start.10 = (bf16[160,768]{1,0:T(8,128)(2,1)S(1)}, bf16[160,768]{1,0:T(8,128)(2,1)S(1)}, u32[]{:S(2)}, u32[]{:S(2)}) collective-permute-start(bf16[160,768]{1,0:T(8,128)(2,1)S(1)} %collective-permute-done.7.refs_2_), channel_id=1, source_target_pairs={{0,1},{1,0},{2,3},{3,2},{4,5},{5,4},{6,7},{7,6},{8,9},{9,8},{10,11... | collective-permute-start | bytes 737288 | tf_op jit(solution)/shard_map/ppermute | solution.py:475
  87.0 4.4 %copy-start.14 = (bf16[160,768]{1,0:T(8,128)(2,1)}, bf16[160,768]{1,0:T(8,128)(2,1)S(1)}, u32[]{:S(2)}) copy-start(bf16[160,768]{1,0:T(8,128)(2,1)S(1)} %collective-permute-done.8.refs_3_) | copy-start | bytes 737284
  87.0 4.4 %collective-permute-start.11 = (bf16[160,768]{1,0:T(8,128)(2,1)S(1)}, bf16[160,768]{1,0:T(8,128)(2,1)S(1)}, u32[]{:S(2)}, u32[]{:S(2)}) collective-permute-start(bf16[160,768]{1,0:T(8,128)(2,1)S(1)} %collective-permute-done.8.refs_3_), channel_id=1, source_target_pairs={{0,1},{1,0},{2,3},{3,2},{4,5},{5,4},{6,7},{7,6},{8,9},{9,8},{10,11... | collective-permute-start | bytes 737288 | tf_op jit(solution)/shard_map/ppermute | solution.py:475
  90.2 1.2 copy-start.15
  91.3 0.7 copy-start.16
  91.3 0.9 copy-start.11
  91.3 1.0 copy-start.12
  91.4 1.3 copy-start.10
  97.7 32.5 %all-to-all-start.3 = ((bf16[16,40,640]{2,1,0:T(8,128)(2,1)}), bf16[16,40,640]{2,1,0:T(8,128)(2,1)S(1)}, u32[]{:S(2)}, u32[]{:S(2)}) async-start(bf16[16,40,640]{2,1,0:T(8,128)(2,1)} %shard_map.151), calls=%async_computation.3 | async-start | bytes 1638400 | tf_op jit(solution)/shard_map/all_to_all | solution.py:538
  108.8 21.4 %copy-start.8 = (s32[4]{0:T(128)S(1)}, s32[4]{0:T(128)}, u32[]{:S(2)}) copy-start(s32[4]{0:T(128)} %copy-done.7) | copy-start | bytes 52
  110.1 56.4 %copy-start = (bf16[640,320]{0,1:T(8,128)(2,1)S(1)}, bf16[640,320]{0,1:T(8,128)(2,1)}, u32[]{:S(2)}) copy-start(bf16[640,320]{0,1:T(8,128)(2,1)} %param.17) | copy-start | bytes 1228804
  110.1 56.4 %copy-start.1 = (bf16[640,320]{0,1:T(8,128)(2,1)S(1)}, bf16[640,320]{0,1:T(8,128)(2,1)}, u32[]{:S(2)}) copy-start(bf16[640,320]{0,1:T(8,128)(2,1)} %param.19) | copy-start | bytes 1228804
  110.1 35.6 %collective-permute-start.14 = (bf16[3,160,512]{2,1,0:T(8,128)(2,1)S(1)}, bf16[3,160,512]{2,1,0:T(8,128)(2,1)S(1)}, u32[]{:S(2)}, u32[]{:S(2)}) collective-permute-start(bf16[3,160,512]{2,1,0:T(8,128)(2,1)S(1)} %pad_maximum_fusion.1.refs_3_), channel_id=1, source_target_pairs={{0,128},{128,256},{256,384},{384,0},{1,129},{129,257},{257,385},{3... | collective-permute-start | bytes 1474568 | tf_op jit(solution)/shard_map/ppermute | solution.py:475
  113.3 32.4 %collective-permute-start.15 = (bf16[3,160,512]{2,1,0:T(8,128)(2,1)S(1)}, bf16[3,160,512]{2,1,0:T(8,128)(2,1)S(1)}, u32[]{:S(2)}, u32[]{:S(2)}) collective-permute-start(bf16[3,160,512]{2,1,0:T(8,128)(2,1)S(1)} %pad_maximum_fusion.1.refs_3_), channel_id=1, source_target_pairs={{0,256},{128,384},{256,0},{384,128},{1,257},{129,385},{257,1},{385... | collective-permute-start | bytes 1474568 | tf_op jit(solution)/shard_map/ppermute | solution.py:475
  117.0 28.7 %collective-permute-start.16 = (bf16[3,160,512]{2,1,0:T(8,128)(2,1)S(1)}, bf16[3,160,512]{2,1,0:T(8,128)(2,1)}, u32[]{:S(2)}, u32[]{:S(2)}) collective-permute-start(bf16[3,160,512]{2,1,0:T(8,128)(2,1)S(1)} %pad_maximum_fusion.1.refs_3_), channel_id=1, source_target_pairs={{0,384},{128,0},{256,128},{384,256},{1,385},{129,1},{257,129},{385... | collective-permute-start | bytes 1474568 | tf_op jit(solution)/shard_map/ppermute | solution.py:475
  130.3 0.8 copy-start.6
  132.1 0.7 copy-start.9
  146.4 20.0 %all-to-all-start.5 = ((f32[32,8,128]{2,1,0:T(8,128)}), f32[32,8,128]{2,1,0:T(8,128)S(1)}, u32[]{:S(2)}, u32[]{:S(2)}) async-start(f32[32,8,128]{2,1,0:T(8,128)} %broadcast_in_dim.3), calls=%async_computation.5 | async-start | bytes 262144 | tf_op jit(solution)/shard_map/all_to_all | solution.py:554
  155.5 1.6 collective-permute-start.13
